TPU v7x, 256 devices: a whole 4x4x8 slice. The times are simulated.
256 devices in a mesh: lon: 16 (over y, x_lo, core), lat: 16 (over x_hi, z).
Axes of the slice: x: 4 (x_hi: 2, x_lo: 2; x = x_hi * 2 + x_lo), y: 4, z: 8, core: 2. Of those that a mesh axis runs over, the one named last changes fastest.
Arguments:
- cells: bfloat16 [2, 96, 576, 384], P(None, 'lat', 'lon'), may hold values from -48 to 48
- qkv_weight: bfloat16 [384, 1152], replicated, may hold values from -0.3125 to 0.3125
- out_weight: bfloat16 [384, 384], replicated, may hold values from -0.3125 to 0.3125
- earth_bias: float32 [16, 12, 3312], P('lat'), may hold values from -3 to 445
- cotangent: bfloat16 [2, 96, 576, 384], P(None, 'lat', 'lon'), may hold values from -6 to 6
Outputs:
- result: bfloat16 [2, 96, 576, 384], P(None, 'lat', 'lon')
- grad_cells: bfloat16 [2, 96, 576, 384], P(None, 'lat', 'lon')
- grad_qkv_weight: float32 [384, 1152], replicated
- grad_out_weight: float32 [384, 384], replicated
- grad_earth_bias: float32 [16, 12, 3312], P('lat')
All inputs are finite; a program needn't handle non-finite values.
Results may differ from a plain program's by a relative error of at most 0.0095.
Values may be sent and summed in bfloat16 or wider, within the bound.
A program may use at most 64 MiB of HBM per device.

v0:
```python
import jax
import jax.numpy as jnp
from jax import lax
from jax.sharding import PartitionSpec as P

LEV = 2
WH = 6
WW = 12


def passed_along(block, axis, distance):
    devices = range(lax.axis_size(axis))
    route = [((i - distance) % len(devices), i) for i in devices]
    return lax.ppermute(block, axis, route)


def normalize(samples):
    average = jnp.mean(samples, axis=-1, keepdims=True)
    centred = samples - average
    spread = jnp.mean(centred * centred, axis=-1, keepdims=True)
    return centred * lax.rsqrt(spread + 1e-05)


def bias_layout(tokens):
    position = jnp.arange(tokens, dtype=jnp.int32)
    level_of = position // (WH * WW)
    row_of = position // WW % WH
    column = position % WW
    pair_index = (
        (level_of[:, None] * LEV + level_of[None, :]) * (WH * WH)
        + row_of[:, None] * WH
        + row_of[None, :]
    )
    return pair_index * (2 * WW - 1) + column[:, None] - column[None, :] + (WW - 1)


def blocked_pairs(tokens, last_rows):
    position = jnp.arange(tokens, dtype=jnp.int32)
    region = position // WW % WH >= WH - WH // 2
    crossing = region[:, None] != region[None, :]
    return jnp.logical_and(last_rows[:, None, None, None, None], crossing[None, None, None, :, :])


def attend(projected, tables, last_rows):
    channels = projected.shape[-1] // 3
    head_count = tables.shape[1]
    head_size = channels // head_count
    split_shape = projected.shape[:3] + (head_count, head_size)
    queries = projected[..., :channels].reshape(split_shape)
    key_rows = projected[..., channels : 2 * channels].reshape(split_shape)
    values = projected[..., 2 * channels :].reshape(split_shape)
    scores = jnp.einsum(
        "rwqhd,rwkhd->rwhqk", queries, key_rows, preferred_element_type=jnp.float32
    ) * head_size ** (-0.5)
    layout = bias_layout(projected.shape[2])
    scores = scores + jnp.take(tables, layout, axis=2)[:, None]
    scores = jnp.where(blocked_pairs(projected.shape[2], last_rows), -1000000000.0, scores)
    row_top = lax.stop_gradient(jnp.max(scores, axis=-1, keepdims=True))
    weights = jnp.exp(scores - row_top)
    attention = (weights / jnp.sum(weights, axis=-1, keepdims=True)).astype(jnp.bfloat16)
    mixture = jnp.einsum(
        "rwhqk,rwkhd->rwqhd", attention, values, preferred_element_type=jnp.float32
    )
    return mixture.astype(jnp.bfloat16).reshape(projected.shape[:3] + (channels,))


def window_pass(win_cells, win_cot, tables, last_rows, qkv_weight, out_weight):
    channels = win_cells.shape[-1]
    cell_values = win_cells.reshape(-1, channels).astype(jnp.float32)
    normed = normalize(cell_values).astype(jnp.bfloat16)
    projected = jnp.dot(normed, qkv_weight, preferred_element_type=jnp.float32).astype(jnp.bfloat16)
    projected = projected.reshape(win_cells.shape[:3] + (3 * channels,))

    def attend_here(projected_in, tables_in):
        return attend(projected_in, tables_in, last_rows)

    mixture, pullback = jax.vjp(attend_here, projected, tables)
    mixture_rows = mixture.reshape(-1, channels)
    out_rows = (
        cell_values + jnp.dot(mixture_rows, out_weight, preferred_element_type=jnp.float32)
    ).astype(jnp.bfloat16)
    cot_rows = win_cot.reshape(-1, channels)
    grad_out = jnp.einsum("nc,nd->cd", mixture_rows, cot_rows, preferred_element_type=jnp.float32)
    d_mixture = jnp.einsum(
        "nd,cd->nc", cot_rows, out_weight, preferred_element_type=jnp.float32
    ).astype(jnp.bfloat16)
    d_projected, d_tables = pullback(d_mixture.reshape(mixture.shape))
    d_rows = d_projected.reshape(-1, 3 * channels)
    grad_qkv = jnp.einsum("nc,nd->cd", normed, d_rows, preferred_element_type=jnp.float32)
    d_normed = jnp.einsum("nd,cd->nc", d_rows, qkv_weight, preferred_element_type=jnp.float32)
    d_values = jax.vjp(normalize, cell_values)[1](d_normed)[0]
    d_cells = (d_values + cot_rows.astype(jnp.float32)).astype(jnp.bfloat16)
    return (out_rows, d_cells, grad_qkv, grad_out, d_tables)


def on_device(cells, qkv_weight, out_weight, earth_bias, cotangent):
    levels, lat_rows, lon_cols, channels = cells.shape
    half_rows = WH // 2
    half_cols = WW // 2
    rim_cells = passed_along(
        jnp.stack([cells[:, :, :half_cols], cotangent[:, :, :half_cols]]), "lon", -1
    )
    fields = jnp.concatenate(
        [jnp.stack([cells[:, :, half_cols:], cotangent[:, :, half_cols:]]), rim_cells], axis=3
    )
    rim_cells = passed_along(fields[:, :, :half_rows], "lat", -1)
    fields = jnp.concatenate([fields[:, :, half_rows:], rim_cells], axis=2)
    rows_here = lat_rows // WH
    cols_here = lon_cols // WW
    tokens = levels * WH * WW
    windowed = fields.reshape(2, levels, rows_here, WH, cols_here, WW, channels)
    windowed = windowed.transpose(0, 2, 4, 1, 3, 5, 6).reshape(
        2, rows_here, cols_here, tokens, channels
    )
    first_row = lax.axis_index("lat") * rows_here
    total_rows = lax.axis_size("lat") * rows_here
    last_rows = first_row + jnp.arange(rows_here, dtype=jnp.int32) == total_rows - 1
    out_rows, d_cells, grad_qkv, grad_out, grad_tables = window_pass(
        windowed[0], windowed[1], earth_bias, last_rows, qkv_weight, out_weight
    )
    cell_count = levels * lat_rows * lon_cols * lax.axis_size("lat") * lax.axis_size("lon")
    padded = jnp.zeros((total_rows,) + grad_tables.shape[1:], jnp.float32)
    padded = lax.dynamic_update_slice_in_dim(padded, grad_tables, first_row, 0)
    grad_qkv, grad_out, padded = lax.psum((grad_qkv, grad_out, padded), ("lon", "lat"))
    grad_tables = lax.dynamic_slice_in_dim(padded, first_row, rows_here, 0)
    grad_scale = cell_count ** (-0.5)
    results = jnp.stack([out_rows, d_cells]).reshape(
        2, rows_here, cols_here, levels, WH, WW, channels
    )
    results = results.transpose(0, 3, 1, 4, 2, 5, 6).reshape(
        2, levels, lat_rows, lon_cols, channels
    )
    rim_cells = passed_along(results[:, :, lat_rows - half_rows :], "lat", 1)
    results = jnp.concatenate([rim_cells, results[:, :, : lat_rows - half_rows]], axis=2)
    rim_cells = passed_along(results[:, :, :, lon_cols - half_cols :], "lon", 1)
    results = jnp.concatenate([rim_cells, results[:, :, :, : lon_cols - half_cols]], axis=3)
    return (results[0], results[1], grad_qkv * grad_scale, grad_out * grad_scale, grad_tables)


def solution(mesh):
    placed = (
        P(None, "lat", "lon", None),
        P(),
        P(),
        P("lat", None, None),
        P(None, "lat", "lon", None),
    )
    return jax.shard_map(
        on_device,
        mesh=mesh,
        in_specs=placed,
        out_specs=(
            P(None, "lat", "lon", None),
            P(None, "lat", "lon", None),
            P(),
            P(),
            P("lat", None, None),
        ),
        check_vma=False,
    )
```

profile of v0, /device:TPU:1, one launch (start us, length us, event | category | flops | bytes accessed | tf_op | source)
XLA Modules:
  0.0 546.6 jit_solution(241897307178719328)
XLA Ops:
  7.2 1.0 slice_bitcast_fusion.4
  8.4 3.3 collective-permute-start
  11.7 1.4 slice_bitcast_fusion.2
  13.7 1.0 pad_maximum_fusion.1
  15.2 8.0 %collective-permute-start.1 = (bf16[2,2,3,36,384]{4,1,3,2,0:T(2,128)(2,1)S(1)}, bf16[2,2,3,36,384]{4,1,3,2,0:T(2,128)(2,1)}, u32[]{:S(2)}, u32[]{:S(2)}) collective-permute-start(bf16[2,2,3,36,384]{4,1,3,2,0:T(2,128)(2,1)S(1)} %get-tuple-element.22), channel_id=1, source_target_pairs={{1,0},{2,1},{3,2},{4,3},{5,4},{6,5},{7,6},{8,7},{9,8},{10,9},{11,1... | collective-permute-start | bytes 995336 | tf_op jit(solution)/shard_map/ppermute | solution.py:14
  24.0 1.4 copy.83
  25.4 38.7 %gather_fusion = f32[20736,12]{1,0:T(8,128)} fusion(f32[12,3312]{0,1:T(8,128)S(1)} %bitcast.80, s32[21504]{0:T(1024)S(1)} %pad_clamp_fusion), kind=kCustom, calls=%fused_computation | custom fusion | bytes 2073600 | tf_op jit(solution)/shard_map/jvp(jit(_take))/gather | solution.py:56
  64.1 11.6 %copy.84 = f32[144,144,12]{0,1,2:T(8,128)S(1)} copy(f32[144,144,12]{2,1,0:T(8,128)} %bitcast.83) | data formatting | bytes 1990656 | tf_op jit(solution)/shard_map/jvp(jit(_take))/gather | solution.py:56
  75.7 1.4 select_bitcast_fusion
  77.1 1.8 pad_maximum_fusion.2
  79.1 1.0 slice_convert_fusion
  81.0 1.4 reshape.548
  84.7 2.0 copy.82
  86.7 1.1 copy.81
  87.8 6.4 %fusion.50 = (f32[3,12,144]{2,1,0:T(8,128)S(1)}, f32[3,12,144,144]{2,3,1,0:T(8,128)}) fusion(bf16[3,144,12,32]{1,3,2,0:T(8,128)(2,1)} %bitcast.103, bf16[3,144,12,32]{1,3,2,0:T(8,128)(2,1)} %bitcast.101, f32[12,144,144]{1,2,0:T(8,128)} %select_bitcast_fusion, pred[144,144]{0,1:T(8,128)(4,1)S(1)} %copy-done.16), kind=kOutput, calls=%fused_computation.104 | convolution fusion | flops 51508368 | bytes 4686336 | tf_op jit(solution)/shard_map/jvp()/sub | solution.py:59
  94.9 1.1 copy.80
  96.4 0.9 copy.87
  97.4 2.9 reshape_reshape.3
  100.2 4.2 fusion.5
  104.6 2.3 fusion.22
  106.9 2.4 fusion.19
  109.3 3.3 fusion.44
  113.5 1.3 fusion.25
  114.9 2.0 copy.95
  116.9 2.0 copy.93
  118.9 0.9 copy.90
  119.8 1.3 pad_add_fusion
  121.1 1.6 multiply_reduce_fusion.1
  122.8 1.4 copy.86
  124.2 2.4 reshape.541
  126.6 1.0 multiply_convert_fusion
  127.6 1.1 convert_element_type.108
  128.7 1.9 fusion.51
  130.6 2.3 fusion.52
  132.9 11.3 %copy.104 = f32[144,144,12]{2,1,0:T(8,128)} copy(f32[144,144,12]{0,1,2:T(8,128)} %bitcast.91) | data formatting | bytes 1990656 | tf_op jit(solution)/shard_map/transpose(jvp())/broadcast_in_dim | solution.py:56
  144.1 113.9 %scatter_custom_fusion = f32[12,3312]{0,1:T(8,128)} fusion(s32[20736]{0:T(1024)} %copy-done.13, f32[20736,12]{1,0:T(8,128)} %bitcast.88, f32[]{:T(128)} %constant.79.clone.1), kind=kCustom, calls=%fused_computation.43 | custom fusion | flops 248832 | bytes 159488 | tf_op jit(solution)/shard_map/transpose(jvp(jit(_take)))/scatter-add | solution.py:56
  258.0 2.0 copy.99
  260.0 1.7 broadcast_in_dim.75
  261.7 3.7 dynamic_update_slice.3
  266.2 1.4 fusion.26
  268.9 10.9 %collective-permute-done.2 = bf16[2,2,3,36,384]{4,1,3,2,0:T(2,128)(2,1)S(1)} collective-permute-done((bf16[2,2,3,36,384]{4,1,3,2,0:T(2,128)(2,1)S(1)}, bf16[2,2,3,36,384]{4,1,3,2,0:T(2,128)(2,1)S(1)}, u32[]{:S(2)}, u32[]{:S(2)}) %collective-permute-start.2) | collective-permute-done | bytes 331808 | tf_op jit(solution)/shard_map/ppermute | solution.py:14
  280.0 2.9 collective-permute-start.3
  282.8 2.1 collective-permute-done.3
  285.8 1.3 slice_bitcast_fusion
  287.1 245.8 %all-reduce.6.cloned.1.call-done = (f32[384,1152]{1,0:T(8,128)}, f32[384,384]{1,0:T(8,128)}, f32[16,12,3312]{2,0,1:T(8,128)}) async-done(((f32[384,1152]{1,0:T(8,128)}, f32[384,384]{1,0:T(8,128)}, f32[16,12,3312]{2,0,1:T(8,128)}), (f32[384,1152]{1,0:T(8,128)}, f32[384,384]{1,0:T(8,128)}, f32[16,12,3312]{2,0,1:T(8,128)})) %all-reduce.6.cloned.1.call-update) | async-done | bytes 4902928 | tf_op jit(solution)/shard_map/psum | solution.py:124
  532.9 2.8 broadcast_multiply_fusion
  535.8 1.9 broadcast_multiply_fusion.1
  537.7 2.1 constant_dynamic-slice_fusion
  (89 shorter events, 10.3 us)
Async XLA Ops:
  7.2 75.9 %copy-start = (bf16[384,1152]{1,0:T(8,128)(2,1)S(1)}, bf16[384,1152]{1,0:T(8,128)(2,1)}, u32[]{:S(2)}) copy-start(bf16[384,1152]{1,0:T(8,128)(2,1)} %param.6) | copy-start | bytes 2654212
  7.2 525.8 %all-reduce.6.cloned.1.call-start = ((), (), s32[]{:S(2)}) async-start(), calls=%async_computation | async-start | bytes 9830400 | tf_op jit(solution)/shard_map/psum | solution.py:124
  8.4 5.3 collective-permute-start
  13.6 9.6 %copy-start.13 = (s32[20736]{0:T(1024)}, s32[20736]{0:T(1024)S(1)}, u32[]{:S(2)}) copy-start(s32[20736]{0:T(1024)S(1)} %reshape.553) | copy-start | bytes 248836
  15.2 61.9 %collective-permute-start.1 = (bf16[2,2,3,36,384]{4,1,3,2,0:T(2,128)(2,1)S(1)}, bf16[2,2,3,36,384]{4,1,3,2,0:T(2,128)(2,1)}, u32[]{:S(2)}, u32[]{:S(2)}) collective-permute-start(bf16[2,2,3,36,384]{4,1,3,2,0:T(2,128)(2,1)S(1)} %get-tuple-element.22), channel_id=1, source_target_pairs={{1,0},{2,1},{3,2},{4,3},{5,4},{6,5},{7,6},{8,7},{9,8},{10,9},{11,1... | collective-permute-start | bytes 995336 | tf_op jit(solution)/shard_map/ppermute | solution.py:14
  80.1 7.7 %copy-start.16 = (pred[144,144]{0,1:T(8,128)(4,1)S(1)}, pred[144,144]{0,1:T(8,128)(4,1)}, u32[]{:S(2)}) copy-start(pred[144,144]{0,1:T(8,128)(4,1)} %compare_and_fusion.1) | copy-start | bytes 62212
  80.3 0.6 copy-start.11
  81.0 15.0 %copy-start.2 = (bf16[432,384]{1,0:T(8,128)(2,1)}, bf16[432,384]{1,0:T(8,128)(2,1)S(1)}, u32[]{:S(2)}) copy-start(bf16[432,384]{1,0:T(8,128)(2,1)S(1)} %reshape_squeeze.4) | copy-start | bytes 995332
  83.1 11.2 %copy-start.19 = (f32[432]{0:T(512)}, f32[432]{0:T(512)S(1)}, u32[]{:S(2)}) copy-start(f32[432]{0:T(512)S(1)} %rsqrt.14) | copy-start | bytes 5188
  87.8 8.2 %copy-start.8 = (bf16[384,384]{1,0:T(8,128)(2,1)S(1)}, bf16[384,384]{1,0:T(8,128)(2,1)}, u32[]{:S(2)}) copy-start(bf16[384,384]{1,0:T(8,128)(2,1)} %param.7) | copy-start | bytes 884740
  94.3 2.1 copy-start.14
  97.4 7.2 %slice-start = ((s8[5308416]{0:T(1024)(128)(4,1)}), s8[1114112]{0:T(1024)(128)(4,1)S(1)}, s32[]{:S(2)}) async-start(s8[5308416]{0:T(1024)(128)(4,1)} %bitcast.81), calls=%async_computation.1 | async-start | bytes 2228224
  100.2 4.3 copy-start.9
  100.2 4.3 copy-start.15
  100.2 4.3 copy-start.17
  100.2 4.3 slice-start.1
  104.6 2.3 copy-start.10
  109.3 3.3 copy-start.4
  109.3 4.2 copy-start.1
  114.8 11.7 %copy-start.12 = (f32[3,2,6,12]{3,2,1,0:T(8,128)S(1)}, f32[3,2,6,12]{3,2,1,0:T(8,128)}, u32[]{:S(2)}) copy-start(f32[3,2,6,12]{3,2,1,0:T(8,128)} %copy-done.11) | copy-start | bytes 5188
  114.9 11.7 %copy-start.18 = (f32[3,2,6,12]{3,2,1,0:T(8,128)S(1)}, f32[3,2,6,12]{3,2,1,0:T(8,128)}, u32[]{:S(2)}) copy-start(f32[3,2,6,12]{3,2,1,0:T(8,128)} %get-tuple-element.23) | copy-start | bytes 5188
  119.8 3.0 copy-start.7
  144.1 121.4 %copy-start.6 = (f32[432,384]{1,0:T(8,128)S(1)}, f32[432,384]{1,0:T(8,128)}, u32[]{:S(2)}) copy-start(f32[432,384]{1,0:T(8,128)} %get-tuple-element.30) | copy-start | bytes 1990660
  144.1 121.4 %copy-start.20 = (f32[432]{0:T(512)S(1)}, f32[432]{0:T(512)}, u32[]{:S(2)}) copy-start(f32[432]{0:T(512)} %copy-done.19) | copy-start | bytes 5188
  260.0 5.9 %copy-start.3 = (bf16[432,384]{1,0:T(8,128)(2,1)S(1)}, bf16[432,384]{1,0:T(8,128)(2,1)}, u32[]{:S(2)}) copy-start(bf16[432,384]{1,0:T(8,128)(2,1)} %copy-done.2) | copy-start | bytes 995332
  261.7 4.4 copy-start.5
  268.8 11.0 %collective-permute-start.2 = (bf16[2,2,3,36,384]{4,1,3,2,0:T(2,128)(2,1)S(1)}, bf16[2,2,3,36,384]{4,1,3,2,0:T(2,128)(2,1)S(1)}, u32[]{:S(2)}, u32[]{:S(2)}) collective-permute-start(bf16[2,2,3,36,384]{4,1,3,2,0:T(2,128)(2,1)S(1)} %get-tuple-element.19), channel_id=1, source_target_pairs={{15,0},{0,1},{1,2},{2,3},{3,4},{4,5},{5,6},{6,7},{7,8},{8,9},{9,10... | collective-permute-start | bytes 995336 | tf_op jit(solution)/shard_map/ppermute | solution.py:14
  280.0 4.9 collective-permute-start.3
Sparse Core Ops, SparseCore 0:
  265.6 267.2 all-reduce.5
where the time goes:
time: 548 us; the launch traced here: 547 us
  waiting for transfers between devices  259 us (47%)
  other arithmetic  134 us (24%)
  local copies, waits for them, and re-layouts  98.6 us (18%)
  matrix products  26.1 us (5%)
  between operations  14.5 us (3%)
  starting transfers between devices  14.3 us (3%)
    psum x1, waiting for transfers between devices, on_device(): lax.psum((grad_qkv, grad_out, padded), ('lon', 'lat'))  246 us
    scatter-add x1, other arithmetic, attend(): scores = scores + jnp.take(tables, layout, axis=2)[:, None]  114 us
    gather x2, local copies, waits for them, and re-layouts, attend(): scores = scores + jnp.take(tables, layout, axis=2)[:, None]  50.3 us
    ppermute x4, starting transfers between devices, passed_along(): return lax.ppermute(block, axis, route)  14.3 us
    ppermute x4, waiting for transfers between devices, passed_along(): return lax.ppermute(block, axis, route)  13 us
    broadcast_in_dim x1, local copies, waits for them, and re-layouts, attend(): scores = scores + jnp.take(tables, layout, axis=2)[:, None]  11.3 us
  transfers between devices with their start and end apart: 5, of which 3 were waited for; matrix products, arithmetic and copies ran while one was open for 11% of the time, Pallas kernels for 0%

commit v1 on v0

v1 whole, which is shorter than its diff:
```python
import numpy as np
import jax
import jax.numpy as jnp
from jax import lax
from jax.experimental import pallas as pl
from jax.experimental.pallas import tpu as pltpu
from jax.sharding import PartitionSpec as P

LEV = 2
WH = 6
WW = 12
TOK = LEV * WH * WW
SLABS = LEV * WH
SPAN = 2 * WW - 1
GROUP = 4
LANES = GROUP * TOK
F32 = jnp.float32
BF16 = jnp.bfloat16


def nn(a, b):
    return lax.dot_general(a, b, (((1,), (0,)), ((), ())), preferred_element_type=F32)


def nt(a, b):
    return lax.dot_general(a, b, (((1,), (1,)), ((), ())), preferred_element_type=F32)


def constants(heads):
    j1, i2, j2 = np.meshgrid(np.arange(WW), np.arange(WH), np.arange(WW), indexing="ij")
    spot = (i2 * SPAN + j1 - j2 + WW - 1).reshape(-1)
    spread = (spot[:, None] == np.arange(WH * SPAN)[None, :]).astype(np.float32)
    lane = np.arange(LANES)
    lane_col, lane_slab = lane // (SLABS * GROUP), lane // GROUP % SLABS
    token_of_lane = lane_slab * WW + lane_col
    pick = (np.arange(TOK)[:, None] == token_of_lane[None, :]).astype(np.float32)
    row_half = np.arange(TOK) // WW % WH >= WH - WH // 2
    lane_half = lane_slab % WH >= WH - WH // 2
    cross = np.where(row_half[:, None] != lane_half[None, :], -1e9, 0.0).astype(np.float32)
    return (
        jnp.asarray(spread, BF16),
        jnp.asarray(spread.T, BF16),
        jnp.asarray(pick, BF16),
        jnp.asarray(cross, F32),
    )


def window_kernel(windows, groups, scale, grad_scale, last_ref, x_ref, dy_ref, wqkv_ref, wout_ref, r_ref,
                  spread_ref, gather_ref, pick_ref, cross_ref,
                  out_ref, dx_ref, gqkv_ref, gout_ref, dr_ref,
                  bt, db, normed, mix, dproj, wt):
    c = x_ref.shape[-1]
    half = WH * WW
    blk = SLABS * GROUP
    last = last_ref[0]
    for z2 in range(LEV):
        table = r_ref[z2]
        hi = table.astype(BF16)
        rest = table - hi.astype(F32)
        mid = rest.astype(BF16)
        lo = (rest - mid.astype(F32)).astype(BF16)
        spread = spread_ref[...]
        u = nt(spread, hi) + nt(spread, mid) + nt(spread, lo)
        for g in range(groups):
            rows = jnp.concatenate(
                [u[j * half:(j + 1) * half, g * blk:(g + 1) * blk] for j in range(WW)], axis=1
            )
            keep = pl.ds(z2 * half, half)
            bt[g, keep, :] = rows + cross_ref[keep, :] * last
    row = lax.broadcasted_iota(jnp.int32, (c, c), 0)
    col = lax.broadcasted_iota(jnp.int32, (c, c), 1)
    eye = (row == col).astype(F32).astype(BF16)
    head_row = lax.broadcasted_iota(jnp.int32, (GROUP * 32, LANES), 0) // 32
    head_lane = lax.broadcasted_iota(jnp.int32, (GROUP * 32, LANES), 1) % GROUP
    mine = (head_row == head_lane).astype(F32)

    x = x_ref[...].astype(F32)
    average = jnp.mean(x, axis=-1, keepdims=True)
    centred = x - average
    spread_x = jnp.mean(centred * centred, axis=-1, keepdims=True)
    rstd = lax.rsqrt(spread_x + 1e-05)
    normed[...] = (centred * rstd).astype(BF16)
    for part in range(3):
        wt[part * c:(part + 1) * c, :] = nt(eye, wqkv_ref[:, part * c:(part + 1) * c]).astype(BF16)
    pick = pick_ref[...]
    gw = GROUP * 32

    for w in range(windows):
        at = slice(w * TOK, (w + 1) * TOK)
        here = normed[at, :]
        qkv_t = nt(wt[...], here).astype(BF16)
        kv = nn(here, wqkv_ref[:, c:]).astype(BF16)
        dm_t = nt(wout_ref[...], dy_ref[at, :]).astype(BF16)
        for g in range(groups):
            gs = slice(g * gw, (g + 1) * gw)
            k, v = kv[:, g * gw:(g + 1) * gw], kv[:, c + g * gw:c + (g + 1) * gw]
            k_t, v_t = qkv_t[c + g * gw:c + (g + 1) * gw], qkv_t[2 * c + g * gw:2 * c + (g + 1) * gw]
            q_wide = (nn(qkv_t[gs], pick) * mine).astype(BF16)
            dm_wide = (nn(dm_t[gs], pick) * mine).astype(BF16)
            s = nn(k, q_wide) * scale + bt[g]
            top = jnp.max(s, axis=0, keepdims=True)
            e = jnp.exp(s - top)
            soft = e * (1.0 / jnp.sum(e, axis=0, keepdims=True))
            a = soft.astype(BF16)
            da = nn(v, dm_wide)
            ds = soft * (da - jnp.sum(soft * da, axis=0, keepdims=True))
            if w == 0:
                db[g] = ds
            else:
                db[g] += ds
            ds = ds.astype(BF16)
            m_t = (nn(v_t, a) * mine).astype(BF16)
            mix[at, gs] = nt(pick, m_t).astype(BF16)
            dq_t = (nn(k_t, ds) * (mine * scale)).astype(BF16)
            dproj[at, gs] = nt(pick, dq_t).astype(BF16)
            dproj[at, c + g * gw:c + (g + 1) * gw] = (nt(ds, q_wide) * scale).astype(BF16)
            dproj[at, 2 * c + g * gw:2 * c + (g + 1) * gw] = nt(a, dm_wide).astype(BF16)

    for z2 in range(LEV):
        keep = slice(z2 * half, (z2 + 1) * half)
        rows = jnp.concatenate(
            [
                jnp.concatenate([db[g, keep, j * blk:(j + 1) * blk] for g in range(groups)], axis=1)
                for j in range(WW)
            ],
            axis=0,
        ).astype(BF16)
        dr_ref[z2] = nn(gather_ref[...], rows)
    out_ref[...] = (x + nn(mix[...], wout_ref[...])).astype(BF16)
    gout_ref[...] = nn(nt(eye, mix[...]).astype(BF16), dy_ref[...]) * grad_scale
    gqkv_ref[...] = nn(nt(eye, normed[...]).astype(BF16), dproj[...]) * grad_scale
    dn = nt(dproj[...], wqkv_ref[...])
    n = centred * rstd
    dx = (dn - jnp.mean(dn, axis=-1, keepdims=True) - n * jnp.mean(dn * n, axis=-1, keepdims=True)) * rstd
    dx_ref[...] = (dx + dy_ref[...].astype(F32)).astype(BF16)


def window_pass(x, dy, qkv_weight, out_weight, table, last, cells_total):
    rows, c = x.shape
    windows = rows // TOK
    heads = table.shape[0]
    groups = heads // GROUP
    spread, gather, pick, cross = constants(heads)
    table = table.reshape(groups, GROUP, LEV, LEV, WH, WH * SPAN)
    table = table.transpose(3, 0, 2, 4, 1, 5).reshape(LEV, heads * SLABS, WH * SPAN)
    kernel = lambda *refs: window_kernel(
        windows, groups, (c // heads) ** -0.5, cells_total ** -0.5, *refs
    )
    vmem = pl.BlockSpec(memory_space=pltpu.VMEM)
    out, dx, gqkv, gout, dr = pl.pallas_call(
        kernel,
        out_shape=(
            jax.ShapeDtypeStruct((rows, c), BF16),
            jax.ShapeDtypeStruct((rows, c), BF16),
            jax.ShapeDtypeStruct((c, 3 * c), F32),
            jax.ShapeDtypeStruct((c, c), F32),
            jax.ShapeDtypeStruct((LEV, WH * SPAN, heads * SLABS), F32),
        ),
        in_specs=[pl.BlockSpec(memory_space=pltpu.SMEM)] + [vmem] * 9,
        out_specs=(vmem,) * 5,
        scratch_shapes=[
            pltpu.VMEM((groups, TOK, LANES), F32),
            pltpu.VMEM((groups, TOK, LANES), F32),
            pltpu.VMEM((rows, c), BF16),
            pltpu.VMEM((rows, c), BF16),
            pltpu.VMEM((rows, 3 * c), BF16),
            pltpu.VMEM((3 * c, c), BF16),
        ],
        compiler_params=pltpu.CompilerParams(vmem_limit_bytes=48 * 1024 * 1024),
        cost_estimate=pl.CostEstimate(flops=5_500_000_000, bytes_accessed=6_000_000, transcendentals=800_000),
    )(last, x, dy, qkv_weight, out_weight, table, spread, gather, pick, cross)
    return out, dx, gqkv, gout, dr


def table_grad(dr, heads):
    groups = heads // GROUP
    dr = dr.reshape(LEV, WH * SPAN, groups, LEV, WH, GROUP)
    return dr.transpose(2, 5, 3, 0, 4, 1).reshape(1, heads, LEV * LEV * WH * WH * SPAN)


def passed_along(block, axis, distance):
    devices = range(lax.axis_size(axis))
    route = [((i - distance) % len(devices), i) for i in devices]
    return lax.ppermute(block, axis, route)


def on_device(cells, qkv_weight, out_weight, earth_bias, cotangent):
    levels, lat_rows, lon_cols, channels = cells.shape
    half_rows = WH // 2
    half_cols = WW // 2
    rim_cells = passed_along(
        jnp.stack([cells[:, :, :half_cols], cotangent[:, :, :half_cols]]), "lon", -1
    )
    fields = jnp.concatenate(
        [jnp.stack([cells[:, :, half_cols:], cotangent[:, :, half_cols:]]), rim_cells], axis=3
    )
    rim_cells = passed_along(fields[:, :, :half_rows], "lat", -1)
    fields = jnp.concatenate([fields[:, :, half_rows:], rim_cells], axis=2)
    cols_here = lon_cols // WW
    windowed = fields.reshape(2, levels, WH, cols_here, WW, channels)
    windowed = windowed.transpose(0, 3, 1, 2, 4, 5).reshape(2, cols_here * TOK, channels)
    last = (lax.axis_index("lat") == lax.axis_size("lat") - 1).astype(F32).reshape(1)
    cell_count = levels * lat_rows * lon_cols * lax.axis_size("lat") * lax.axis_size("lon")
    out_rows, d_cells, grad_qkv, grad_out, dr = window_pass(
        windowed[0], windowed[1], qkv_weight, out_weight, earth_bias[0], last, cell_count
    )
    grad_qkv, grad_out = lax.psum((grad_qkv, grad_out), ("lon", "lat"))
    grad_tables = table_grad(lax.psum(dr, "lon"), earth_bias.shape[1])
    results = jnp.stack([out_rows, d_cells]).reshape(2, cols_here, levels, WH, WW, channels)
    results = results.transpose(0, 2, 3, 1, 4, 5).reshape(2, levels, lat_rows, lon_cols, channels)
    rim_cells = passed_along(results[:, :, lat_rows - half_rows :], "lat", 1)
    results = jnp.concatenate([rim_cells, results[:, :, : lat_rows - half_rows]], axis=2)
    rim_cells = passed_along(results[:, :, :, lon_cols - half_cols :], "lon", 1)
    results = jnp.concatenate([rim_cells, results[:, :, :, : lon_cols - half_cols]], axis=3)
    return (results[0], results[1], grad_qkv, grad_out, grad_tables)


def solution(mesh):
    grid = P(None, "lat", "lon", None)
    return jax.shard_map(
        on_device,
        mesh=mesh,
        in_specs=(grid, P(), P(), P("lat", None, None), grid),
        out_specs=(grid, grid, P(), P(), P("lat", None, None)),
        check_vma=False,
    )
```

time: 548 us -> 445 us (0.81)
  other arithmetic: 134 us -> 3.67 us
  waiting for transfers between devices: 259 us -> 380 us
  local copies, waits for them, and re-layouts: 98.6 us -> 16.7 us
  matrix products: 26.1 us -> 0 us
  Pallas kernels: 0 us -> 13.6 us
    psum x1 -> x2, waiting for transfers between devices: 246 us -> 364 us  [the longest x1 263 us: on_device(): grad_qkv, grad_out = lax.psum((grad_qkv, grad_out), ('lon', 'lat'))]
    scatter-add x1 -> x0, other arithmetic: 114 us -> none  [attend(): scores = scores + jnp.take(tables, layout, axis=2)[:, None]]
    gather x2 -> x0, local copies, waits for them, and re-layouts: 50.3 us -> none  [attend(): scores = scores + jnp.take(tables, layout, axis=2)[:, None]]
    dot_general x11 -> x0, matrix products: 19.7 us -> none  [the longest x3 6.48 us: attend(): jnp.einsum('rwhqk,rwkhd->rwqhd', attention, values, preferred_element_typ...]
    pallas_call x0 -> x1, Pallas kernels: none -> 13.6 us  [window_pass(): pl.pallas_call(kernel, out_shape=(jax.ShapeDtypeStruct((rows, c), BF16),...]
    broadcast_in_dim x2 -> x0, local copies, waits for them, and re-layouts: 13 us -> none  [the longest x1 11.3 us: attend(): scores = scores + jnp.take(tables, layout, axis=2)[:, None]]
    unnamed x47 -> x19, local copies, waits for them, and re-layouts: 1.7 us -> 9.38 us
    sub x1 -> x0, matrix products: 6.44 us -> none  [attend(): weights = jnp.exp(scores - row_top)]
  transfers between devices with their start and end apart: 5 -> 6, of which waited for: 3 -> 5; matrix products, arithmetic and copies ran while one was open for 11% -> 2% of each run, Pallas kernels for 0% -> 0%
where the time goes in v1:
time: 445 us; the launch traced here: 444 us
  waiting for transfers between devices  380 us (85%)
  local copies, waits for them, and re-layouts  16.7 us (4%)
  starting transfers between devices  16.3 us (4%)
  between operations  14.2 us (3%)
  Pallas kernels  13.6 us (3%)
    psum x1, waiting for transfers between devices, on_device(): grad_qkv, grad_out = lax.psum((grad_qkv, grad_out), ('lon', 'lat'))  263 us
    psum x1, waiting for transfers between devices, on_device(): grad_tables = table_grad(lax.psum(dr, 'lon'), earth_bias.shape[1])  101 us
    ppermute x4, starting transfers between devices, passed_along(): return lax.ppermute(block, axis, route)  16.2 us
    ppermute x4, waiting for transfers between devices, passed_along(): return lax.ppermute(block, axis, route)  15.7 us
    pallas_call x1, Pallas kernels, window_pass(): pl.pallas_call(kernel, out_shape=(jax.ShapeDtypeStruct((rows, c), BF16),...  13.6 us
    unnamed x19, local copies, waits for them, and re-layouts  9.38 us
  transfers between devices with their start and end apart: 6, of which 5 were waited for; matrix products, arithmetic and copies ran while one was open for 2% of the time, Pallas kernels for 0%

profile of v1, /device:TPU:1, one launch (start us, length us, event | category | flops | bytes accessed | tf_op | source)
XLA Modules:
  0.0 444.0 jit_solution(5051401545023015086)
XLA Ops:
  7.2 0.0 all-reduce.4.cloned.1.call-start
  7.2 0.9 slice_bitcast_fusion.4
  8.1 0.2 pad_maximum_fusion.4
  8.3 3.3 collective-permute-start
  11.6 1.4 slice_bitcast_fusion.2
  13.1 0.4 collective-permute-done
  13.4 1.0 pad_maximum_fusion.1
  14.5 0.5 fusion.3
  14.9 8.3 %collective-permute-start.1 = (bf16[2,2,3,36,384]{4,1,3,2,0:T(2,128)(2,1)S(1)}, bf16[2,2,3,36,384]{4,1,3,2,0:T(2,128)(2,1)S(1)}, u32[]{:S(2)}, u32[]{:S(2)}) collective-permute-start(bf16[2,2,3,36,384]{4,1,3,2,0:T(2,128)(2,1)S(1)} %get-tuple-element.34), channel_id=1, source_target_pairs={{1,0},{2,1},{3,2},{4,3},{5,4},{6,5},{7,6},{8,7},{9,8},{10,9},{11,1... | collective-permute-start | bytes 995336 | tf_op jit(solution)/shard_map/ppermute | solution.py:184
  23.2 0.4 reduce
  23.6 0.4 reshape_squeeze.3
  23.9 0.2 copy.25
  24.1 4.2 collective-permute-done.1
  28.4 0.9 pad_maximum_fusion.2
  29.2 0.1 copy.32
  29.4 0.0 copy-start.2
  29.4 0.1 fusion.1
  29.5 0.1 squeeze.13.refs_2_
  29.6 0.1 squeeze.12.refs_1_
  29.7 0.9 copy-done
  30.5 0.1 copy-done.1
  30.6 0.1 copy-done.2
  30.7 1.0 copy-done.3
  31.7 0.9 copy-done.4
  32.7 0.9 copy-done.5
  33.6 13.6 %shard_map.128 = (bf16[432,384]{1,0:T(8,128)(2,1)S(1)}, bf16[432,384]{1,0:T(8,128)(2,1)S(1)}, f32[384,1152]{1,0:T(8,128)}, f32[384,384]{1,0:T(8,128)}, f32[2,138,144]{2,1,0:T(8,128)S(1)}) custom-call(f32[1]{0:T(128)} %bitcast.refs_0_, bf16[432,384]{1,0:T(8,128)(2,1)S(1)} %squeeze.12.refs_1_, bf16[432,384]{1,0:T(8,128)(2,1)S(1)} %squeeze.13.refs_2_, ...), custom_call_target="tpu_custom_call" | custom-call | flops 5500000256 | bytes 6000000 | tf_op jit(solution)/shard_map/pallas_call | solution.py:150
  47.2 0.2 copy.28
  47.4 0.1 copy.29
  47.5 0.9 reshape.46
  48.4 0.0 all-reduce.4.cloned.1.call-update
  48.4 0.0 all-reduce.6.cloned.1.call-start
  48.4 0.1 stack.33
  48.5 0.1 stack.34
  48.6 0.2 maximum_bitcast_fusion
  48.8 0.5 copy.27
  49.3 0.0 all-reduce.6.cloned.1.call-update
  49.3 0.5 fusion.2
  49.8 0.1 collective-permute-start.2
  49.9 11.1 %collective-permute-done.2 = bf16[2,2,3,36,384]{4,1,3,2,0:T(2,128)(2,1)S(1)} collective-permute-done((bf16[2,2,3,36,384]{4,1,3,2,0:T(2,128)(2,1)S(1)}, bf16[2,2,3,36,384]{4,1,3,2,0:T(2,128)(2,1)S(1)}, u32[]{:S(2)}, u32[]{:S(2)}) %collective-permute-start.2) | collective-permute-done | bytes 331808 | tf_op jit(solution)/shard_map/ppermute | solution.py:184
  61.0 0.1 pad_maximum_fusion.3
  61.1 4.5 %collective-permute-start.3 = (bf16[2,2,6,6,384]{4,1,3,2,0:T(2,128)(2,1)S(1)}, bf16[2,2,6,6,384]{4,1,3,2,0:T(2,128)(2,1)S(1)}, u32[]{:S(2)}, u32[]{:S(2)}) collective-permute-start(bf16[2,2,6,6,384]{4,1,3,2,0:T(2,128)(2,1)S(1)} %pad_maximum_fusion.3), channel_id=1, source_target_pairs={{240,0},{0,16},{16,32},{32,48},{48,64},{64,80},{80,96},{96,112},{1... | collective-permute-start | bytes 331784 | tf_op jit(solution)/shard_map/ppermute | solution.py:184
  65.6 100.5 %all-reduce.4.cloned.1.call-done = f32[1,12,3312]{2,1,0:T(8,128)} async-done(((f32[1,12,3312]{2,1,0:T(8,128)}), f32[1,12,3312]{2,1,0:T(8,128)}) %all-reduce.4.cloned.1.call-update) | async-done | bytes 158992 | tf_op jit(solution)/shard_map/psum | solution.py:208
  166.2 1.8 copy.30
  167.9 0.9 fusion
  168.9 1.3 slice_bitcast_fusion
  170.2 263.3 %all-reduce.6.cloned.1.call-done = (f32[384,1152]{1,0:T(8,128)}, f32[384,384]{1,0:T(8,128)}) async-done(((f32[384,1152]{1,0:T(8,128)}, f32[384,384]{1,0:T(8,128)}), (f32[384,1152]{1,0:T(8,128)}, f32[384,384]{1,0:T(8,128)})) %all-reduce.6.cloned.1.call-update) | async-done | bytes 2359312 | tf_op jit(solution)/shard_map/psum | solution.py:207
  433.4 2.9 copy.36
  436.3 0.8 copy.37
  (11 shorter events, 0.0 us)
Async XLA Ops:
  7.2 159.0 %all-reduce.4.cloned.1.call-start = ((), (), s32[]{:S(2)}) async-start(), calls=%async_computation | async-start | bytes 425984 | tf_op jit(solution)/shard_map/psum | solution.py:208
  8.3 14.9 %copy-start.7 = (f32[1,12,3312]{2,0,1:T(1,128)S(1)}, f32[1,12,3312]{2,0,1:T(1,128)}, u32[]{:S(2)}) copy-start(f32[1,12,3312]{2,0,1:T(1,128)} %param.12) | copy-start | bytes 476932
  8.3 5.1 %collective-permute-start = (bf16[2,2,6,6,384]{4,1,3,2,0:T(2,128)(2,1)S(1)}, bf16[2,2,6,6,384]{4,1,3,2,0:T(2,128)(2,1)S(1)}, u32[]{:S(2)}, u32[]{:S(2)}) collective-permute-start(bf16[2,2,6,6,384]{4,1,3,2,0:T(2,128)(2,1)S(1)} %pad_maximum_fusion.4), channel_id=1, source_target_pairs={{16,0},{32,16},{48,32},{64,48},{80,64},{96,80},{112,96},{128,112},... | collective-permute-start | bytes 331784 | tf_op jit(solution)/shard_map/ppermute | solution.py:184
  14.9 13.4 %collective-permute-start.1 = (bf16[2,2,3,36,384]{4,1,3,2,0:T(2,128)(2,1)S(1)}, bf16[2,2,3,36,384]{4,1,3,2,0:T(2,128)(2,1)S(1)}, u32[]{:S(2)}, u32[]{:S(2)}) collective-permute-start(bf16[2,2,3,36,384]{4,1,3,2,0:T(2,128)(2,1)S(1)} %get-tuple-element.34), channel_id=1, source_target_pairs={{1,0},{2,1},{3,2},{4,3},{5,4},{6,5},{7,6},{8,7},{9,8},{10,9},{11,1... | collective-permute-start | bytes 995336 | tf_op jit(solution)/shard_map/ppermute | solution.py:184
  29.4 1.2 copy-start
  29.4 1.2 copy-start.1
  29.4 1.3 copy-start.2
  30.7 1.0 copy-start.3
  31.7 0.9 copy-start.4
  32.7 0.9 copy-start.5
  48.4 385.1 %all-reduce.6.cloned.1.call-start = ((), (), s32[]{:S(2)}) async-start(), calls=%async_computation.1 | async-start | bytes 4718592 | tf_op jit(solution)/shard_map/psum | solution.py:207
  49.8 11.2 %collective-permute-start.2 = (bf16[2,2,3,36,384]{4,1,3,2,0:T(2,128)(2,1)S(1)}, bf16[2,2,3,36,384]{4,1,3,2,0:T(2,128)(2,1)S(1)}, u32[]{:S(2)}, u32[]{:S(2)}) collective-permute-start(bf16[2,2,3,36,384]{4,1,3,2,0:T(2,128)(2,1)S(1)} %get-tuple-element.31), channel_id=1, source_target_pairs={{15,0},{0,1},{1,2},{2,3},{3,4},{4,5},{5,6},{6,7},{7,8},{8,9},{9,10... | collective-permute-start | bytes 995336 | tf_op jit(solution)/shard_map/ppermute | solution.py:184
  61.1 106.8 %collective-permute-start.3 = (bf16[2,2,6,6,384]{4,1,3,2,0:T(2,128)(2,1)S(1)}, bf16[2,2,6,6,384]{4,1,3,2,0:T(2,128)(2,1)S(1)}, u32[]{:S(2)}, u32[]{:S(2)}) collective-permute-start(bf16[2,2,6,6,384]{4,1,3,2,0:T(2,128)(2,1)S(1)} %pad_maximum_fusion.3), channel_id=1, source_target_pairs={{240,0},{0,16},{16,32},{32,48},{48,64},{64,80},{80,96},{96,112},{1... | collective-permute-start | bytes 331784 | tf_op jit(solution)/shard_map/ppermute | solution.py:184
  433.4 2.9 copy-start.6
Sparse Core Ops, SparseCore 0:
  48.5 117.6 all-reduce.3
  173.3 260.1 all-reduce.5

commit v2 on v1

v2 whole, which is shorter than its diff:
```python
import functools

import numpy as np
import jax
import jax.numpy as jnp
from jax import lax
from jax.experimental import pallas as pl
from jax.experimental.pallas import tpu as pltpu
from jax.sharding import PartitionSpec as P

LEV = 2
WH = 6
WW = 12
TOK = LEV * WH * WW
SLABS = LEV * WH
SPAN = 2 * WW - 1
GROUP = 4
HEAD = 32
LANES = GROUP * TOK
WINDOWS = 3
ROWS = WINDOWS * TOK
COLS = WINDOWS * WW
PITCH = 48
RIMS = ((0, 208), (208, 48), (256, 48))
RIM = 304
TILES = 96
BIAS_TILES = 32
F32 = jnp.float32
BF16 = jnp.bfloat16
MESH = pl.DeviceIdType.MESH


def nn(a, b):
    return lax.dot_general(a, b, (((1,), (0,)), ((), ())), preferred_element_type=F32)


def nt(a, b):
    return lax.dot_general(a, b, (((1,), (1,)), ((), ())), preferred_element_type=F32)


def constants():
    j1, i2, j2 = np.meshgrid(np.arange(WW), np.arange(WH), np.arange(WW), indexing="ij")
    spot = (i2 * SPAN + j1 - j2 + WW - 1).reshape(-1)
    spread = (spot[:, None] == np.arange(WH * SPAN)[None, :]).astype(np.float32)
    gather = np.zeros((144, spread.shape[0]), np.float32)
    gather[: WH * SPAN] = spread.T
    lane = np.arange(LANES)
    lane_col, lane_slab = lane // (SLABS * GROUP), lane // GROUP % SLABS
    token_of_lane = lane_slab * WW + lane_col
    pick = (np.arange(TOK)[:, None] == token_of_lane[None, :]).astype(np.float32)
    row_half = np.arange(TOK) // WW % WH >= WH - WH // 2
    lane_half = lane_slab % WH >= WH - WH // 2
    cross = np.where(row_half[:, None] != lane_half[None, :], -1e9, 0.0).astype(np.float32)
    own = np.zeros((ROWS, SLABS * PITCH), np.float32)
    rim = np.zeros((ROWS, RIM), np.float32)
    send = np.zeros((RIM, SLABS * PITCH), np.float32)
    h = WH // 2
    for w in range(WINDOWS):
        for z in range(LEV):
            for i in range(WH):
                for j in range(WW):
                    t = w * TOK + (z * WH + i) * WW + j
                    col = WW // 2 + w * WW + j
                    below, beside = i >= h, col >= COLS
                    row, k = ((i - h) if below else (i + h)), i % h
                    slab = (z * WH + row) * PITCH + col % COLS
                    if not below and not beside:
                        own[t, slab] = 1
                        continue
                    if beside:
                        at = (256 if below else 208) + z * 18 + k * 6 + j - 6
                    elif w == WINDOWS - 1:
                        at = 160 + z * 18 + k * 6 + j
                    else:
                        at = 80 * w + z * 36 + k * 12 + j
                    rim[t, at] = 1
                    send[at, slab] = 1
    bf = lambda a: jnp.asarray(np.ascontiguousarray(a), BF16)
    return (
        bf(spread), bf(gather), bf(pick), jnp.asarray(cross, F32),
        bf(own), bf(rim), bf(send), bf(own.T), bf(rim.T), bf(send.T),
    )


N_IN = 15


def body(lon_size, lat_size, groups, scale, grad_scale, *refs):
    (cells_h, cot_h, wqkv_h, wout_h, r_h) = refs[:5]
    consts_h = refs[5:N_IN]
    (out_ref, dx_ref, gqkv_ref, gout_ref, dr_ref) = refs[N_IN:N_IN + 5]
    (cells_v, cot_v, wqkv_ref, wout_ref, r_ref,
     spread_ref, gather_ref, pick_ref, cross_ref, own_ref, rim_ref, send_ref, ownt_ref, rimt_ref, sendt_ref,
     load_sem, slab, rim_snd, rim_in, bt, db, x_w, dy_w, normed, normed_t, mix, dproj, wt, ow, rim_osnd, rim_out,
     gb, crecv, xs, xrecv, zbuf, fin, bb, bcrecv, bs, brecv, bfin,
     halo_sem, core_sem, xy_sem, z_sem, ag_sem, fwd_sem, bcore_sem, bxy_sem, bag_sem, bfwd_sem) = refs[N_IN + 5:]
    c = wout_ref.shape[0]
    ny, nz = lon_size // 4, lat_size // 2
    nxy, nb = 4 * ny, 2 * ny
    half = WH * WW
    blk = SLABS * GROUP
    gw = GROUP * HEAD

    lon, lat = lax.axis_index("lon"), lax.axis_index("lat")
    core, x_lo, y = lon % 2, lon // 2 % 2, lon // 4
    x_hi, z = lat // nz, lat % nz
    p = y * 4 + x_hi * 2 + x_lo
    b = y * 2 + x_lo
    other = 1 - core

    def dev(lon_at, lat_at):
        return {"lon": lon_at, "lat": lat_at}

    sibling = dev(lon + 1 - 2 * core, lat)

    def xy_at(o):
        q = (p + o) % nxy
        return q, dev((q // 4 * 2 + q % 2) * 2 + core, q // 2 % 2 * nz + z)

    def b_at(o):
        q = (b + o) % nb
        return q, dev(q * 2 + core, lat)

    def z_at(o):
        q = (z + o) % nz
        return q, dev(lon, x_hi * nz + q)

    lon_prev, lon_next = (lon + lon_size - 1) % lon_size, (lon + 1) % lon_size
    lat_prev, lat_next = (lat + lat_size - 1) % lat_size, (lat + 1) % lat_size
    back = (dev(lon, lat_prev), dev(lon_prev, lat), dev(lon_prev, lat_prev))
    ahead = (dev(lon, lat_next), dev(lon_next, lat), dev(lon_next, lat_next))

    def remote(src, dst, send_sem, recv_sem, device):
        return pltpu.make_async_remote_copy(
            src_ref=src, dst_ref=dst, send_sem=send_sem, recv_sem=recv_sem, device_id=device, device_id_type=MESH
        )

    dsts = (cells_v, cot_v, send_ref, r_ref, spread_ref, cross_ref, wqkv_ref, wout_ref, own_ref, rim_ref, pick_ref,
            gather_ref, ownt_ref, rimt_ref, sendt_ref)
    srcs = (cells_h, cot_h, consts_h[6], r_h, consts_h[0], consts_h[3], wqkv_h, wout_h, consts_h[4], consts_h[5],
            consts_h[2], consts_h[1], consts_h[7], consts_h[8], consts_h[9])
    loads = [pltpu.make_async_copy(s, d, load_sem.at[i]) for i, (s, d) in enumerate(zip(srcs, dsts))]
    for load in loads:
        load.start()

    barrier = pltpu.get_barrier_semaphore()

    def greet(device):
        pl.semaphore_signal(barrier, inc=1, device_id=device, device_id_type=MESH)

    for device in back + ahead + (sibling,):
        greet(device)

    @pl.loop(1, nxy)
    def _(o):
        greet(xy_at(o)[1])

    @pl.loop(1, nz)
    def _(o):
        greet(z_at(o)[1])

    slab[...] = jnp.zeros_like(slab)
    for f in range(2):
        loads[f].wait()
        src = (cells_v, cot_v)[f]
        for s in range(SLABS):
            slab[f, s * PITCH:s * PITCH + COLS, :] = src[s // WH, s % WH]
    loads[2].wait()
    for f in range(2):
        rim_snd[f] = nn(send_ref[...], slab[f]).astype(BF16)
    pl.semaphore_wait(barrier, 7 + (nxy - 1) + (nz - 1))

    def rim_copies(snd, rcv, devices, base):
        return [
            remote(
                snd.at[f, pl.ds(at, size)], rcv.at[f, pl.ds(at, size)],
                halo_sem.at[0, base + f * 3 + k], halo_sem.at[1, base + f * 3 + k], devices[k],
            )
            for f in range(2)
            for k, (at, size) in enumerate(RIMS)
        ]

    rims_in = rim_copies(rim_snd, rim_in, back, 0)
    rims_out = rim_copies(rim_osnd, rim_out, ahead, 6)
    for copy in rims_in:
        copy.start()

    for load in loads[3:6]:
        load.wait()
    last = (lat == lat_size - 1).astype(F32)
    for z2 in range(LEV):
        table = r_ref[z2]
        hi = table.astype(BF16)
        rest = table - hi.astype(F32)
        mid = rest.astype(BF16)
        lo = (rest - mid.astype(F32)).astype(BF16)
        spread = spread_ref[...]
        u = nt(spread, hi) + nt(spread, mid) + nt(spread, lo)
        for g in range(groups):
            rows = jnp.concatenate(
                [u[j * half:(j + 1) * half, g * blk:(g + 1) * blk] for j in range(WW)], axis=1
            )
            keep = pl.ds(z2 * half, half)
            bt[g, keep, :] = rows + cross_ref[keep, :] * last
    row = lax.broadcasted_iota(jnp.int32, (c, c), 0)
    col = lax.broadcasted_iota(jnp.int32, (c, c), 1)
    eye = (row == col).astype(F32).astype(BF16)
    head_row = lax.broadcasted_iota(jnp.int32, (gw, LANES), 0) // HEAD
    head_lane = lax.broadcasted_iota(jnp.int32, (gw, LANES), 1) % GROUP
    mine = (head_row == head_lane).astype(F32)
    for load in loads[6:]:
        load.wait()
    for part in range(3):
        wt[part * c:(part + 1) * c, :] = nt(eye, wqkv_ref[:, part * c:(part + 1) * c]).astype(BF16)
    pick = pick_ref[...]

    for copy in rims_in:
        copy.wait()
    x_w[...] = (nn(own_ref[...], slab[0]) + nn(rim_ref[...], rim_in[0])).astype(BF16)
    dy_w[...] = (nn(own_ref[...], slab[1]) + nn(rim_ref[...], rim_in[1])).astype(BF16)
    x = x_w[...].astype(F32)
    average = jnp.mean(x, axis=-1, keepdims=True)
    centred = x - average
    variance = jnp.mean(centred * centred, axis=-1, keepdims=True)
    rstd = lax.rsqrt(variance + 1e-05)
    normed[...] = (centred * rstd).astype(BF16)
    normed_t[...] = nt(eye, normed[...]).astype(BF16)

    def unit(g, w):
        at = slice(w * TOK, (w + 1) * TOK)
        gs = slice(g * gw, (g + 1) * gw)
        cols = [slice(part * c + g * gw, part * c + (g + 1) * gw) for part in range(3)]
        here = normed[at, :]
        q_t, k_t, v_t = [nt(wt[cols[part], :], here).astype(BF16) for part in range(3)]
        k, v = [nn(here, wqkv_ref[:, cols[part]]).astype(BF16) for part in (1, 2)]
        dm_t = nt(wout_ref[gs, :], dy_w[at, :]).astype(BF16)
        q_wide = (nn(q_t, pick) * mine).astype(BF16)
        dm_wide = (nn(dm_t, pick) * mine).astype(BF16)
        s = nn(k, q_wide) * scale + bt[g]
        top = jnp.max(s, axis=0, keepdims=True)
        e = jnp.exp(s - top)
        soft = e * (1.0 / jnp.sum(e, axis=0, keepdims=True))
        a = soft.astype(BF16)
        da = nn(v, dm_wide)
        ds = soft * (da - jnp.sum(soft * da, axis=0, keepdims=True))
        if w == 0:
            db[g] = ds
        else:
            db[g] += ds
        ds = ds.astype(BF16)
        m_t = (nn(v_t, a) * mine).astype(BF16)
        mix[at, gs] = nt(pick, m_t).astype(BF16)
        dq_t = (nn(k_t, ds) * (mine * scale)).astype(BF16)
        dproj[at, cols[0]] = nt(pick, dq_t).astype(BF16)
        dproj[at, cols[1]] = (nt(ds, q_wide) * scale).astype(BF16)
        dproj[at, cols[2]] = nt(a, dm_wide).astype(BF16)

    share = TILES // 2 // nxy

    def put(g, t, value):
        gb[g, t // (TILES // 2), t % (TILES // 2) // share, t % share] = value.astype(BF16)

    def weight_grads(g):
        for part in range(3):
            grad = nn(normed_t[...], dproj[:, part * c + g * gw:part * c + (g + 1) * gw]) * grad_scale
            for r in range(24):
                put(g, part * 24 + r, grad[r * 16:(r + 1) * 16])
        mix_t = nt(eye[:gw, :gw], mix[:, g * gw:(g + 1) * gw]).astype(BF16)
        grad = nn(mix_t, dy_w[...]) * grad_scale
        for k in range(3):
            for r in range(8):
                put(g, 72 + k * 8 + r, grad[r * 16:(r + 1) * 16, k * 128:(k + 1) * 128])

    def core_copy(g):
        return remote(gb.at[g, other], crecv.at[g], core_sem.at[0, g], core_sem.at[1, g], sibling)

    def xy_copy(g, o):
        q, device = xy_at(o)
        return remote(xs.at[g, q], xrecv.at[g, o], xy_sem.at[0, g, o], xy_sem.at[1, g, o], device)

    def z_copy(g, o):
        return remote(zbuf.at[g, z], zbuf.at[g, z], z_sem.at[0, g, o], z_sem.at[1, g, o], z_at(o)[1])

    def ag_copy(g, o):
        mine_at = fin.at[g, core, p]
        return remote(mine_at, mine_at, ag_sem.at[0, g, o], ag_sem.at[1, g, o], xy_at(o)[1])

    def fwd_copy(g, o):
        from_at = fin.at[g, core, (p + nxy - o) % nxy]
        return remote(from_at, from_at, fwd_sem.at[0, g, o], fwd_sem.at[1, g, o], sibling)

    def each(first, count, act):
        pl.loop(first, count)(act)

    def stage_core(g):
        core_copy(g).start()

    def stage_xy(g):
        core_copy(g).wait()
        xs[g] = (gb[g, core].astype(F32) + crecv[g].astype(F32)).astype(BF16)
        each(1, nxy, lambda o: xy_copy(g, o).start())

    def stage_z(g):
        each(1, nxy, lambda o: xy_copy(g, o).wait())
        total = xs[g, p].astype(F32)
        for o in range(1, nxy):
            total += xrecv[g, o].astype(F32)
        zbuf[g, z] = total.astype(BF16)
        each(1, nz, lambda o: z_copy(g, o).start())

    def z_recv(g, o):
        from_at = zbuf.at[g, (z + nz - o) % nz]
        return remote(from_at, from_at, z_sem.at[0, g, o], z_sem.at[1, g, o], z_at(o)[1])

    def stage_ag(g):
        each(1, nz, lambda o: z_copy(g, o).wait_send())
        each(1, nz, lambda o: z_recv(g, o).wait_recv())
        total = zbuf[g, 0].astype(F32)
        for k in range(1, nz):
            total += zbuf[g, k].astype(F32)
        fin[g, core, p] = total.astype(BF16)
        each(1, nxy, lambda o: ag_copy(g, o).start())
        fwd_copy(g, 0).start()

    def ag_recv(g, o):
        from_at = fin.at[g, core, (p + nxy - o) % nxy]
        return remote(from_at, from_at, ag_sem.at[0, g, o], ag_sem.at[1, g, o], xy_at(o)[1])

    def fwd_recv(g, o):
        from_at = fin.at[g, other, (p + nxy - o) % nxy]
        return remote(from_at, from_at, fwd_sem.at[0, g, o], fwd_sem.at[1, g, o], sibling)

    def stage_fwd(g):
        def pass_on(o):
            ag_recv(g, o).wait_recv()
            fwd_copy(g, o).start()

        each(1, nxy, pass_on)

    def stage_end(g):
        each(1, nxy, lambda o: ag_copy(g, o).wait_send())
        each(0, nxy, lambda o: fwd_copy(g, o).wait_send())
        each(0, nxy, lambda o: fwd_recv(g, o).wait_recv())

        def get(t):
            return fin[g, t // (TILES // 2), t % (TILES // 2) // share, t % share].astype(F32)

        for part in range(3):
            for r in range(24):
                gqkv_ref[r * 16:(r + 1) * 16, part * c + g * gw:part * c + (g + 1) * gw] = get(part * 24 + r)
        for k in range(3):
            for r in range(8):
                gout_ref[g * gw + r * 16:g * gw + (r + 1) * 16, k * 128:(k + 1) * 128] = get(72 + k * 8 + r)

    bshare = BIAS_TILES // 2 // nb

    def bcore_copy():
        return remote(bb.at[other], bcrecv, bcore_sem.at[0], bcore_sem.at[1], sibling)

    def bxy_copy(o):
        q, device = b_at(o)
        return remote(bs.at[q], brecv.at[o], bxy_sem.at[0, o], bxy_sem.at[1, o], device)

    def bag_copy(o):
        at = bfin.at[core, b]
        return remote(at, at, bag_sem.at[0, o], bag_sem.at[1, o], b_at(o)[1])

    def bag_recv(o):
        at = bfin.at[core, (b + nb - o) % nb]
        return remote(at, at, bag_sem.at[0, o], bag_sem.at[1, o], b_at(o)[1])

    def bfwd_copy(o):
        at = bfin.at[core, (b + nb - o) % nb]
        return remote(at, at, bfwd_sem.at[0, o], bfwd_sem.at[1, o], sibling)

    def bfwd_recv(o):
        at = bfin.at[other, (b + nb - o) % nb]
        return remote(at, at, bfwd_sem.at[0, o], bfwd_sem.at[1, o], sibling)

    def bias_core():
        rows = jnp.concatenate(
            [
                jnp.concatenate(
                    [
                        db[g, z2 * half:(z2 + 1) * half, j * blk:(j + 1) * blk]
                        for z2 in range(LEV)
                        for g in range(groups)
                    ]
                    + [jnp.zeros((half, 96), F32)],
                    axis=1,
                )
                for j in range(WW)
            ],
            axis=0,
        ).astype(BF16)
        dr = nn(gather_ref[...], rows).astype(BF16)
        for t in range(BIAS_TILES):
            k, r = t // 9, t % 9
            tile = dr[r * 16:(r + 1) * 16, k * 128:(k + 1) * 128] if k < 3 else jnp.zeros((16, 128), BF16)
            bb[t // 16, t % 16 // bshare, t % bshare] = tile
        bcore_copy().start()

    def bias_xy():
        bcore_copy().wait()
        bs[...] = (bb[core].astype(F32) + bcrecv[...].astype(F32)).astype(BF16)
        each(1, nb, lambda o: bxy_copy(o).start())

    def bias_ag():
        each(1, nb, lambda o: bxy_copy(o).wait())
        total = bs[b].astype(F32)
        for o in range(1, nb):
            total += brecv[o].astype(F32)
        bfin[core, b] = total.astype(BF16)
        each(1, nb, lambda o: bag_copy(o).start())
        bfwd_copy(0).start()

    def bias_fwd():
        def pass_on(o):
            bag_recv(o).wait_recv()
            bfwd_copy(o).start()

        each(1, nb, pass_on)

    def bias_end():
        each(1, nb, lambda o: bag_copy(o).wait_send())
        each(0, nb, lambda o: bfwd_copy(o).wait_send())
        each(0, nb, lambda o: bfwd_recv(o).wait_recv())
        for t in range(27):
            k, r = t // 9, t % 9
            dr_ref[r * 16:(r + 1) * 16, k * 128:(k + 1) * 128] = bfin[
                t // 16, t % 16 // bshare, t % bshare
            ].astype(F32)

    stages = (stage_core, stage_xy, stage_z, stage_ag, stage_fwd, stage_end)
    queue = []

    def advance():
        for item in list(queue):
            g, done = item
            stages[done](g)
            item[1] += 1
            if item[1] == len(stages):
                queue.remove(item)

    for g in range(groups):
        for w in range(WINDOWS):
            unit(g, w)
            advance()
        weight_grads(g)
        queue.append([g, 0])
        advance()

    bias_core()
    ow[0] = (x + nn(mix[...], wout_ref[...])).astype(BF16)
    rim_osnd[0] = nn(rimt_ref[...], ow[0]).astype(BF16)
    for copy in rims_out[:3]:
        copy.start()
    advance()
    dn = nt(dproj[...], wqkv_ref[...])
    n = centred * rstd
    dx = (dn - jnp.mean(dn, axis=-1, keepdims=True) - n * jnp.mean(dn * n, axis=-1, keepdims=True)) * rstd
    ow[1] = (dx + dy_w[...].astype(F32)).astype(BF16)
    rim_osnd[1] = nn(rimt_ref[...], ow[1]).astype(BF16)
    for copy in rims_out[3:]:
        copy.start()
    bias_xy()
    advance()

    def finish(f, ref):
        for copy in rims_out[3 * f:3 * f + 3]:
            copy.wait()
        full = (nn(ownt_ref[...], ow[f]) + nn(sendt_ref[...], rim_out[f])).astype(BF16)
        for s in range(SLABS):
            ref[s // WH, s % WH] = full[s * PITCH:s * PITCH + COLS]

    finish(0, out_ref)
    bias_ag()
    advance()
    finish(1, dx_ref)
    bias_fwd()
    advance()
    bias_end()
    while queue:
        advance()


def fused(cells, cot, qkv_weight, out_weight, table, lon_size, lat_size, cells_total):
    c = out_weight.shape[0]
    heads = table.shape[0]
    groups = heads // GROUP
    consts = constants()
    table = table.reshape(groups, GROUP, LEV, LEV, WH, WH * SPAN)
    table = table.transpose(3, 0, 2, 4, 1, 5).reshape(LEV, heads * SLABS, WH * SPAN)
    ins = (cells, cot, qkv_weight, out_weight, table) + consts
    ny, nz = lon_size // 4, lat_size // 2
    nxy, nb = 4 * ny, 2 * ny
    share, bshare = TILES // 2 // nxy, BIAS_TILES // 2 // nb
    vm = pltpu.VMEM
    dma = pltpu.SemaphoreType.DMA
    scratch = [vm(a.shape, a.dtype) for a in ins] + [
        dma((len(ins),)),
        vm((2, SLABS * PITCH, c), BF16),
        vm((2, RIM, c), BF16),
        vm((2, RIM, c), BF16),
        vm((groups, TOK, LANES), F32),
        vm((groups, TOK, LANES), F32),
        vm((ROWS, c), BF16),
        vm((ROWS, c), BF16),
        vm((ROWS, c), BF16),
        vm((c, ROWS), BF16),
        vm((ROWS, c), BF16),
        vm((ROWS, 3 * c), BF16),
        vm((3 * c, c), BF16),
        vm((2, ROWS, c), BF16),
        vm((2, RIM, c), BF16),
        vm((2, RIM, c), BF16),
        vm((groups, 2, nxy, share, 16, 128), BF16),
        vm((groups, nxy, share, 16, 128), BF16),
        vm((groups, nxy, share, 16, 128), BF16),
        vm((groups, nxy, share, 16, 128), BF16),
        vm((groups, nz, share, 16, 128), BF16),
        vm((groups, 2, nxy, share, 16, 128), BF16),
        vm((2, nb, bshare, 16, 128), BF16),
        vm((nb, bshare, 16, 128), BF16),
        vm((nb, bshare, 16, 128), BF16),
        vm((nb, bshare, 16, 128), BF16),
        vm((2, nb, bshare, 16, 128), BF16),
        dma((2, 12)),
        dma((2, groups)),
        dma((2, groups, nxy)),
        dma((2, groups, nz)),
        dma((2, groups, nxy)),
        dma((2, groups, nxy)),
        dma((2,)),
        dma((2, nb)),
        dma((2, nb)),
        dma((2, nb)),
    ]
    kernel = functools.partial(
        body, lon_size, lat_size, groups, (c // heads) ** -0.5, cells_total ** -0.5
    )
    out_shape = (
        jax.ShapeDtypeStruct(cells.shape, BF16),
        jax.ShapeDtypeStruct(cells.shape, BF16),
        jax.ShapeDtypeStruct((c, 3 * c), F32),
        jax.ShapeDtypeStruct((c, c), F32),
        jax.ShapeDtypeStruct((144, 384), F32),
    )
    return pl.pallas_call(
        kernel,
        out_shape=out_shape,
        in_specs=[pl.BlockSpec(memory_space=pl.ANY)] * len(ins),
        out_specs=(pl.BlockSpec(memory_space=pltpu.VMEM),) * len(out_shape),
        scratch_shapes=scratch,
        compiler_params=pltpu.CompilerParams(
            vmem_limit_bytes=60 * 1024 * 1024, collective_id=0, has_side_effects=True
        ),
        cost_estimate=pl.CostEstimate(flops=6_000_000_000, bytes_accessed=10_000_000, transcendentals=800_000),
    )(*ins)


def on_device(cells, qkv_weight, out_weight, earth_bias, cotangent):
    lon_size, lat_size = lax.axis_size("lon"), lax.axis_size("lat")
    heads = earth_bias.shape[1]
    cells_total = LEV * cells.shape[1] * cells.shape[2] * lon_size * lat_size
    out, dx, gqkv, gout, dr = fused(
        cells, cotangent, qkv_weight, out_weight, earth_bias[0], lon_size, lat_size, cells_total
    )
    dr = dr[: WH * SPAN, : 2 * heads * SLABS].reshape(WH * SPAN, LEV, heads // GROUP, LEV, WH, GROUP)
    dr = dr.transpose(2, 5, 3, 1, 4, 0).reshape(earth_bias.shape)
    return out, dx, gqkv, gout, dr


def solution(mesh):
    grid = P(None, "lat", "lon", None)
    return jax.shard_map(
        on_device,
        mesh=mesh,
        in_specs=(grid, P(), P(), P("lat", None, None), grid),
        out_specs=(grid, grid, P(), P(), P("lat", None, None)),
        check_vma=False,
    )
```

time: 445 us -> 104 us (0.23)
  waiting for transfers between devices: 380 us -> 0 us
  Pallas kernels: 13.6 us -> 90.7 us
  starting transfers between devices: 16.3 us -> 0 us
  between operations: 14.2 us -> 0.72 us
  local copies, waits for them, and re-layouts: 16.7 us -> 10.5 us
    psum x2 -> x0, waiting for transfers between devices: 364 us -> none  [the longest x1 263 us: on_device(): grad_qkv, grad_out = lax.psum((grad_qkv, grad_out), ('lon', 'lat'))]
    pallas_call x1, Pallas kernels: 13.6 us -> 90.7 us  [fused(): pl.pallas_call(kernel, out_shape=out_shape, in_specs=[pl.BlockSpec(memory...]
    ppermute x4 -> x0, starting transfers between devices: 16.2 us -> none  [passed_along(): return lax.ppermute(block, axis, route)]
    ppermute x4 -> x0, waiting for transfers between devices: 15.7 us -> none  [passed_along(): return lax.ppermute(block, axis, route)]
    unnamed x19 -> x16, local copies, waits for them, and re-layouts: 9.38 us -> 6.97 us
  transfers between devices with their start and end apart: 6 -> 0, of which waited for: 5 -> 0; matrix products, arithmetic and copies ran while one was open for 2% -> 0% of each run, Pallas kernels for 0% -> 0%
where the time goes in v2:
time: 104 us; the launch traced here: 103 us
  Pallas kernels  90.7 us (87%)
  local copies, waits for them, and re-layouts  10.5 us (10%)
  other arithmetic  1.36 us (1%)
    pallas_call x1, Pallas kernels, fused(): pl.pallas_call(kernel, out_shape=out_shape, in_specs=[pl.BlockSpec(memory...  90.7 us
    unnamed x16, local copies, waits for them, and re-layouts  6.97 us

profile of v2, /device:TPU:1, one launch (start us, length us, event | category | flops | bytes accessed | tf_op | source)
XLA Modules:
  0.0 103.3 jit_solution(7907483520646125569)
XLA Ops:
  0.6 0.0 copy-start.4
  0.6 0.0 copy-start.3
  0.7 1.4 %reduce = f32[12,3312]{1,0:T(8,128)S(1)} reduce(f32[1,12,3312]{2,0,1:T(1,128)} %param.18, f32[]{:T(128)} %constant.33), dimensions={0}, to_apply=%param.18.reduce_sub_computation | reduce | bytes 317956 | tf_op args[3]
  2.0 0.4 reshape_squeeze.3
  2.4 0.2 copy.26
  2.5 0.7 copy.29.refs_4_
  3.3 0.0 copy-done.3
  3.3 0.8 copy.27.refs_0_
  4.1 0.0 copy-done.4
  4.1 0.8 copy.28.refs_1_
  4.9 90.7 %shard_map.182 = (bf16[2,6,36,384]{3,2,1,0:T(8,128)(2,1)}, bf16[2,6,36,384]{3,2,1,0:T(8,128)(2,1)}, f32[384,1152]{1,0:T(8,128)}, f32[384,384]{1,0:T(8,128)}, f32[144,384]{1,0:T(8,128)}) custom-call(bf16[2,6,36,384]{3,2,1,0:T(8,128)(2,1)} %copy.27.refs_0_, bf16[2,6,36,384]{3,2,1,0:T(8,128)(2,1)} %copy.28.refs_1_, bf16[384,1152]{1,0:T(8,128)(2,1)} %refs_2_.1, ...), custom_call_target="tpu_custom_call" | custom-call | flops 6000000000 | bytes 10000000 | tf_op jit(solution)/shard_map/pallas_call | solution.py:549
  95.6 0.0 copy-start.2
  95.6 0.0 copy-start
  95.6 2.1 %copy.32 = bf16[2,6,36,384]{3,0,2,1:T(2,128)(2,1)} copy(bf16[2,6,36,384]{3,2,1,0:T(8,128)(2,1)} %get-tuple-element.20) | data formatting | bytes 663552
  97.7 1.1 %copy.30 = f32[138,288]{0,1:T(8,128)S(1)} copy(f32[138,288]{1,0:T(8,128)} %bitcast.9) | data formatting | bytes 317952 | tf_op jit(solution)/shard_map/slice | solution.py:569
  98.8 0.1 reshape.20
  98.9 0.1 copy.31
  99.0 1.1 %reshape.22 = f32[1,12,3312]{2,0,1:T(1,128)} reshape(f32[3,4,2,2,6,138]{5,4,3,2,1,0:T(8,128)S(1)} %copy.31) | data formatting | bytes 317952 | tf_op jit(solution)/shard_map/reshape | solution.py:570
  100.1 0.0 copy-done.2
  100.1 1.0 copy.33
  101.0 0.0 copy-done
  101.1 0.0 copy-start.1
  101.1 1.2 %copy.37 = f32[384,1152]{1,0:T(8,128)} copy(f32[384,1152]{1,0:T(8,128)S(1)} %copy-done) | data formatting | bytes 3538944
  102.3 0.3 copy-done.1
  102.5 0.8 copy.38
Async XLA Ops:
  0.6 3.4 %copy-start.4 = (bf16[2,6,36,384]{3,0,2,1:T(2,128)(2,1)S(1)}, bf16[2,6,36,384]{3,0,2,1:T(2,128)(2,1)}, u32[]{:S(2)}) copy-start(bf16[2,6,36,384]{3,0,2,1:T(2,128)(2,1)} %param.19) | copy-start | bytes 995332
  0.6 2.6 %copy-start.3 = (bf16[2,6,36,384]{3,0,2,1:T(2,128)(2,1)S(1)}, bf16[2,6,36,384]{3,0,2,1:T(2,128)(2,1)}, u32[]{:S(2)}) copy-start(bf16[2,6,36,384]{3,0,2,1:T(2,128)(2,1)} %param.15) | copy-start | bytes 995332
  95.6 4.5 %copy-start.2 = (bf16[2,6,36,384]{3,2,1,0:T(8,128)(2,1)S(1)}, bf16[2,6,36,384]{3,2,1,0:T(8,128)(2,1)}, u32[]{:S(2)}) copy-start(bf16[2,6,36,384]{3,2,1,0:T(8,128)(2,1)} %get-tuple-element.21) | copy-start | bytes 995332
  95.6 5.4 %copy-start = (f32[384,1152]{1,0:T(8,128)S(1)}, f32[384,1152]{1,0:T(8,128)}, u32[]{:S(2)}) copy-start(f32[384,1152]{1,0:T(8,128)} %get-tuple-element.32) | copy-start | bytes 5308420
  101.1 1.5 %copy-start.1 = (f32[384,384]{1,0:T(8,128)S(1)}, f32[384,384]{1,0:T(8,128)}, u32[]{:S(2)}) copy-start(f32[384,384]{1,0:T(8,128)} %get-tuple-element.33) | copy-start | bytes 1769476

commit v3 on v2

--- a/solution.py
+++ b/solution.py
@@ -25,6 +25,8 @@
 RIM = 304
 TILES = 96
 BIAS_TILES = 32
+CHUNKS = ((0, 1), (2,))
+X_HI = 2
 F32 = jnp.float32
 BF16 = jnp.bfloat16
 MESH = pl.DeviceIdType.MESH
@@ -92,11 +94,11 @@
     (cells_v, cot_v, wqkv_ref, wout_ref, r_ref,
      spread_ref, gather_ref, pick_ref, cross_ref, own_ref, rim_ref, send_ref, ownt_ref, rimt_ref, sendt_ref,
      load_sem, slab, rim_snd, rim_in, bt, db, x_w, dy_w, normed, normed_t, mix, dproj, wt, ow, rim_osnd, rim_out,
-     gb, crecv, xs, xrecv, zbuf, fin, bb, bcrecv, bs, brecv, bfin,
-     halo_sem, core_sem, xy_sem, z_sem, ag_sem, fwd_sem, bcore_sem, bxy_sem, bag_sem, bfwd_sem) = refs[N_IN + 5:]
+     halo_sem, *comm) = refs[N_IN + 5:]
+    chunk_refs = [comm[i * 10:i * 10 + 10] for i in range(len(CHUNKS))]
+    (bb, bcrecv, bs, bxrecv, by, byrecv, bfin, b_sem) = comm[len(CHUNKS) * 10:]
     c = wout_ref.shape[0]
-    ny, nz = lon_size // 4, lat_size // 2
-    nxy, nb = 4 * ny, 2 * ny
+    n, nz = lon_size // 4, lat_size // X_HI
     half = WH * WW
     blk = SLABS * GROUP
     gw = GROUP * HEAD
@@ -104,26 +106,29 @@
     lon, lat = lax.axis_index("lon"), lax.axis_index("lat")
     core, x_lo, y = lon % 2, lon // 2 % 2, lon // 4
     x_hi, z = lat // nz, lat % nz
-    p = y * 4 + x_hi * 2 + x_lo
-    b = y * 2 + x_lo
+    x = x_hi * 2 + x_lo
     other = 1 - core
+    one = jnp.where(core == 0, x, y)
+    two = jnp.where(core == 0, y, x)
 
     def dev(lon_at, lat_at):
         return {"lon": lon_at, "lat": lat_at}
 
+    def chip(x_at, y_at):
+        return dev((y_at * 2 + x_at % 2) * 2 + core, x_at // 2 * nz + z)
+
     sibling = dev(lon + 1 - 2 * core, lat)
-
-    def xy_at(o):
-        q = (p + o) % nxy
-        return q, dev((q // 4 * 2 + q % 2) * 2 + core, q // 2 % 2 * nz + z)
-
-    def b_at(o):
-        q = (b + o) % nb
-        return q, dev(q * 2 + core, lat)
-
-    def z_at(o):
-        q = (z + o) % nz
-        return q, dev(lon, x_hi * nz + q)
+    ones, twos, zs, ys = [], [], [], []
+    for o in range(1, n):
+        q = (one + o) % n
+        ones.append((q, chip(jnp.where(core == 0, q, x), jnp.where(core == 0, y, q)), (one + n - o) % n))
+        q = (two + o) % n
+        twos.append((q, chip(jnp.where(core == 0, x, q), jnp.where(core == 0, q, y)), (two + n - o) % n))
+        q = (y + o) % n
+        ys.append((q, chip(x, q), (y + n - o) % n))
+    for o in range(1, nz):
+        zs.append((dev(lon, x_hi * nz + (z + o) % nz), (z + nz - o) % nz))
+    pair = dev((y * 2 + 1 - x_lo) * 2 + core, lat)
 
     lon_prev, lon_next = (lon + lon_size - 1) % lon_size, (lon + 1) % lon_size
     lat_prev, lat_next = (lat + lat_size - 1) % lat_size, (lat + 1) % lat_size
@@ -148,16 +153,10 @@
     def greet(device):
         pl.semaphore_signal(barrier, inc=1, device_id=device, device_id_type=MESH)
 
-    for device in back + ahead + (sibling,):
+    partners = back + ahead + (sibling, pair)
+    partners += tuple(d for _, d, _ in ones + twos + ys) + tuple(d for d, _ in zs)
+    for device in partners:
         greet(device)
-
-    @pl.loop(1, nxy)
-    def _(o):
-        greet(xy_at(o)[1])
-
-    @pl.loop(1, nz)
-    def _(o):
-        greet(z_at(o)[1])
 
     slab[...] = jnp.zeros_like(slab)
     for f in range(2):
@@ -168,7 +167,7 @@
     loads[2].wait()
     for f in range(2):
         rim_snd[f] = nn(send_ref[...], slab[f]).astype(BF16)
-    pl.semaphore_wait(barrier, 7 + (nxy - 1) + (nz - 1))
+    pl.semaphore_wait(barrier, len(partners))
 
     def rim_copies(snd, rcv, devices, base):
         return [
@@ -218,9 +217,9 @@
         copy.wait()
     x_w[...] = (nn(own_ref[...], slab[0]) + nn(rim_ref[...], rim_in[0])).astype(BF16)
     dy_w[...] = (nn(own_ref[...], slab[1]) + nn(rim_ref[...], rim_in[1])).astype(BF16)
-    x = x_w[...].astype(F32)
-    average = jnp.mean(x, axis=-1, keepdims=True)
-    centred = x - average
+    cells = x_w[...].astype(F32)
+    average = jnp.mean(cells, axis=-1, keepdims=True)
+    centred = cells - average
     variance = jnp.mean(centred * centred, axis=-1, keepdims=True)
     rstd = lax.rsqrt(variance + 1e-05)
     normed[...] = (centred * rstd).astype(BF16)
@@ -255,10 +254,19 @@
         dproj[at, cols[1]] = (nt(ds, q_wide) * scale).astype(BF16)
         dproj[at, cols[2]] = nt(a, dm_wide).astype(BF16)
 
-    share = TILES // 2 // nxy
+    def chunk_of(g):
+        return next((i, groups_in.index(g)) for i, groups_in in enumerate(CHUNKS) if g in groups_in)
+
+    def tile_at(g, t):
+        i, k = chunk_of(g)
+        t += k * TILES
+        half_tiles = len(CHUNKS[i]) * TILES // 2
+        share = half_tiles // (n * n)
+        return i, (t // half_tiles, t % half_tiles // (n * share), t % (n * share) // share, t % share)
 
     def put(g, t, value):
-        gb[g, t // (TILES // 2), t % (TILES // 2) // share, t % share] = value.astype(BF16)
+        i, at = tile_at(g, t)
+        chunk_refs[i][0][at] = value.astype(BF16)
 
     def weight_grads(g):
         for part in range(3):
@@ -271,79 +279,116 @@
             for r in range(8):
                 put(g, 72 + k * 8 + r, grad[r * 16:(r + 1) * 16, k * 128:(k + 1) * 128])
 
-    def core_copy(g):
-        return remote(gb.at[g, other], crecv.at[g], core_sem.at[0, g], core_sem.at[1, g], sibling)
-
-    def xy_copy(g, o):
-        q, device = xy_at(o)
-        return remote(xs.at[g, q], xrecv.at[g, o], xy_sem.at[0, g, o], xy_sem.at[1, g, o], device)
-
-    def z_copy(g, o):
-        return remote(zbuf.at[g, z], zbuf.at[g, z], z_sem.at[0, g, o], z_sem.at[1, g, o], z_at(o)[1])
-
-    def ag_copy(g, o):
-        mine_at = fin.at[g, core, p]
-        return remote(mine_at, mine_at, ag_sem.at[0, g, o], ag_sem.at[1, g, o], xy_at(o)[1])
-
-    def fwd_copy(g, o):
-        from_at = fin.at[g, core, (p + nxy - o) % nxy]
-        return remote(from_at, from_at, fwd_sem.at[0, g, o], fwd_sem.at[1, g, o], sibling)
-
-    def each(first, count, act):
-        pl.loop(first, count)(act)
-
-    def stage_core(g):
-        core_copy(g).start()
-
-    def stage_xy(g):
-        core_copy(g).wait()
-        xs[g] = (gb[g, core].astype(F32) + crecv[g].astype(F32)).astype(BF16)
-        each(1, nxy, lambda o: xy_copy(g, o).start())
-
-    def stage_z(g):
-        each(1, nxy, lambda o: xy_copy(g, o).wait())
-        total = xs[g, p].astype(F32)
-        for o in range(1, nxy):
-            total += xrecv[g, o].astype(F32)
-        zbuf[g, z] = total.astype(BF16)
-        each(1, nz, lambda o: z_copy(g, o).start())
-
-    def z_recv(g, o):
-        from_at = zbuf.at[g, (z + nz - o) % nz]
-        return remote(from_at, from_at, z_sem.at[0, g, o], z_sem.at[1, g, o], z_at(o)[1])
-
-    def stage_ag(g):
-        each(1, nz, lambda o: z_copy(g, o).wait_send())
-        each(1, nz, lambda o: z_recv(g, o).wait_recv())
-        total = zbuf[g, 0].astype(F32)
-        for k in range(1, nz):
-            total += zbuf[g, k].astype(F32)
-        fin[g, core, p] = total.astype(BF16)
-        each(1, nxy, lambda o: ag_copy(g, o).start())
-        fwd_copy(g, 0).start()
-
-    def ag_recv(g, o):
-        from_at = fin.at[g, core, (p + nxy - o) % nxy]
-        return remote(from_at, from_at, ag_sem.at[0, g, o], ag_sem.at[1, g, o], xy_at(o)[1])
-
-    def fwd_recv(g, o):
-        from_at = fin.at[g, other, (p + nxy - o) % nxy]
-        return remote(from_at, from_at, fwd_sem.at[0, g, o], fwd_sem.at[1, g, o], sibling)
-
-    def stage_fwd(g):
-        def pass_on(o):
-            ag_recv(g, o).wait_recv()
-            fwd_copy(g, o).start()
-
-        each(1, nxy, pass_on)
-
-    def stage_end(g):
-        each(1, nxy, lambda o: ag_copy(g, o).wait_send())
-        each(0, nxy, lambda o: fwd_copy(g, o).wait_send())
-        each(0, nxy, lambda o: fwd_recv(g, o).wait_recv())
-
+    class Chain:
+        def __init__(self, refs):
+            (self.gb, self.crecv, self.xs, self.arecv, self.ys, self.brecv, self.zbuf, self.fin,
+             self.sem, self.zsem) = refs
+
+        def copy(self, k, src, dst, device):
+            return remote(src, dst, self.sem.at[0, k], self.sem.at[1, k], device)
+
+        def core_copy(self):
+            return self.copy(0, self.gb.at[other], self.crecv, sibling)
+
+        def one_copies(self):
+            return [self.copy(1 + o, self.xs.at[q], self.arecv.at[o], d) for o, (q, d, _) in enumerate(ones)]
+
+        def two_copies(self):
+            return [self.copy(4 + o, self.ys.at[q], self.brecv.at[o], d) for o, (q, d, _) in enumerate(twos)]
+
+        def z_copies(self, here=True):
+            at = [z if here else q for _, q in zs]
+            return [
+                remote(self.zbuf.at[at[o]], self.zbuf.at[at[o]], self.zsem.at[0, o], self.zsem.at[1, o], d)
+                for o, (d, _) in enumerate(zs)
+            ]
+
+        def back_two(self, here=True):
+            at = [two if here else q for _, _, q in twos]
+            return [
+                self.copy(7 + o, self.fin.at[core, one, at[o]], self.fin.at[core, one, at[o]], d)
+                for o, (_, d, _) in enumerate(twos)
+            ]
+
+        def back_one(self, here=True):
+            at = [one if here else q for _, _, q in ones]
+            return [
+                self.copy(10 + o, self.fin.at[core, at[o]], self.fin.at[core, at[o]], d)
+                for o, (_, d, _) in enumerate(ones)
+            ]
+
+        def back_core(self, o, half_at):
+            at = one if o == 0 else ones[o - 1][2]
+            return self.copy(13 + o, self.fin.at[half_at, at], self.fin.at[half_at, at], sibling)
+
+        def start(self):
+            self.core_copy().start()
+
+        def first(self):
+            self.core_copy().wait()
+            self.xs[...] = (self.gb[core].astype(F32) + self.crecv[...].astype(F32)).astype(BF16)
+            for copy in self.one_copies():
+                copy.start()
+
+        def second(self):
+            for copy in self.one_copies():
+                copy.wait()
+            total = self.xs[one].astype(F32)
+            for o in range(n - 1):
+                total += self.arecv[o].astype(F32)
+            self.ys[...] = total.astype(BF16)
+            for copy in self.two_copies():
+                copy.start()
+
+        def third(self):
+            for copy in self.two_copies():
+                copy.wait()
+            total = self.ys[two].astype(F32)
+            for o in range(n - 1):
+                total += self.brecv[o].astype(F32)
+            self.zbuf[z] = total.astype(BF16)
+            for copy in self.z_copies():
+                copy.start()
+
+        def fourth(self):
+            for copy in self.z_copies():
+                copy.wait_send()
+            for copy in self.z_copies(False):
+                copy.wait_recv()
+            total = self.zbuf[0].astype(F32)
+            for k in range(1, nz):
+                total += self.zbuf[k].astype(F32)
+            self.fin[core, one, two] = total.astype(BF16)
+            for copy in self.back_two():
+                copy.start()
+
+        def fifth(self):
+            for copy in self.back_two():
+                copy.wait_send()
+            for copy in self.back_two(False):
+                copy.wait_recv()
+            for copy in self.back_one():
+                copy.start()
+            self.back_core(0, core).start()
+
+        def sixth(self):
+            for o, copy in enumerate(self.back_one(False)):
+                copy.wait_recv()
+                self.back_core(o + 1, core).start()
+
+        def last(self):
+            for copy in self.back_one():
+                copy.wait_send()
+            for o in range(n):
+                self.back_core(o, core).wait_send()
+                self.back_core(o, other).wait_recv()
+
+    chains = [Chain(r) for r in chunk_refs]
+
+    def unpack(g):
         def get(t):
-            return fin[g, t // (TILES // 2), t % (TILES // 2) // share, t % share].astype(F32)
+            i, at = tile_at(g, t)
+            return chains[i].fin[at].astype(F32)
 
         for part in range(3):
             for r in range(24):
@@ -352,30 +397,32 @@
             for r in range(8):
                 gout_ref[g * gw + r * 16:g * gw + (r + 1) * 16, k * 128:(k + 1) * 128] = get(72 + k * 8 + r)
 
-    bshare = BIAS_TILES // 2 // nb
+    bshare = BIAS_TILES // (4 * n)
+
+    def bcopy(k, src, dst, device):
+        return remote(src, dst, b_sem.at[0, k], b_sem.at[1, k], device)
 
     def bcore_copy():
-        return remote(bb.at[other], bcrecv, bcore_sem.at[0], bcore_sem.at[1], sibling)
-
-    def bxy_copy(o):
-        q, device = b_at(o)
-        return remote(bs.at[q], brecv.at[o], bxy_sem.at[0, o], bxy_sem.at[1, o], device)
-
-    def bag_copy(o):
-        at = bfin.at[core, b]
-        return remote(at, at, bag_sem.at[0, o], bag_sem.at[1, o], b_at(o)[1])
-
-    def bag_recv(o):
-        at = bfin.at[core, (b + nb - o) % nb]
-        return remote(at, at, bag_sem.at[0, o], bag_sem.at[1, o], b_at(o)[1])
-
-    def bfwd_copy(o):
-        at = bfin.at[core, (b + nb - o) % nb]
-        return remote(at, at, bfwd_sem.at[0, o], bfwd_sem.at[1, o], sibling)
-
-    def bfwd_recv(o):
-        at = bfin.at[other, (b + nb - o) % nb]
-        return remote(at, at, bfwd_sem.at[0, o], bfwd_sem.at[1, o], sibling)
+        return bcopy(0, bb.at[other], bcrecv, sibling)
+
+    def bx_copy():
+        return bcopy(1, bs.at[1 - x_lo], bxrecv, pair)
+
+    def by_copies():
+        return [bcopy(2 + o, by.at[q], byrecv.at[o], d) for o, (q, d, _) in enumerate(ys)]
+
+    def by_back(here=True):
+        at = [y if here else q for _, _, q in ys]
+        return [
+            bcopy(5 + o, bfin.at[core, x_lo, at[o]], bfin.at[core, x_lo, at[o]], d)
+            for o, (_, d, _) in enumerate(ys)
+        ]
+
+    def bx_back(x_at):
+        return bcopy(8, bfin.at[core, x_at], bfin.at[core, x_at], pair)
+
+    def bcore_back(half_at):
+        return bcopy(9, bfin.at[half_at], bfin.at[half_at], sibling)
 
     def bias_core():
         rows = jnp.concatenate(
@@ -397,74 +444,51 @@
         for t in range(BIAS_TILES):
             k, r = t // 9, t % 9
             tile = dr[r * 16:(r + 1) * 16, k * 128:(k + 1) * 128] if k < 3 else jnp.zeros((16, 128), BF16)
-            bb[t // 16, t % 16 // bshare, t % bshare] = tile
+            bb[bias_at(t)] = tile
         bcore_copy().start()
 
-    def bias_xy():
+    def bias_at(t):
+        return t // 16, t % 16 // (n * bshare), t % (n * bshare) // bshare, t % bshare
+
+    def bias_x():
         bcore_copy().wait()
         bs[...] = (bb[core].astype(F32) + bcrecv[...].astype(F32)).astype(BF16)
-        each(1, nb, lambda o: bxy_copy(o).start())
-
-    def bias_ag():
-        each(1, nb, lambda o: bxy_copy(o).wait())
-        total = bs[b].astype(F32)
-        for o in range(1, nb):
-            total += brecv[o].astype(F32)
-        bfin[core, b] = total.astype(BF16)
-        each(1, nb, lambda o: bag_copy(o).start())
-        bfwd_copy(0).start()
-
-    def bias_fwd():
-        def pass_on(o):
-            bag_recv(o).wait_recv()
-            bfwd_copy(o).start()
-
-        each(1, nb, pass_on)
+        bx_copy().start()
+
+    def bias_y():
+        bx_copy().wait()
+        by[...] = (bs[x_lo].astype(F32) + bxrecv[...].astype(F32)).astype(BF16)
+        for copy in by_copies():
+            copy.start()
+
+    def bias_back_y():
+        for copy in by_copies():
+            copy.wait()
+        total = by[y].astype(F32)
+        for o in range(n - 1):
+            total += byrecv[o].astype(F32)
+        bfin[core, x_lo, y] = total.astype(BF16)
+        for copy in by_back():
+            copy.start()
+
+    def bias_back_x():
+        for copy in by_back():
+            copy.wait_send()
+        for copy in by_back(False):
+            copy.wait_recv()
+        bx_back(x_lo).start()
+
+    def bias_back_core():
+        bx_back(x_lo).wait_send()
+        bx_back(1 - x_lo).wait_recv()
+        bcore_back(core).start()
 
     def bias_end():
-        each(1, nb, lambda o: bag_copy(o).wait_send())
-        each(0, nb, lambda o: bfwd_copy(o).wait_send())
-        each(0, nb, lambda o: bfwd_recv(o).wait_recv())
+        bcore_back(core).wait_send()
+        bcore_back(other).wait_recv()
         for t in range(27):
             k, r = t // 9, t % 9
-            dr_ref[r * 16:(r + 1) * 16, k * 128:(k + 1) * 128] = bfin[
-                t // 16, t % 16 // bshare, t % bshare
-            ].astype(F32)
-
-    stages = (stage_core, stage_xy, stage_z, stage_ag, stage_fwd, stage_end)
-    queue = []
-
-    def advance():
-        for item in list(queue):
-            g, done = item
-            stages[done](g)
-            item[1] += 1
-            if item[1] == len(stages):
-                queue.remove(item)
-
-    for g in range(groups):
-        for w in range(WINDOWS):
-            unit(g, w)
-            advance()
-        weight_grads(g)
-        queue.append([g, 0])
-        advance()
-
-    bias_core()
-    ow[0] = (x + nn(mix[...], wout_ref[...])).astype(BF16)
-    rim_osnd[0] = nn(rimt_ref[...], ow[0]).astype(BF16)
-    for copy in rims_out[:3]:
-        copy.start()
-    advance()
-    dn = nt(dproj[...], wqkv_ref[...])
-    n = centred * rstd
-    dx = (dn - jnp.mean(dn, axis=-1, keepdims=True) - n * jnp.mean(dn * n, axis=-1, keepdims=True)) * rstd
-    ow[1] = (dx + dy_w[...].astype(F32)).astype(BF16)
-    rim_osnd[1] = nn(rimt_ref[...], ow[1]).astype(BF16)
-    for copy in rims_out[3:]:
-        copy.start()
-    bias_xy()
-    advance()
+            dr_ref[r * 16:(r + 1) * 16, k * 128:(k + 1) * 128] = bfin[bias_at(t)].astype(F32)
 
     def finish(f, ref):
         for copy in rims_out[3 * f:3 * f + 3]:
@@ -473,15 +497,54 @@
         for s in range(SLABS):
             ref[s // WH, s % WH] = full[s * PITCH:s * PITCH + COLS]
 
+    early, late = chains
+    for g in (0, 1):
+        for w in range(WINDOWS):
+            unit(g, w)
+        weight_grads(g)
+    early.start()
+    unit(2, 0)
+    early.first()
+    unit(2, 1)
+    unit(2, 2)
+    weight_grads(2)
+    late.start()
+    bias_core()
+    early.second()
+    ow[0] = (cells + nn(mix[...], wout_ref[...])).astype(BF16)
+    rim_osnd[0] = nn(rimt_ref[...], ow[0]).astype(BF16)
+    late.first()
+    for copy in rims_out[:3]:
+        copy.start()
+    dn = nt(dproj[...], wqkv_ref[...])
+    n_w = centred * rstd
+    dx = (dn - jnp.mean(dn, axis=-1, keepdims=True) - n_w * jnp.mean(dn * n_w, axis=-1, keepdims=True)) * rstd
+    ow[1] = (dx + dy_w[...].astype(F32)).astype(BF16)
+    rim_osnd[1] = nn(rimt_ref[...], ow[1]).astype(BF16)
+    late.second()
+    for copy in rims_out[3:]:
+        copy.start()
+    bias_x()
+    early.third()
+    bias_y()
+    late.third()
+    bias_back_y()
+    early.fourth()
+    late.fourth()
+    bias_back_x()
+    early.fifth()
+    late.fifth()
+    bias_back_core()
+    early.sixth()
     finish(0, out_ref)
-    bias_ag()
-    advance()
+    late.sixth()
     finish(1, dx_ref)
-    bias_fwd()
-    advance()
     bias_end()
-    while queue:
-        advance()
+    early.last()
+    unpack(0)
+    unpack(1)
+    late.last()
+    unpack(2)
 
 
 def fused(cells, cot, qkv_weight, out_weight, table, lon_size, lat_size, cells_total):
@@ -492,9 +555,8 @@
     table = table.reshape(groups, GROUP, LEV, LEV, WH, WH * SPAN)
     table = table.transpose(3, 0, 2, 4, 1, 5).reshape(LEV, heads * SLABS, WH * SPAN)
     ins = (cells, cot, qkv_weight, out_weight, table) + consts
-    ny, nz = lon_size // 4, lat_size // 2
-    nxy, nb = 4 * ny, 2 * ny
-    share, bshare = TILES // 2 // nxy, BIAS_TILES // 2 // nb
+    n, nz = lon_size // 4, lat_size // X_HI
+    bshare = BIAS_TILES // (4 * n)
     vm = pltpu.VMEM
     dma = pltpu.SemaphoreType.DMA
     scratch = [vm(a.shape, a.dtype) for a in ins] + [
@@ -514,27 +576,32 @@
         vm((2, ROWS, c), BF16),
         vm((2, RIM, c), BF16),
         vm((2, RIM, c), BF16),
-        vm((groups, 2, nxy, share, 16, 128), BF16),
-        vm((groups, nxy, share, 16, 128), BF16),
-        vm((groups, nxy, share, 16, 128), BF16),
-        vm((groups, nxy, share, 16, 128), BF16),
-        vm((groups, nz, share, 16, 128), BF16),
-        vm((groups, 2, nxy, share, 16, 128), BF16),
-        vm((2, nb, bshare, 16, 128), BF16),
-        vm((nb, bshare, 16, 128), BF16),
-        vm((nb, bshare, 16, 128), BF16),
-        vm((nb, bshare, 16, 128), BF16),
-        vm((2, nb, bshare, 16, 128), BF16),
         dma((2, 12)),
-        dma((2, groups)),
-        dma((2, groups, nxy)),
-        dma((2, groups, nz)),
-        dma((2, groups, nxy)),
-        dma((2, groups, nxy)),
-        dma((2,)),
-        dma((2, nb)),
-        dma((2, nb)),
-        dma((2, nb)),
+    ]
+    tile = (16, 128)
+    for groups_in in CHUNKS:
+        share = len(groups_in) * TILES // (2 * n * n)
+        scratch += [
+            vm((2, n, n, share) + tile, BF16),
+            vm((n, n, share) + tile, BF16),
+            vm((n, n, share) + tile, BF16),
+            vm((n - 1, n, share) + tile, BF16),
+            vm((n, share) + tile, BF16),
+            vm((n - 1, share) + tile, BF16),
+            vm((nz, share) + tile, BF16),
+            vm((2, n, n, share) + tile, BF16),
+            dma((2, 17)),
+            dma((2, nz)),
+        ]
+    scratch += [
+        vm((2, 2, n, bshare) + tile, BF16),
+        vm((2, n, bshare) + tile, BF16),
+        vm((2, n, bshare) + tile, BF16),
+        vm((n, bshare) + tile, BF16),
+        vm((n, bshare) + tile, BF16),
+        vm((n - 1, bshare) + tile, BF16),
+        vm((2, 2, n, bshare) + tile, BF16),
+        dma((2, 10)),
     ]
     kernel = functools.partial(
         body, lon_size, lat_size, groups, (c // heads) ** -0.5, cells_total ** -0.5

time: 104 us -> 83.7 us (0.80)
  Pallas kernels: 90.7 us -> 70.9 us
    pallas_call x1, Pallas kernels: 90.7 us -> 70.9 us  [fused(): pl.pallas_call(kernel, out_shape=out_shape, in_specs=[pl.BlockSpec(memory...]
where the time goes in v3:
time: 83.7 us; the launch traced here: 83.5 us
  Pallas kernels  70.9 us (85%)
  local copies, waits for them, and re-layouts  10.5 us (13%)
  other arithmetic  1.36 us (2%)
    pallas_call x1, Pallas kernels, fused(): pl.pallas_call(kernel, out_shape=out_shape, in_specs=[pl.BlockSpec(memory...  70.9 us
    unnamed x16, local copies, waits for them, and re-layouts  6.97 us

profile of v3, /device:TPU:1, one launch (start us, length us, event | category | flops | bytes accessed | tf_op | source)
XLA Modules:
  0.0 83.5 jit_solution(9928402195368278492)
XLA Ops:
  0.6 0.0 copy-start.4
  0.6 0.0 copy-start.3
  0.7 1.4 %reduce = f32[12,3312]{1,0:T(8,128)S(1)} reduce(f32[1,12,3312]{2,0,1:T(1,128)} %param.18, f32[]{:T(128)} %constant.33), dimensions={0}, to_apply=%param.18.reduce_sub_computation | reduce | bytes 317956 | tf_op args[3]
  2.0 0.4 reshape_squeeze.3
  2.4 0.2 copy.26
  2.5 0.7 copy.29.refs_4_
  3.3 0.0 copy-done.3
  3.3 0.8 copy.27.refs_0_
  4.1 0.0 copy-done.4
  4.1 0.8 copy.28.refs_1_
  4.9 70.9 %shard_map.182 = (bf16[2,6,36,384]{3,2,1,0:T(8,128)(2,1)}, bf16[2,6,36,384]{3,2,1,0:T(8,128)(2,1)}, f32[384,1152]{1,0:T(8,128)}, f32[384,384]{1,0:T(8,128)}, f32[144,384]{1,0:T(8,128)}) custom-call(bf16[2,6,36,384]{3,2,1,0:T(8,128)(2,1)} %copy.27.refs_0_, bf16[2,6,36,384]{3,2,1,0:T(8,128)(2,1)} %copy.28.refs_1_, bf16[384,1152]{1,0:T(8,128)(2,1)} %refs_2_.1, ...), custom_call_target="tpu_custom_call" | custom-call | flops 6000000000 | bytes 10000000 | tf_op jit(solution)/shard_map/pallas_call | solution.py:616
  75.8 0.0 copy-start.2
  75.8 0.0 copy-start
  75.8 2.1 %copy.32 = bf16[2,6,36,384]{3,0,2,1:T(2,128)(2,1)} copy(bf16[2,6,36,384]{3,2,1,0:T(8,128)(2,1)} %get-tuple-element.20) | data formatting | bytes 663552
  77.9 1.1 %copy.30 = f32[138,288]{0,1:T(8,128)S(1)} copy(f32[138,288]{1,0:T(8,128)} %bitcast.9) | data formatting | bytes 317952 | tf_op jit(solution)/shard_map/slice | solution.py:636
  79.0 0.1 reshape.20
  79.1 0.1 copy.31
  79.2 1.1 %reshape.22 = f32[1,12,3312]{2,0,1:T(1,128)} reshape(f32[3,4,2,2,6,138]{5,4,3,2,1,0:T(8,128)S(1)} %copy.31) | data formatting | bytes 317952 | tf_op jit(solution)/shard_map/reshape | solution.py:637
  80.2 0.0 copy-done.2
  80.2 1.0 %copy.33 = bf16[2,6,36,384]{3,0,2,1:T(2,128)(2,1)} copy(bf16[2,6,36,384]{3,2,1,0:T(8,128)(2,1)S(1)} %copy-done.2) | data formatting | bytes 663552
  81.2 0.0 copy-done
  81.2 0.0 copy-start.1
  81.2 1.2 %copy.37 = f32[384,1152]{1,0:T(8,128)} copy(f32[384,1152]{1,0:T(8,128)S(1)} %copy-done) | data formatting | bytes 3538944
  82.4 0.3 copy-done.1
  82.7 0.8 copy.38
Async XLA Ops:
  0.6 3.4 %copy-start.4 = (bf16[2,6,36,384]{3,0,2,1:T(2,128)(2,1)S(1)}, bf16[2,6,36,384]{3,0,2,1:T(2,128)(2,1)}, u32[]{:S(2)}) copy-start(bf16[2,6,36,384]{3,0,2,1:T(2,128)(2,1)} %param.19) | copy-start | bytes 995332
  0.6 2.6 %copy-start.3 = (bf16[2,6,36,384]{3,0,2,1:T(2,128)(2,1)S(1)}, bf16[2,6,36,384]{3,0,2,1:T(2,128)(2,1)}, u32[]{:S(2)}) copy-start(bf16[2,6,36,384]{3,0,2,1:T(2,128)(2,1)} %param.15) | copy-start | bytes 995332
  75.8 4.5 %copy-start.2 = (bf16[2,6,36,384]{3,2,1,0:T(8,128)(2,1)S(1)}, bf16[2,6,36,384]{3,2,1,0:T(8,128)(2,1)}, u32[]{:S(2)}) copy-start(bf16[2,6,36,384]{3,2,1,0:T(8,128)(2,1)} %get-tuple-element.21) | copy-start | bytes 995332
  75.8 5.4 %copy-start = (f32[384,1152]{1,0:T(8,128)S(1)}, f32[384,1152]{1,0:T(8,128)}, u32[]{:S(2)}) copy-start(f32[384,1152]{1,0:T(8,128)} %get-tuple-element.32) | copy-start | bytes 5308420
  81.2 1.5 %copy-start.1 = (f32[384,384]{1,0:T(8,128)S(1)}, f32[384,384]{1,0:T(8,128)}, u32[]{:S(2)}) copy-start(f32[384,384]{1,0:T(8,128)} %get-tuple-element.33) | copy-start | bytes 1769476

commit v4 on v3

--- a/solution.py
+++ b/solution.py
@@ -23,9 +23,8 @@
 PITCH = 48
 RIMS = ((0, 208), (208, 48), (256, 48))
 RIM = 304
-TILES = 96
 BIAS_TILES = 32
-CHUNKS = ((0, 1), (2,))
+CHUNKS = (64, 128, 96)
 X_HI = 2
 F32 = jnp.float32
 BF16 = jnp.bfloat16
@@ -94,6 +93,7 @@
     (cells_v, cot_v, wqkv_ref, wout_ref, r_ref,
      spread_ref, gather_ref, pick_ref, cross_ref, own_ref, rim_ref, send_ref, ownt_ref, rimt_ref, sendt_ref,
      load_sem, slab, rim_snd, rim_in, bt, db, x_w, dy_w, normed, normed_t, mix, dproj, wt, ow, rim_osnd, rim_out,
+     kv, k_ts, q_ws, soft_s, m_ts, dm_ws, dq_ts,
      halo_sem, *comm) = refs[N_IN + 5:]
     chunk_refs = [comm[i * 10:i * 10 + 10] for i in range(len(CHUNKS))]
     (bb, bcrecv, bs, bxrecv, by, byrecv, bfin, b_sem) = comm[len(CHUNKS) * 10:]
@@ -140,11 +140,13 @@
             src_ref=src, dst_ref=dst, send_sem=send_sem, recv_sem=recv_sem, device_id=device, device_id_type=MESH
         )
 
-    dsts = (cells_v, cot_v, send_ref, r_ref, spread_ref, cross_ref, wqkv_ref, wout_ref, own_ref, rim_ref, pick_ref,
-            gather_ref, ownt_ref, rimt_ref, sendt_ref)
-    srcs = (cells_h, cot_h, consts_h[6], r_h, consts_h[0], consts_h[3], wqkv_h, wout_h, consts_h[4], consts_h[5],
-            consts_h[2], consts_h[1], consts_h[7], consts_h[8], consts_h[9])
-    loads = [pltpu.make_async_copy(s, d, load_sem.at[i]) for i, (s, d) in enumerate(zip(srcs, dsts))]
+    order = (
+        (cells_h, cells_v), (consts_h[6], send_ref), (cot_h, cot_v), (r_h, r_ref), (consts_h[0], spread_ref),
+        (consts_h[3], cross_ref), (wqkv_h, wqkv_ref), (consts_h[4], own_ref), (consts_h[5], rim_ref),
+        (consts_h[2], pick_ref), (wout_h, wout_ref), (consts_h[8], rimt_ref), (consts_h[7], ownt_ref),
+        (consts_h[9], sendt_ref), (consts_h[1], gather_ref),
+    )
+    loads = [pltpu.make_async_copy(s, d, load_sem.at[i]) for i, (s, d) in enumerate(order)]
     for load in loads:
         load.start()
 
@@ -157,17 +159,6 @@
     partners += tuple(d for _, d, _ in ones + twos + ys) + tuple(d for d, _ in zs)
     for device in partners:
         greet(device)
-
-    slab[...] = jnp.zeros_like(slab)
-    for f in range(2):
-        loads[f].wait()
-        src = (cells_v, cot_v)[f]
-        for s in range(SLABS):
-            slab[f, s * PITCH:s * PITCH + COLS, :] = src[s // WH, s % WH]
-    loads[2].wait()
-    for f in range(2):
-        rim_snd[f] = nn(send_ref[...], slab[f]).astype(BF16)
-    pl.semaphore_wait(barrier, len(partners))
 
     def rim_copies(snd, rcv, devices, base):
         return [
@@ -181,8 +172,18 @@
 
     rims_in = rim_copies(rim_snd, rim_in, back, 0)
     rims_out = rim_copies(rim_osnd, rim_out, ahead, 6)
-    for copy in rims_in:
-        copy.start()
+    slab[...] = jnp.zeros_like(slab)
+    for f, src in enumerate((cells_v, cot_v)):
+        loads[2 * f].wait()
+        for s in range(SLABS):
+            slab[f, s * PITCH:s * PITCH + COLS, :] = src[s // WH, s % WH]
+        if f == 0:
+            loads[1].wait()
+        rim_snd[f] = nn(send_ref[...], slab[f]).astype(BF16)
+        if f == 0:
+            pl.semaphore_wait(barrier, len(partners))
+        for copy in rims_in[3 * f:3 * f + 3]:
+            copy.start()
 
     for load in loads[3:6]:
         load.wait()
@@ -213,10 +214,12 @@
         wt[part * c:(part + 1) * c, :] = nt(eye, wqkv_ref[:, part * c:(part + 1) * c]).astype(BF16)
     pick = pick_ref[...]
 
-    for copy in rims_in:
-        copy.wait()
-    x_w[...] = (nn(own_ref[...], slab[0]) + nn(rim_ref[...], rim_in[0])).astype(BF16)
-    dy_w[...] = (nn(own_ref[...], slab[1]) + nn(rim_ref[...], rim_in[1])).astype(BF16)
+    def arrive(f, ref):
+        for copy in rims_in[3 * f:3 * f + 3]:
+            copy.wait()
+        ref[...] = (nn(own_ref[...], slab[f]) + nn(rim_ref[...], rim_in[f])).astype(BF16)
+
+    arrive(0, x_w)
     cells = x_w[...].astype(F32)
     average = jnp.mean(cells, axis=-1, keepdims=True)
     centred = cells - average
@@ -225,59 +228,78 @@
     normed[...] = (centred * rstd).astype(BF16)
     normed_t[...] = nt(eye, normed[...]).astype(BF16)
 
-    def unit(g, w):
-        at = slice(w * TOK, (w + 1) * TOK)
-        gs = slice(g * gw, (g + 1) * gw)
-        cols = [slice(part * c + g * gw, part * c + (g + 1) * gw) for part in range(3)]
-        here = normed[at, :]
-        q_t, k_t, v_t = [nt(wt[cols[part], :], here).astype(BF16) for part in range(3)]
-        k, v = [nn(here, wqkv_ref[:, cols[part]]).astype(BF16) for part in (1, 2)]
-        dm_t = nt(wout_ref[gs, :], dy_w[at, :]).astype(BF16)
-        q_wide = (nn(q_t, pick) * mine).astype(BF16)
-        dm_wide = (nn(dm_t, pick) * mine).astype(BF16)
-        s = nn(k, q_wide) * scale + bt[g]
-        top = jnp.max(s, axis=0, keepdims=True)
-        e = jnp.exp(s - top)
-        soft = e * (1.0 / jnp.sum(e, axis=0, keepdims=True))
-        a = soft.astype(BF16)
-        da = nn(v, dm_wide)
+    kv[...] = nn(normed[...], wqkv_ref[:, c:]).astype(BF16)
+
+    def at_of(w):
+        return slice(w * TOK, (w + 1) * TOK)
+
+    def g_of(g, part=0):
+        return slice(part * c + g * gw, part * c + (g + 1) * gw)
+
+    def forward(w):
+        at = at_of(w)
+        turned = nt(wt[...], normed[at, :]).astype(BF16)
+        q_all = nn(turned[:c], pick)
+        k_ts[w] = turned[c:2 * c]
+        for g in range(groups):
+            q_wide = (q_all[g_of(g)] * mine).astype(BF16)
+            q_ws[w, g] = q_wide
+            s = nn(kv[at, g_of(g)], q_wide) * scale + bt[g]
+            top = jnp.max(s, axis=0, keepdims=True)
+            e = jnp.exp(s - top)
+            soft = e * (1.0 / jnp.sum(e, axis=0, keepdims=True))
+            soft_s[w, g] = soft
+            m_ts[g_of(g), :] = (nn(turned[g_of(g, 2)], soft.astype(BF16)) * mine).astype(BF16)
+        mix[at, :] = nt(pick, m_ts[...]).astype(BF16)
+
+    def widen(w):
+        dm_t = nt(wout_ref[...], dy_w[at_of(w), :]).astype(BF16)
+        dm_all = nn(dm_t, pick)
+        for g in range(groups):
+            dm_ws[w, g] = (dm_all[g_of(g)] * mine).astype(BF16)
+
+    def backward(g, w):
+        at = at_of(w)
+        soft = soft_s[w, g]
+        dm_wide = dm_ws[w, g]
+        da = nn(kv[at, g_of(g, 1)], dm_wide)
         ds = soft * (da - jnp.sum(soft * da, axis=0, keepdims=True))
         if w == 0:
             db[g] = ds
         else:
             db[g] += ds
         ds = ds.astype(BF16)
-        m_t = (nn(v_t, a) * mine).astype(BF16)
-        mix[at, gs] = nt(pick, m_t).astype(BF16)
-        dq_t = (nn(k_t, ds) * (mine * scale)).astype(BF16)
-        dproj[at, cols[0]] = nt(pick, dq_t).astype(BF16)
-        dproj[at, cols[1]] = (nt(ds, q_wide) * scale).astype(BF16)
-        dproj[at, cols[2]] = nt(a, dm_wide).astype(BF16)
-
-    def chunk_of(g):
-        return next((i, groups_in.index(g)) for i, groups_in in enumerate(CHUNKS) if g in groups_in)
-
-    def tile_at(g, t):
-        i, k = chunk_of(g)
-        t += k * TILES
-        half_tiles = len(CHUNKS[i]) * TILES // 2
+        dq_ts[w * gw:(w + 1) * gw, :] = (nn(k_ts[w, g_of(g), :], ds) * (mine * scale)).astype(BF16)
+        dproj[at, g_of(g, 1)] = (nt(ds, q_ws[w, g]) * scale).astype(BF16)
+        dproj[at, g_of(g, 2)] = nt(soft.astype(BF16), dm_wide).astype(BF16)
+
+    def tile_at(t):
+        i = 0
+        while t >= CHUNKS[i]:
+            t -= CHUNKS[i]
+            i += 1
+        half_tiles = CHUNKS[i] // 2
         share = half_tiles // (n * n)
         return i, (t // half_tiles, t % half_tiles // (n * share), t % (n * share) // share, t % share)
 
-    def put(g, t, value):
-        i, at = tile_at(g, t)
+    def put(t, value):
+        i, at = tile_at(t)
         chunk_refs[i][0][at] = value.astype(BF16)
 
-    def weight_grads(g):
+    def out_grads():
+        grad = nn(nt(eye, mix[...]).astype(BF16), dy_w[...]) * grad_scale
+        for k in range(3):
+            for r in range(24):
+                put(k * 24 + r, grad[r * 16:(r + 1) * 16, k * 128:(k + 1) * 128])
+
+    def qkv_grads(g):
+        dq = nt(pick, dq_ts[...]).astype(BF16)
+        for w in range(WINDOWS):
+            dproj[at_of(w), g_of(g)] = dq[:, w * gw:(w + 1) * gw]
         for part in range(3):
-            grad = nn(normed_t[...], dproj[:, part * c + g * gw:part * c + (g + 1) * gw]) * grad_scale
+            grad = nn(normed_t[...], dproj[:, g_of(g, part)]) * grad_scale
             for r in range(24):
-                put(g, part * 24 + r, grad[r * 16:(r + 1) * 16])
-        mix_t = nt(eye[:gw, :gw], mix[:, g * gw:(g + 1) * gw]).astype(BF16)
-        grad = nn(mix_t, dy_w[...]) * grad_scale
-        for k in range(3):
-            for r in range(8):
-                put(g, 72 + k * 8 + r, grad[r * 16:(r + 1) * 16, k * 128:(k + 1) * 128])
+                put(72 + 72 * g + part * 24 + r, grad[r * 16:(r + 1) * 16])
 
     class Chain:
         def __init__(self, refs):
@@ -385,17 +407,17 @@
 
     chains = [Chain(r) for r in chunk_refs]
 
-    def unpack(g):
-        def get(t):
-            i, at = tile_at(g, t)
-            return chains[i].fin[at].astype(F32)
-
-        for part in range(3):
-            for r in range(24):
-                gqkv_ref[r * 16:(r + 1) * 16, part * c + g * gw:part * c + (g + 1) * gw] = get(part * 24 + r)
-        for k in range(3):
-            for r in range(8):
-                gout_ref[g * gw + r * 16:g * gw + (r + 1) * 16, k * 128:(k + 1) * 128] = get(72 + k * 8 + r)
+    def unpack(first, end):
+        for t in range(first, end):
+            i, at = tile_at(t)
+            value = chains[i].fin[at].astype(F32)
+            r, k = t % 24, t // 24
+            rows = slice(r * 16, (r + 1) * 16)
+            if k < 3:
+                gout_ref[rows, k * 128:(k + 1) * 128] = value
+            else:
+                g, part = (k - 3) // 3, (k - 3) % 3
+                gqkv_ref[rows, g_of(g, part)] = value
 
     bshare = BIAS_TILES // (4 * n)
 
@@ -497,54 +519,71 @@
         for s in range(SLABS):
             ref[s // WH, s % WH] = full[s * PITCH:s * PITCH + COLS]
 
-    early, late = chains
-    for g in (0, 1):
-        for w in range(WINDOWS):
-            unit(g, w)
-        weight_grads(g)
-    early.start()
-    unit(2, 0)
-    early.first()
-    unit(2, 1)
-    unit(2, 2)
-    weight_grads(2)
-    late.start()
-    bias_core()
-    early.second()
+    c0, c1, c2 = chains
+    for w in range(WINDOWS):
+        forward(w)
     ow[0] = (cells + nn(mix[...], wout_ref[...])).astype(BF16)
     rim_osnd[0] = nn(rimt_ref[...], ow[0]).astype(BF16)
-    late.first()
     for copy in rims_out[:3]:
         copy.start()
+    arrive(1, dy_w)
+    out_grads()
+    c0.start()
+    for w in range(WINDOWS):
+        widen(w)
+    backward(0, 0)
+    c0.first()
+    backward(0, 1)
+    backward(0, 2)
+    qkv_grads(0)
+    c0.second()
+    for w in range(WINDOWS):
+        backward(1, w)
+    qkv_grads(1)
+    c1.start()
+    c0.third()
+    backward(2, 0)
+    backward(2, 1)
+    c1.first()
+    backward(2, 2)
+    qkv_grads(2)
+    c2.start()
     dn = nt(dproj[...], wqkv_ref[...])
     n_w = centred * rstd
     dx = (dn - jnp.mean(dn, axis=-1, keepdims=True) - n_w * jnp.mean(dn * n_w, axis=-1, keepdims=True)) * rstd
     ow[1] = (dx + dy_w[...].astype(F32)).astype(BF16)
+    c2.first()
     rim_osnd[1] = nn(rimt_ref[...], ow[1]).astype(BF16)
-    late.second()
     for copy in rims_out[3:]:
         copy.start()
+    c0.fourth()
+    bias_core()
+    c1.second()
+    c2.second()
     bias_x()
-    early.third()
+    c1.third()
+    c2.third()
+    c0.fifth()
     bias_y()
-    late.third()
+    finish(0, out_ref)
+    c1.fourth()
+    c2.fourth()
     bias_back_y()
-    early.fourth()
-    late.fourth()
+    c0.sixth()
+    c1.fifth()
+    c2.fifth()
     bias_back_x()
-    early.fifth()
-    late.fifth()
+    finish(1, dx_ref)
+    c1.sixth()
+    c2.sixth()
     bias_back_core()
-    early.sixth()
-    finish(0, out_ref)
-    late.sixth()
-    finish(1, dx_ref)
+    c0.last()
+    unpack(0, CHUNKS[0])
+    c1.last()
+    unpack(CHUNKS[0], CHUNKS[0] + CHUNKS[1])
     bias_end()
-    early.last()
-    unpack(0)
-    unpack(1)
-    late.last()
-    unpack(2)
+    c2.last()
+    unpack(CHUNKS[0] + CHUNKS[1], sum(CHUNKS))
 
 
 def fused(cells, cot, qkv_weight, out_weight, table, lon_size, lat_size, cells_total):
@@ -557,6 +596,7 @@
     ins = (cells, cot, qkv_weight, out_weight, table) + consts
     n, nz = lon_size // 4, lat_size // X_HI
     bshare = BIAS_TILES // (4 * n)
+    gw = GROUP * HEAD
     vm = pltpu.VMEM
     dma = pltpu.SemaphoreType.DMA
     scratch = [vm(a.shape, a.dtype) for a in ins] + [
@@ -576,11 +616,18 @@
         vm((2, ROWS, c), BF16),
         vm((2, RIM, c), BF16),
         vm((2, RIM, c), BF16),
+        vm((ROWS, 2 * c), BF16),
+        vm((WINDOWS, c, TOK), BF16),
+        vm((WINDOWS, groups, gw, LANES), BF16),
+        vm((WINDOWS, groups, TOK, LANES), F32),
+        vm((c, LANES), BF16),
+        vm((WINDOWS, groups, gw, LANES), BF16),
+        vm((WINDOWS * gw, LANES), BF16),
         dma((2, 12)),
     ]
     tile = (16, 128)
-    for groups_in in CHUNKS:
-        share = len(groups_in) * TILES // (2 * n * n)
+    for tiles in CHUNKS:
+        share = tiles // (2 * n * n)
         scratch += [
             vm((2, n, n, share) + tile, BF16),
             vm((n, n, share) + tile, BF16),

time: 83.7 us -> 83.6 us (level)
  no operation moved by 1% of the time
where the time goes in v4:
time: 83.6 us; the launch traced here: 83.4 us
  Pallas kernels  70.8 us (85%)
  local copies, waits for them, and re-layouts  10.5 us (13%)
  other arithmetic  1.36 us (2%)
    pallas_call x1, Pallas kernels, fused(): pl.pallas_call(kernel, out_shape=out_shape, in_specs=[pl.BlockSpec(memory...  70.8 us
    unnamed x16, local copies, waits for them, and re-layouts  6.97 us

profile of v4, /device:TPU:1, one launch (start us, length us, event | category | flops | bytes accessed | tf_op | source)
XLA Modules:
  0.0 83.4 jit_solution(16684529002793947020)
XLA Ops:
  0.6 0.0 copy-start.4
  0.6 0.0 copy-start.3
  0.7 1.4 %reduce = f32[12,3312]{1,0:T(8,128)S(1)} reduce(f32[1,12,3312]{2,0,1:T(1,128)} %param.18, f32[]{:T(128)} %constant.33), dimensions={0}, to_apply=%param.18.reduce_sub_computation | reduce | bytes 317956 | tf_op args[3]
  2.0 0.4 reshape_squeeze.3
  2.4 0.2 copy.26
  2.5 0.7 copy.29.refs_4_
  3.3 0.0 copy-done.3
  3.3 0.8 copy.27.refs_0_
  4.1 0.0 copy-done.4
  4.1 0.8 copy.28.refs_1_
  4.9 70.8 %shard_map.182 = (bf16[2,6,36,384]{3,2,1,0:T(8,128)(2,1)}, bf16[2,6,36,384]{3,2,1,0:T(8,128)(2,1)}, f32[384,1152]{1,0:T(8,128)}, f32[384,384]{1,0:T(8,128)}, f32[144,384]{1,0:T(8,128)}) custom-call(bf16[2,6,36,384]{3,2,1,0:T(8,128)(2,1)} %copy.27.refs_0_, bf16[2,6,36,384]{3,2,1,0:T(8,128)(2,1)} %copy.28.refs_1_, bf16[384,1152]{1,0:T(8,128)(2,1)} %refs_2_.1, ...), custom_call_target="tpu_custom_call" | custom-call | flops 6000000000 | bytes 10000000 | tf_op jit(solution)/shard_map/pallas_call | solution.py:663
  75.7 0.0 copy-start.2
  75.7 0.0 copy-start
  75.7 2.1 %copy.32 = bf16[2,6,36,384]{3,0,2,1:T(2,128)(2,1)} copy(bf16[2,6,36,384]{3,2,1,0:T(8,128)(2,1)} %get-tuple-element.20) | data formatting | bytes 663552
  77.8 1.1 %copy.30 = f32[138,288]{0,1:T(8,128)S(1)} copy(f32[138,288]{1,0:T(8,128)} %bitcast.9) | data formatting | bytes 317952 | tf_op jit(solution)/shard_map/slice | solution.py:683
  78.9 0.1 reshape.20
  79.0 0.1 copy.31
  79.1 1.1 %reshape.22 = f32[1,12,3312]{2,0,1:T(1,128)} reshape(f32[3,4,2,2,6,138]{5,4,3,2,1,0:T(8,128)S(1)} %copy.31) | data formatting | bytes 317952 | tf_op jit(solution)/shard_map/reshape | solution.py:684
  80.1 0.0 copy-done.2
  80.1 1.0 %copy.33 = bf16[2,6,36,384]{3,0,2,1:T(2,128)(2,1)} copy(bf16[2,6,36,384]{3,2,1,0:T(8,128)(2,1)S(1)} %copy-done.2) | data formatting | bytes 663552
  81.1 0.0 copy-done
  81.1 0.0 copy-start.1
  81.1 1.2 %copy.37 = f32[384,1152]{1,0:T(8,128)} copy(f32[384,1152]{1,0:T(8,128)S(1)} %copy-done) | data formatting | bytes 3538944
  82.3 0.3 copy-done.1
  82.6 0.8 copy.38
Async XLA Ops:
  0.6 3.4 %copy-start.4 = (bf16[2,6,36,384]{3,0,2,1:T(2,128)(2,1)S(1)}, bf16[2,6,36,384]{3,0,2,1:T(2,128)(2,1)}, u32[]{:S(2)}) copy-start(bf16[2,6,36,384]{3,0,2,1:T(2,128)(2,1)} %param.19) | copy-start | bytes 995332
  0.6 2.6 %copy-start.3 = (bf16[2,6,36,384]{3,0,2,1:T(2,128)(2,1)S(1)}, bf16[2,6,36,384]{3,0,2,1:T(2,128)(2,1)}, u32[]{:S(2)}) copy-start(bf16[2,6,36,384]{3,0,2,1:T(2,128)(2,1)} %param.15) | copy-start | bytes 995332
  75.7 4.5 %copy-start.2 = (bf16[2,6,36,384]{3,2,1,0:T(8,128)(2,1)S(1)}, bf16[2,6,36,384]{3,2,1,0:T(8,128)(2,1)}, u32[]{:S(2)}) copy-start(bf16[2,6,36,384]{3,2,1,0:T(8,128)(2,1)} %get-tuple-element.21) | copy-start | bytes 995332
  75.7 5.4 %copy-start = (f32[384,1152]{1,0:T(8,128)S(1)}, f32[384,1152]{1,0:T(8,128)}, u32[]{:S(2)}) copy-start(f32[384,1152]{1,0:T(8,128)} %get-tuple-element.32) | copy-start | bytes 5308420
  81.1 1.5 %copy-start.1 = (f32[384,384]{1,0:T(8,128)S(1)}, f32[384,384]{1,0:T(8,128)}, u32[]{:S(2)}) copy-start(f32[384,384]{1,0:T(8,128)} %get-tuple-element.33) | copy-start | bytes 1769476

commit v5 on v4

--- a/solution.py
+++ b/solution.py
@@ -20,7 +20,7 @@
 WINDOWS = 3
 ROWS = WINDOWS * TOK
 COLS = WINDOWS * WW
-PITCH = 48
+PITCH = 80
 RIMS = ((0, 208), (208, 48), (256, 48))
 RIM = 304
 BIAS_TILES = 32
@@ -52,9 +52,9 @@
     row_half = np.arange(TOK) // WW % WH >= WH - WH // 2
     lane_half = lane_slab % WH >= WH - WH // 2
     cross = np.where(row_half[:, None] != lane_half[None, :], -1e9, 0.0).astype(np.float32)
-    own = np.zeros((ROWS, SLABS * PITCH), np.float32)
+    own = np.zeros((ROWS, WH * PITCH), np.float32)
     rim = np.zeros((ROWS, RIM), np.float32)
-    send = np.zeros((RIM, SLABS * PITCH), np.float32)
+    send = np.zeros((RIM, WH * PITCH), np.float32)
     h = WH // 2
     for w in range(WINDOWS):
         for z in range(LEV):
@@ -64,7 +64,7 @@
                     col = WW // 2 + w * WW + j
                     below, beside = i >= h, col >= COLS
                     row, k = ((i - h) if below else (i + h)), i % h
-                    slab = (z * WH + row) * PITCH + col % COLS
+                    slab = row * PITCH + col % COLS * LEV + z
                     if not below and not beside:
                         own[t, slab] = 1
                         continue
@@ -93,10 +93,10 @@
     (cells_v, cot_v, wqkv_ref, wout_ref, r_ref,
      spread_ref, gather_ref, pick_ref, cross_ref, own_ref, rim_ref, send_ref, ownt_ref, rimt_ref, sendt_ref,
      load_sem, slab, rim_snd, rim_in, bt, db, x_w, dy_w, normed, normed_t, mix, dproj, wt, ow, rim_osnd, rim_out,
-     kv, k_ts, q_ws, soft_s, m_ts, dm_ws, dq_ts,
+     kv, k_ts, q_ws, soft_s, m_ts, dm_ws, dq_ts, tab, rows_of, turned,
      halo_sem, *comm) = refs[N_IN + 5:]
-    chunk_refs = [comm[i * 10:i * 10 + 10] for i in range(len(CHUNKS))]
-    (bb, bcrecv, bs, bxrecv, by, byrecv, bfin, b_sem) = comm[len(CHUNKS) * 10:]
+    chunk_refs = [comm[i * 9:i * 9 + 9] for i in range(len(CHUNKS))]
+    (bb, bcrecv, bs, bxrecv, by, byrecv, bfin, b_sem) = comm[len(CHUNKS) * 9:]
     c = wout_ref.shape[0]
     n, nz = lon_size // 4, lat_size // X_HI
     half = WH * WW
@@ -172,11 +172,12 @@
 
     rims_in = rim_copies(rim_snd, rim_in, back, 0)
     rims_out = rim_copies(rim_osnd, rim_out, ahead, 6)
-    slab[...] = jnp.zeros_like(slab)
     for f, src in enumerate((cells_v, cot_v)):
         loads[2 * f].wait()
-        for s in range(SLABS):
-            slab[f, s * PITCH:s * PITCH + COLS, :] = src[s // WH, s % WH]
+        for s in range(WH):
+            slab[f, s * PITCH:(s + 1) * PITCH, :] = jnp.concatenate(
+                [src[s].reshape(COLS * LEV, c), jnp.zeros((PITCH - COLS * LEV, c), BF16)], axis=0
+            )
         if f == 0:
             loads[1].wait()
         rim_snd[f] = nn(send_ref[...], slab[f]).astype(BF16)
@@ -188,8 +189,20 @@
     for load in loads[3:6]:
         load.wait()
     last = (lat == lat_size - 1).astype(F32)
+    tab[...] = r_ref[:, 0, :]
+    width = WH * SPAN
+
+    def segment(z1, z2, i1):
+        return pl.ds(((z1 * LEV + z2) * WH + i1) * width, width)
+
     for z2 in range(LEV):
-        table = r_ref[z2]
+        for z1 in range(LEV):
+            for i1 in range(WH):
+                piece = tab[:, segment(z1, z2, i1)]
+                for g in range(groups):
+                    at = g * blk + (z1 * WH + i1) * GROUP
+                    rows_of[at:at + GROUP, :] = piece[g * GROUP:(g + 1) * GROUP]
+        table = rows_of[...]
         hi = table.astype(BF16)
         rest = table - hi.astype(F32)
         mid = rest.astype(BF16)
@@ -238,9 +251,9 @@
 
     def forward(w):
         at = at_of(w)
-        turned = nt(wt[...], normed[at, :]).astype(BF16)
-        q_all = nn(turned[:c], pick)
-        k_ts[w] = turned[c:2 * c]
+        qkv_t = nt(wt[...], normed[at, :]).astype(BF16)
+        q_all = nn(qkv_t[:c], pick)
+        k_ts[w] = qkv_t[c:2 * c]
         for g in range(groups):
             q_wide = (q_all[g_of(g)] * mine).astype(BF16)
             q_ws[w, g] = q_wide
@@ -249,7 +262,7 @@
             e = jnp.exp(s - top)
             soft = e * (1.0 / jnp.sum(e, axis=0, keepdims=True))
             soft_s[w, g] = soft
-            m_ts[g_of(g), :] = (nn(turned[g_of(g, 2)], soft.astype(BF16)) * mine).astype(BF16)
+            m_ts[g_of(g), :] = (nn(qkv_t[g_of(g, 2)], soft.astype(BF16)) * mine).astype(BF16)
         mix[at, :] = nt(pick, m_ts[...]).astype(BF16)
 
     def widen(w):
@@ -303,114 +316,81 @@
 
     class Chain:
         def __init__(self, refs):
-            (self.gb, self.crecv, self.xs, self.arecv, self.ys, self.brecv, self.zbuf, self.fin,
-             self.sem, self.zsem) = refs
-
-        def copy(self, k, src, dst, device):
-            return remote(src, dst, self.sem.at[0, k], self.sem.at[1, k], device)
-
-        def core_copy(self):
-            return self.copy(0, self.gb.at[other], self.crecv, sibling)
-
-        def one_copies(self):
-            return [self.copy(1 + o, self.xs.at[q], self.arecv.at[o], d) for o, (q, d, _) in enumerate(ones)]
-
-        def two_copies(self):
-            return [self.copy(4 + o, self.ys.at[q], self.brecv.at[o], d) for o, (q, d, _) in enumerate(twos)]
-
-        def z_copies(self, here=True):
-            at = [z if here else q for _, q in zs]
-            return [
-                remote(self.zbuf.at[at[o]], self.zbuf.at[at[o]], self.zsem.at[0, o], self.zsem.at[1, o], d)
-                for o, (d, _) in enumerate(zs)
-            ]
-
-        def back_two(self, here=True):
-            at = [two if here else q for _, _, q in twos]
-            return [
-                self.copy(7 + o, self.fin.at[core, one, at[o]], self.fin.at[core, one, at[o]], d)
-                for o, (_, d, _) in enumerate(twos)
-            ]
-
-        def back_one(self, here=True):
-            at = [one if here else q for _, _, q in ones]
-            return [
-                self.copy(10 + o, self.fin.at[core, at[o]], self.fin.at[core, at[o]], d)
-                for o, (_, d, _) in enumerate(ones)
-            ]
-
-        def back_core(self, o, half_at):
-            at = one if o == 0 else ones[o - 1][2]
-            return self.copy(13 + o, self.fin.at[half_at, at], self.fin.at[half_at, at], sibling)
+            (self.gb, self.crecv, self.xs, self.arecv, self.ys, self.brecv, self.zbuf, self.fin, self.sem) = refs
+
+        def send(self, stage, src, dst, device):
+            remote(src, dst, self.sem.at[0, stage], self.sem.at[1, stage], device).start()
+
+        def wait(self, side, stage, like):
+            pltpu.make_async_copy(like, like, self.sem.at[side, stage]).wait()
 
         def start(self):
-            self.core_copy().start()
+            self.send(0, self.gb.at[other], self.crecv, sibling)
 
         def first(self):
-            self.core_copy().wait()
+            self.wait(1, 0, self.crecv)
             self.xs[...] = (self.gb[core].astype(F32) + self.crecv[...].astype(F32)).astype(BF16)
-            for copy in self.one_copies():
-                copy.start()
+            for o, (q, d, _) in enumerate(ones):
+                self.send(1, self.xs.at[q], self.arecv.at[o], d)
 
         def second(self):
-            for copy in self.one_copies():
-                copy.wait()
+            self.wait(1, 1, self.arecv)
             total = self.xs[one].astype(F32)
             for o in range(n - 1):
                 total += self.arecv[o].astype(F32)
             self.ys[...] = total.astype(BF16)
-            for copy in self.two_copies():
-                copy.start()
+            for o, (q, d, _) in enumerate(twos):
+                self.send(2, self.ys.at[q], self.brecv.at[o], d)
 
         def third(self):
-            for copy in self.two_copies():
-                copy.wait()
+            self.wait(1, 2, self.brecv)
             total = self.ys[two].astype(F32)
             for o in range(n - 1):
                 total += self.brecv[o].astype(F32)
-            self.zbuf[z] = total.astype(BF16)
-            for copy in self.z_copies():
-                copy.start()
+            self.zbuf[0] = total.astype(BF16)
+            for o, (d, _) in enumerate(zs):
+                self.send(3, self.zbuf.at[0], self.zbuf.at[o + 1], d)
 
         def fourth(self):
-            for copy in self.z_copies():
-                copy.wait_send()
-            for copy in self.z_copies(False):
-                copy.wait_recv()
-            total = self.zbuf[0].astype(F32)
+            if nz > 1:
+                self.wait(1, 3, self.zbuf.at[pl.ds(1, nz - 1)])
+            total = self.zbuf[z].astype(F32)
             for k in range(1, nz):
-                total += self.zbuf[k].astype(F32)
-            self.fin[core, one, two] = total.astype(BF16)
-            for copy in self.back_two():
-                copy.start()
+                total += self.zbuf[(z + nz - k) % nz].astype(F32)
+            mine_at = self.fin.at[core, one, two]
+            mine_at[...] = total.astype(BF16)
+            for _, d, _ in twos:
+                self.send(4, mine_at, mine_at, d)
 
         def fifth(self):
-            for copy in self.back_two():
-                copy.wait_send()
-            for copy in self.back_two(False):
-                copy.wait_recv()
-            for copy in self.back_one():
-                copy.start()
-            self.back_core(0, core).start()
+            self.wait(1, 4, self.fin.at[core, one, pl.ds(0, n - 1)])
+            mine_at = self.fin.at[core, one]
+            for _, d, _ in ones:
+                self.send(5, mine_at, mine_at, d)
 
         def sixth(self):
-            for o, copy in enumerate(self.back_one(False)):
-                copy.wait_recv()
-                self.back_core(o + 1, core).start()
+            self.wait(1, 5, self.fin.at[core, pl.ds(0, n - 1)])
+            self.send(6, self.fin.at[core], self.fin.at[core], sibling)
 
         def last(self):
-            for copy in self.back_one():
-                copy.wait_send()
-            for o in range(n):
-                self.back_core(o, core).wait_send()
-                self.back_core(o, other).wait_recv()
+            self.wait(1, 6, self.fin.at[other])
+
+        def drain(self):
+            self.wait(0, 0, self.crecv)
+            self.wait(0, 1, self.arecv)
+            self.wait(0, 2, self.brecv)
+            if nz > 1:
+                self.wait(0, 3, self.zbuf.at[pl.ds(1, nz - 1)])
+            self.wait(0, 4, self.brecv)
+            self.wait(0, 5, self.arecv)
+            self.wait(0, 6, self.crecv)
 
     chains = [Chain(r) for r in chunk_refs]
 
     def unpack(first, end):
         for t in range(first, end):
             i, at = tile_at(t)
-            value = chains[i].fin[at].astype(F32)
+            value = chains[i].fin[at]
             r, k = t % 24, t // 24
             rows = slice(r * 16, (r + 1) * 16)
             if k < 3:
@@ -508,16 +488,25 @@
     def bias_end():
         bcore_back(core).wait_send()
         bcore_back(other).wait_recv()
+        turned[144:, :] = jnp.zeros((256 - 144, 384), F32)
         for t in range(27):
             k, r = t // 9, t % 9
-            dr_ref[r * 16:(r + 1) * 16, k * 128:(k + 1) * 128] = bfin[bias_at(t)].astype(F32)
+            turned[r * 16:(r + 1) * 16, k * 128:(k + 1) * 128] = bfin[bias_at(t)].astype(F32)
+        flat = turned[...].T
+        for z2 in range(LEV):
+            for z1 in range(LEV):
+                for i1 in range(WH):
+                    for g in range(groups):
+                        at = z2 * groups * blk + g * blk + (z1 * WH + i1) * GROUP
+                        tab[g * GROUP:(g + 1) * GROUP, segment(z1, z2, i1)] = flat[at:at + GROUP, :width]
+        dr_ref[:, 0, :] = tab[...]
 
     def finish(f, ref):
         for copy in rims_out[3 * f:3 * f + 3]:
             copy.wait()
         full = (nn(ownt_ref[...], ow[f]) + nn(sendt_ref[...], rim_out[f])).astype(BF16)
-        for s in range(SLABS):
-            ref[s // WH, s % WH] = full[s * PITCH:s * PITCH + COLS]
+        for s in range(WH):
+            ref[s] = full[s * PITCH:s * PITCH + COLS * LEV].reshape(COLS, LEV, c)
 
     c0, c1, c2 = chains
     for w in range(WINDOWS):
@@ -554,45 +543,45 @@
     ow[1] = (dx + dy_w[...].astype(F32)).astype(BF16)
     c2.first()
     rim_osnd[1] = nn(rimt_ref[...], ow[1]).astype(BF16)
+    c0.fourth()
+    c1.second()
+    c2.second()
+    bias_core()
+    c1.third()
+    c2.third()
     for copy in rims_out[3:]:
         copy.start()
-    c0.fourth()
-    bias_core()
-    c1.second()
-    c2.second()
     bias_x()
-    c1.third()
-    c2.third()
     c0.fifth()
+    finish(0, out_ref)
     bias_y()
-    finish(0, out_ref)
     c1.fourth()
     c2.fourth()
+    c0.sixth()
     bias_back_y()
-    c0.sixth()
     c1.fifth()
     c2.fifth()
     bias_back_x()
-    finish(1, dx_ref)
+    c0.last()
+    unpack(0, CHUNKS[0])
     c1.sixth()
     c2.sixth()
     bias_back_core()
-    c0.last()
-    unpack(0, CHUNKS[0])
+    finish(1, dx_ref)
     c1.last()
     unpack(CHUNKS[0], CHUNKS[0] + CHUNKS[1])
     bias_end()
     c2.last()
     unpack(CHUNKS[0] + CHUNKS[1], sum(CHUNKS))
+    for chain in chains:
+        chain.drain()
 
 
 def fused(cells, cot, qkv_weight, out_weight, table, lon_size, lat_size, cells_total):
     c = out_weight.shape[0]
-    heads = table.shape[0]
+    heads, _, entries = table.shape
     groups = heads // GROUP
     consts = constants()
-    table = table.reshape(groups, GROUP, LEV, LEV, WH, WH * SPAN)
-    table = table.transpose(3, 0, 2, 4, 1, 5).reshape(LEV, heads * SLABS, WH * SPAN)
     ins = (cells, cot, qkv_weight, out_weight, table) + consts
     n, nz = lon_size // 4, lat_size // X_HI
     bshare = BIAS_TILES // (4 * n)
@@ -601,7 +590,7 @@
     dma = pltpu.SemaphoreType.DMA
     scratch = [vm(a.shape, a.dtype) for a in ins] + [
         dma((len(ins),)),
-        vm((2, SLABS * PITCH, c), BF16),
+        vm((2, WH * PITCH, c), BF16),
         vm((2, RIM, c), BF16),
         vm((2, RIM, c), BF16),
         vm((groups, TOK, LANES), F32),
@@ -623,6 +612,9 @@
         vm((c, LANES), BF16),
         vm((WINDOWS, groups, gw, LANES), BF16),
         vm((WINDOWS * gw, LANES), BF16),
+        vm((heads, entries), F32),
+        vm((heads * SLABS, WH * SPAN), F32),
+        vm((256, 384), F32),
         dma((2, 12)),
     ]
     tile = (16, 128)
@@ -637,8 +629,7 @@
             vm((n - 1, share) + tile, BF16),
             vm((nz, share) + tile, BF16),
             vm((2, n, n, share) + tile, BF16),
-            dma((2, 17)),
-            dma((2, nz)),
+            dma((2, 7)),
         ]
     scratch += [
         vm((2, 2, n, bshare) + tile, BF16),
@@ -656,9 +647,9 @@
     out_shape = (
         jax.ShapeDtypeStruct(cells.shape, BF16),
         jax.ShapeDtypeStruct(cells.shape, BF16),
-        jax.ShapeDtypeStruct((c, 3 * c), F32),
-        jax.ShapeDtypeStruct((c, c), F32),
-        jax.ShapeDtypeStruct((144, 384), F32),
+        jax.ShapeDtypeStruct((c, 3 * c), BF16),
+        jax.ShapeDtypeStruct((c, c), BF16),
+        jax.ShapeDtypeStruct(table.shape, F32),
     )
     return pl.pallas_call(
         kernel,
@@ -678,11 +669,11 @@
     heads = earth_bias.shape[1]
     cells_total = LEV * cells.shape[1] * cells.shape[2] * lon_size * lat_size
     out, dx, gqkv, gout, dr = fused(
-        cells, cotangent, qkv_weight, out_weight, earth_bias[0], lon_size, lat_size, cells_total
+        cells.transpose(1, 2, 0, 3), cotangent.transpose(1, 2, 0, 3), qkv_weight, out_weight, earth_bias.transpose(1, 0, 2),
+        lon_size, lat_size, cells_total
     )
-    dr = dr[: WH * SPAN, : 2 * heads * SLABS].reshape(WH * SPAN, LEV, heads // GROUP, LEV, WH, GROUP)
-    dr = dr.transpose(2, 5, 3, 1, 4, 0).reshape(earth_bias.shape)
-    return out, dx, gqkv, gout, dr
+    out, dx = out.transpose(2, 0, 1, 3), dx.transpose(2, 0, 1, 3)
+    return out, dx, gqkv.astype(F32), gout.astype(F32), dr.transpose(1, 0, 2)
 
 
 def solution(mesh):

time: 83.6 us -> 75.1 us (0.90)
  local copies, waits for them, and re-layouts: 10.5 us -> 2.13 us
  other arithmetic: 1.36 us -> 3.42 us
  Pallas kernels: 70.8 us -> 68.8 us
    unnamed x16 -> x11, local copies, waits for them, and re-layouts: 6.97 us -> 2.13 us
    convert_element_type x0 -> x2, other arithmetic: none -> 3.42 us  [on_device(): return (out, dx, gqkv.astype(F32), gout.astype(F32), dr.transpose(1, 0, 2))]
    pallas_call x1, Pallas kernels: 70.8 us -> 68.8 us  [fused(): pl.pallas_call(kernel, out_shape=out_shape, in_specs=[pl.BlockSpec(memory...]
    reshape x3 -> x0, local copies, waits for them, and re-layouts: 1.89 us -> none  [the longest x1 1.07 us: on_device(): dr = dr.transpose(2, 5, 3, 1, 4, 0).reshape(earth_bias.shape)]
    unnamed x1 -> x0, other arithmetic: 1.36 us -> none
    slice x1 -> x0, local copies, waits for them, and re-layouts: 1.07 us -> none  [on_device(): dr[:WH * SPAN, :2 * heads * SLABS]]
where the time goes in v5:
time: 75.1 us; the launch traced here: 75 us
  Pallas kernels  68.8 us (92%)
  other arithmetic  3.42 us (5%)
  local copies, waits for them, and re-layouts  2.13 us (3%)
    pallas_call x1, Pallas kernels, fused(): pl.pallas_call(kernel, out_shape=out_shape, in_specs=[pl.BlockSpec(memory...  68.8 us
    convert_element_type x2, other arithmetic, on_device(): return (out, dx, gqkv.astype(F32), gout.astype(F32), dr.transpose(1, 0, 2))  3.42 us
    unnamed x11, local copies, waits for them, and re-layouts  2.13 us

profile of v5, /device:TPU:1, one launch (start us, length us, event | category | flops | bytes accessed | tf_op | source)
XLA Modules:
  0.0 75.0 jit_solution(12475563820282088073)
XLA Ops:
  0.6 68.8 %shard_map.182 = (bf16[6,36,2,384]{3,2,1,0:T(2,128)(2,1)}, bf16[6,36,2,384]{3,2,1,0:T(2,128)(2,1)}, bf16[384,1152]{1,0:T(8,128)(2,1)}, bf16[384,384]{1,0:T(8,128)(2,1)}, f32[12,1,3312]{2,1,0:T(1,128)}) custom-call(bf16[6,36,2,384]{3,2,1,0:T(2,128)(2,1)} %bitcast.9, bf16[6,36,2,384]{3,2,1,0:T(2,128)(2,1)} %bitcast.10, bf16[384,1152]{1,0:T(8,128)(2,1)} %refs_2_.1, ...), custom_call_target="tpu_custom_call" | custom-call | flops 6000000000 | bytes 10000000 | tf_op jit(solution)/shard_map/pallas_call | solution.py:654
  69.4 0.0 copy-start.2
  69.4 0.0 copy-start.1
  69.4 0.0 copy-start
  69.4 2.6 %convert_element_type.6 = f32[384,1152]{1,0:T(8,128)} convert(bf16[384,1152]{1,0:T(8,128)(2,1)} %get-tuple-element.12) | non-fusion elementwise | flops 442368 | bytes 2654208 | tf_op jit(solution)/shard_map/convert_element_type | solution.py:676
  72.0 0.0 copy-start.3
  72.0 0.0 copy-done.2
  72.0 0.9 %convert_element_type.7 = f32[384,384]{1,0:T(8,128)} convert(bf16[384,384]{1,0:T(8,128)(2,1)S(1)} %copy-done.2) | non-fusion elementwise | flops 147456 | bytes 884736 | tf_op jit(solution)/shard_map/convert_element_type | solution.py:676
  72.9 0.0 copy-done.1
  72.9 0.7 copy.23
  73.6 0.0 copy-done
  73.6 0.7 copy.24
  74.3 0.0 copy-done.3
  74.3 0.7 copy.25
Async XLA Ops:
  69.4 2.6 %copy-start.2 = (bf16[384,384]{1,0:T(8,128)(2,1)S(1)}, bf16[384,384]{1,0:T(8,128)(2,1)}, u32[]{:S(2)}) copy-start(bf16[384,384]{1,0:T(8,128)(2,1)} %get-tuple-element.13) | copy-start | bytes 884740
  69.4 3.4 %copy-start.1 = (bf16[6,36,2,384]{3,2,1,0:T(2,128)(2,1)S(1)}, bf16[6,36,2,384]{3,2,1,0:T(2,128)(2,1)}, u32[]{:S(2)}) copy-start(bf16[6,36,2,384]{3,2,1,0:T(2,128)(2,1)} %get-tuple-element.10) | copy-start | bytes 995332
  69.4 4.2 %copy-start = (bf16[6,36,2,384]{3,2,1,0:T(2,128)(2,1)S(1)}, bf16[6,36,2,384]{3,2,1,0:T(2,128)(2,1)}, u32[]{:S(2)}) copy-start(bf16[6,36,2,384]{3,2,1,0:T(2,128)(2,1)} %get-tuple-element.11) | copy-start | bytes 995332
  72.0 2.3 %copy-start.3 = (f32[12,1,3312]{2,1,0:T(1,128)S(1)}, f32[12,1,3312]{2,1,0:T(1,128)}, u32[]{:S(2)}) copy-start(f32[12,1,3312]{2,1,0:T(1,128)} %get-tuple-element.14) | copy-start | bytes 476932

commit v6 on v5

--- a/solution.py
+++ b/solution.py
@@ -21,10 +21,12 @@
 ROWS = WINDOWS * TOK
 COLS = WINDOWS * WW
 PITCH = 80
-RIMS = ((0, 208), (208, 48), (256, 48))
+FINE_RIMS = ((0, 80, 0), (80, 80, 0), (160, 48, 0), (208, 48, 1), (256, 48, 2))
+RIMS = ((0, 208, 0), (208, 48, 1), (256, 48, 2))
+RIM_OF = ((0, 80), (80, 80), (160, 144))
 RIM = 304
 BIAS_TILES = 32
-CHUNKS = (64, 128, 96)
+CHUNKS = (128, 160)
 X_HI = 2
 F32 = jnp.float32
 BF16 = jnp.bfloat16
@@ -76,14 +78,23 @@
                         at = 80 * w + z * 36 + k * 12 + j
                     rim[t, at] = 1
                     send[at, slab] = 1
+    low = WH // 2 * PITCH
+    rim_w = np.zeros((ROWS, 144), np.float32)
+    rim_wt = np.zeros((RIM, TOK), np.float32)
+    for w, (at, size) in enumerate(RIM_OF):
+        block = rim[w * TOK:(w + 1) * TOK, at:at + size]
+        rim_w[w * TOK:(w + 1) * TOK, :size] = block
+        rim_wt[at:at + size] = block.T
+    send_w = np.concatenate([send[:208, :low], send[208:256, low:], send[256:, :low]], axis=0)
     bf = lambda a: jnp.asarray(np.ascontiguousarray(a), BF16)
     return (
         bf(spread), bf(gather), bf(pick), jnp.asarray(cross, F32),
-        bf(own), bf(rim), bf(send), bf(own.T), bf(rim.T), bf(send.T),
+        bf(own[:, low:]), bf(rim_w), bf(send_w), bf(own[:, low:].T), bf(rim_wt), bf(send[:, :low].T),
+        bf(send[208:256, low:].T),
     )
 
 
-N_IN = 15
+N_IN = 16
 
 
 def body(lon_size, lat_size, groups, scale, grad_scale, *refs):
@@ -92,8 +103,9 @@
     (out_ref, dx_ref, gqkv_ref, gout_ref, dr_ref) = refs[N_IN:N_IN + 5]
     (cells_v, cot_v, wqkv_ref, wout_ref, r_ref,
      spread_ref, gather_ref, pick_ref, cross_ref, own_ref, rim_ref, send_ref, ownt_ref, rimt_ref, sendt_ref,
+     side_ref,
      load_sem, slab, rim_snd, rim_in, bt, db, x_w, dy_w, normed, normed_t, mix, dproj, wt, ow, rim_osnd, rim_out,
-     kv, k_ts, q_ws, soft_s, m_ts, dm_ws, dq_ts, tab, rows_of, turned,
+     kv, k_ts, q_ws, soft_s, m_ts, dm_ws, dq_ts, tab, rows_of, turned, n_s, rstd_s,
      halo_sem, *comm) = refs[N_IN + 5:]
     chunk_refs = [comm[i * 9:i * 9 + 9] for i in range(len(CHUNKS))]
     (bb, bcrecv, bs, bxrecv, by, byrecv, bfin, b_sem) = comm[len(CHUNKS) * 9:]
@@ -144,7 +156,7 @@
         (cells_h, cells_v), (consts_h[6], send_ref), (cot_h, cot_v), (r_h, r_ref), (consts_h[0], spread_ref),
         (consts_h[3], cross_ref), (wqkv_h, wqkv_ref), (consts_h[4], own_ref), (consts_h[5], rim_ref),
         (consts_h[2], pick_ref), (wout_h, wout_ref), (consts_h[8], rimt_ref), (consts_h[7], ownt_ref),
-        (consts_h[9], sendt_ref), (consts_h[1], gather_ref),
+        (consts_h[9], sendt_ref), (consts_h[10], side_ref), (consts_h[1], gather_ref),
     )
     loads = [pltpu.make_async_copy(s, d, load_sem.at[i]) for i, (s, d) in enumerate(order)]
     for load in loads:
@@ -155,23 +167,29 @@
     def greet(device):
         pl.semaphore_signal(barrier, inc=1, device_id=device, device_id_type=MESH)
 
-    partners = back + ahead + (sibling, pair)
-    partners += tuple(d for _, d, _ in ones + twos + ys) + tuple(d for d, _ in zs)
+    partners = back + ahead + (sibling,)
+    partners += tuple(d for _, d, _ in ones + twos) + tuple(d for d, _ in zs)
     for device in partners:
         greet(device)
 
-    def rim_copies(snd, rcv, devices, base):
+    def rim_copies(f, snd, rcv, devices, base, parts):
         return [
             remote(
                 snd.at[f, pl.ds(at, size)], rcv.at[f, pl.ds(at, size)],
-                halo_sem.at[0, base + f * 3 + k], halo_sem.at[1, base + f * 3 + k], devices[k],
+                halo_sem.at[0, base + k], halo_sem.at[1, base + k], devices[to],
             )
-            for f in range(2)
-            for k, (at, size) in enumerate(RIMS)
+            for k, (at, size, to) in enumerate(parts)
         ]
 
-    rims_in = rim_copies(rim_snd, rim_in, back, 0)
-    rims_out = rim_copies(rim_osnd, rim_out, ahead, 6)
+    rims_in = (
+        rim_copies(0, rim_snd, rim_in, back, 0, FINE_RIMS),
+        rim_copies(1, rim_snd, rim_in, back, 5, RIMS),
+    )
+    rims_out = (
+        rim_copies(0, rim_osnd, rim_out, ahead, 8, RIMS),
+        rim_copies(1, rim_osnd, rim_out, ahead, 11, RIMS),
+    )
+    low = WH // 2 * PITCH
     for f, src in enumerate((cells_v, cot_v)):
         loads[2 * f].wait()
         for s in range(WH):
@@ -180,10 +198,12 @@
             )
         if f == 0:
             loads[1].wait()
-        rim_snd[f] = nn(send_ref[...], slab[f]).astype(BF16)
+        rim_snd[f, :208] = nn(send_ref[:208], slab[f, :low]).astype(BF16)
+        rim_snd[f, 208:256] = nn(send_ref[208:256], slab[f, low:]).astype(BF16)
+        rim_snd[f, 256:] = nn(send_ref[256:], slab[f, :low]).astype(BF16)
         if f == 0:
             pl.semaphore_wait(barrier, len(partners))
-        for copy in rims_in[3 * f:3 * f + 3]:
+        for copy in rims_in[f]:
             copy.start()
 
     for load in loads[3:6]:
@@ -227,21 +247,17 @@
         wt[part * c:(part + 1) * c, :] = nt(eye, wqkv_ref[:, part * c:(part + 1) * c]).astype(BF16)
     pick = pick_ref[...]
 
-    def arrive(f, ref):
-        for copy in rims_in[3 * f:3 * f + 3]:
+    def arrive(f, w, ref):
+        if f == 0:
+            parts = rims_in[0][w:w + 1] if w < WINDOWS - 1 else rims_in[0][w:]
+        else:
+            parts = rims_in[1][:1] if w == 0 else rims_in[1][1:] if w == WINDOWS - 1 else []
+        for copy in parts:
             copy.wait()
-        ref[...] = (nn(own_ref[...], slab[f]) + nn(rim_ref[...], rim_in[f])).astype(BF16)
-
-    arrive(0, x_w)
-    cells = x_w[...].astype(F32)
-    average = jnp.mean(cells, axis=-1, keepdims=True)
-    centred = cells - average
-    variance = jnp.mean(centred * centred, axis=-1, keepdims=True)
-    rstd = lax.rsqrt(variance + 1e-05)
-    normed[...] = (centred * rstd).astype(BF16)
-    normed_t[...] = nt(eye, normed[...]).astype(BF16)
-
-    kv[...] = nn(normed[...], wqkv_ref[:, c:]).astype(BF16)
+        at, (first, size) = slice(w * TOK, (w + 1) * TOK), RIM_OF[w]
+        ref[at, :] = (
+            nn(own_ref[at, :], slab[f, low:]) + nn(rim_ref[at, :size], rim_in[f, first:first + size])
+        ).astype(BF16)
 
     def at_of(w):
         return slice(w * TOK, (w + 1) * TOK)
@@ -251,7 +267,18 @@
 
     def forward(w):
         at = at_of(w)
-        qkv_t = nt(wt[...], normed[at, :]).astype(BF16)
+        arrive(0, w, x_w)
+        cells = x_w[at, :].astype(F32)
+        average = jnp.mean(cells, axis=-1, keepdims=True)
+        centred = cells - average
+        rstd = lax.rsqrt(jnp.mean(centred * centred, axis=-1, keepdims=True) + 1e-05)
+        rstd_s[at, :] = rstd
+        n_w = centred * rstd
+        n_s[at, :] = n_w
+        here = n_w.astype(BF16)
+        normed[at, :] = here
+        kv[at, :] = nn(here, wqkv_ref[:, c:]).astype(BF16)
+        qkv_t = nt(wt[...], here).astype(BF16)
         q_all = nn(qkv_t[:c], pick)
         k_ts[w] = qkv_t[c:2 * c]
         for g in range(groups):
@@ -300,6 +327,7 @@
         chunk_refs[i][0][at] = value.astype(BF16)
 
     def out_grads():
+        normed_t[...] = nt(eye, normed[...]).astype(BF16)
         grad = nn(nt(eye, mix[...]).astype(BF16), dy_w[...]) * grad_scale
         for k in range(3):
             for r in range(24):
@@ -390,7 +418,7 @@
     def unpack(first, end):
         for t in range(first, end):
             i, at = tile_at(t)
-            value = chains[i].fin[at]
+            value = chains[i].fin[at].astype(F32)
             r, k = t % 24, t // 24
             rows = slice(r * 16, (r + 1) * 16)
             if k < 3:
@@ -501,78 +529,76 @@
                         tab[g * GROUP:(g + 1) * GROUP, segment(z1, z2, i1)] = flat[at:at + GROUP, :width]
         dr_ref[:, 0, :] = tab[...]
 
+    def pack_out(f):
+        for w, (first, size) in enumerate(RIM_OF):
+            rim_osnd[f, first:first + size] = nn(rimt_ref[first:first + size], ow[f, at_of(w)]).astype(BF16)
+
     def finish(f, ref):
-        for copy in rims_out[3 * f:3 * f + 3]:
+        for copy in rims_out[f]:
             copy.wait()
-        full = (nn(ownt_ref[...], ow[f]) + nn(sendt_ref[...], rim_out[f])).astype(BF16)
+        upper = nn(sendt_ref[...], rim_out[f]).astype(BF16)
+        lower = (nn(ownt_ref[...], ow[f]) + nn(side_ref[...], rim_out[f, 208:256])).astype(BF16)
         for s in range(WH):
-            ref[s] = full[s * PITCH:s * PITCH + COLS * LEV].reshape(COLS, LEV, c)
-
-    c0, c1, c2 = chains
+            full, r = (upper, s) if s < WH // 2 else (lower, s - WH // 2)
+            ref[s] = full[r * PITCH:r * PITCH + COLS * LEV].reshape(COLS, LEV, c)
+
+    c0, c1 = chains
     for w in range(WINDOWS):
         forward(w)
-    ow[0] = (cells + nn(mix[...], wout_ref[...])).astype(BF16)
-    rim_osnd[0] = nn(rimt_ref[...], ow[0]).astype(BF16)
-    for copy in rims_out[:3]:
+    ow[0] = (x_w[...].astype(F32) + nn(mix[...], wout_ref[...])).astype(BF16)
+    pack_out(0)
+    for copy in rims_out[0]:
         copy.start()
-    arrive(1, dy_w)
+    for w in range(WINDOWS):
+        arrive(1, w, dy_w)
     out_grads()
-    c0.start()
     for w in range(WINDOWS):
         widen(w)
-    backward(0, 0)
+    for w in range(WINDOWS):
+        backward(0, w)
+    qkv_grads(0)
+    c0.start()
+    backward(1, 0)
+    backward(1, 1)
     c0.first()
-    backward(0, 1)
-    backward(0, 2)
-    qkv_grads(0)
+    backward(1, 2)
+    qkv_grads(1)
+    backward(2, 0)
     c0.second()
-    for w in range(WINDOWS):
-        backward(1, w)
-    qkv_grads(1)
+    backward(2, 1)
+    backward(2, 2)
+    qkv_grads(2)
     c1.start()
     c0.third()
-    backward(2, 0)
-    backward(2, 1)
+    dn = nt(dproj[...], wqkv_ref[...])
+    n_w = n_s[...]
+    dx = dn - jnp.mean(dn, axis=-1, keepdims=True) - n_w * jnp.mean(dn * n_w, axis=-1, keepdims=True)
+    ow[1] = (dx * rstd_s[...] + dy_w[...].astype(F32)).astype(BF16)
     c1.first()
-    backward(2, 2)
-    qkv_grads(2)
-    c2.start()
-    dn = nt(dproj[...], wqkv_ref[...])
-    n_w = centred * rstd
-    dx = (dn - jnp.mean(dn, axis=-1, keepdims=True) - n_w * jnp.mean(dn * n_w, axis=-1, keepdims=True)) * rstd
-    ow[1] = (dx + dy_w[...].astype(F32)).astype(BF16)
-    c2.first()
-    rim_osnd[1] = nn(rimt_ref[...], ow[1]).astype(BF16)
+    pack_out(1)
+    bias_core()
     c0.fourth()
     c1.second()
-    c2.second()
-    bias_core()
-    c1.third()
-    c2.third()
-    for copy in rims_out[3:]:
-        copy.start()
     bias_x()
     c0.fifth()
+    c1.third()
+    for copy in rims_out[1]:
+        copy.start()
+    bias_y()
     finish(0, out_ref)
-    bias_y()
+    c0.sixth()
     c1.fourth()
-    c2.fourth()
-    c0.sixth()
     bias_back_y()
-    c1.fifth()
-    c2.fifth()
-    bias_back_x()
     c0.last()
     unpack(0, CHUNKS[0])
+    c1.fifth()
+    bias_back_x()
+    finish(1, dx_ref)
+    bias_back_core()
     c1.sixth()
-    c2.sixth()
-    bias_back_core()
-    finish(1, dx_ref)
+    bias_end()
     c1.last()
-    unpack(CHUNKS[0], CHUNKS[0] + CHUNKS[1])
-    bias_end()
-    c2.last()
-    unpack(CHUNKS[0] + CHUNKS[1], sum(CHUNKS))
+    unpack(CHUNKS[0], sum(CHUNKS))
     for chain in chains:
         chain.drain()
 
@@ -615,7 +641,9 @@
         vm((heads, entries), F32),
         vm((heads * SLABS, WH * SPAN), F32),
         vm((256, 384), F32),
-        dma((2, 12)),
+        vm((ROWS, c), F32),
+        vm((ROWS, 1), F32),
+        dma((2, 14)),
     ]
     tile = (16, 128)
     for tiles in CHUNKS:
@@ -647,11 +675,11 @@
     out_shape = (
         jax.ShapeDtypeStruct(cells.shape, BF16),
         jax.ShapeDtypeStruct(cells.shape, BF16),
-        jax.ShapeDtypeStruct((c, 3 * c), BF16),
-        jax.ShapeDtypeStruct((c, c), BF16),
+        jax.ShapeDtypeStruct((c, 3 * c), F32),
+        jax.ShapeDtypeStruct((c, c), F32),
         jax.ShapeDtypeStruct(table.shape, F32),
     )
-    return pl.pallas_call(
+    results = pl.pallas_call(
         kernel,
         out_shape=out_shape,
         in_specs=[pl.BlockSpec(memory_space=pl.ANY)] * len(ins),
@@ -662,6 +690,37 @@
         ),
         cost_estimate=pl.CostEstimate(flops=6_000_000_000, bytes_accessed=10_000_000, transcendentals=800_000),
     )(*ins)
+    return handed_out(results)
+
+
+def handed_out(arrays):
+    cuts = [(i, k) for i, a in enumerate(arrays) for k in range(6 if i == 2 else 2 if i == 3 else 1)]
+
+    def move(*refs):
+        ins, outs, (sem, *held) = refs[:len(arrays)], refs[len(arrays):2 * len(arrays)], refs[2 * len(arrays):]
+        into, out_of = [], []
+        for j, (i, k) in enumerate(cuts):
+            parts = sum(1 for at, _ in cuts if at == i)
+            rows = arrays[i].shape[0] // parts
+            at = pl.ds(k * rows, rows)
+            into.append(pltpu.make_async_copy(ins[i].at[at], held[i].at[at], sem.at[0, j]))
+            out_of.append(pltpu.make_async_copy(held[i].at[at], outs[i].at[at], sem.at[1, j]))
+        for copy in into:
+            copy.start()
+        for first, second in zip(into, out_of):
+            first.wait()
+            second.start()
+        for copy in out_of:
+            copy.wait()
+
+    return pl.pallas_call(
+        move,
+        out_shape=tuple(jax.ShapeDtypeStruct(a.shape, a.dtype) for a in arrays),
+        in_specs=[pl.BlockSpec(memory_space=pl.ANY)] * len(arrays),
+        out_specs=(pl.BlockSpec(memory_space=pl.ANY),) * len(arrays),
+        scratch_shapes=[pltpu.SemaphoreType.DMA((2, len(cuts)))] + [pltpu.VMEM(a.shape, a.dtype) for a in arrays],
+        compiler_params=pltpu.CompilerParams(vmem_limit_bytes=60 * 1024 * 1024),
+    )(*arrays)
 
 
 def on_device(cells, qkv_weight, out_weight, earth_bias, cotangent):
@@ -673,7 +732,7 @@
         lon_size, lat_size, cells_total
     )
     out, dx = out.transpose(2, 0, 1, 3), dx.transpose(2, 0, 1, 3)
-    return out, dx, gqkv.astype(F32), gout.astype(F32), dr.transpose(1, 0, 2)
+    return out, dx, gqkv, gout, dr.transpose(1, 0, 2)
 
 
 def solution(mesh):

time: 75.1 us -> 71.3 us (0.949)
  other arithmetic: 3.42 us -> 0 us
  local copies, waits for them, and re-layouts: 2.13 us -> 0 us
  Pallas kernels: 68.8 us -> 70.4 us
    convert_element_type x2 -> x0, other arithmetic: 3.42 us -> none  [on_device(): return (out, dx, gqkv.astype(F32), gout.astype(F32), dr.transpose(1, 0, 2))]
    pallas_call x0 -> x1, Pallas kernels: none -> 2.83 us  [handed_out(): pl.pallas_call(move, out_shape=tuple((jax.ShapeDtypeStruct(a.shape, a.dty...]
    unnamed x11 -> x0, local copies, waits for them, and re-layouts: 2.13 us -> none
    pallas_call x1, Pallas kernels: 68.8 us -> 67.6 us  [fused(): pl.pallas_call(kernel, out_shape=out_shape, in_specs=[pl.BlockSpec(memory...]
where the time goes in v6:
time: 71.3 us; the launch traced here: 71.2 us
  Pallas kernels  70.4 us (99%)
  between operations  0.8 us (1%)
    pallas_call x1, Pallas kernels, fused(): pl.pallas_call(kernel, out_shape=out_shape, in_specs=[pl.BlockSpec(memory...  67.6 us
    pallas_call x1, Pallas kernels, handed_out(): pl.pallas_call(move, out_shape=tuple((jax.ShapeDtypeStruct(a.shape, a.dty...  2.83 us

profile of v6, /device:TPU:1, one launch (start us, length us, event | category | flops | bytes accessed | tf_op | source)
XLA Modules:
  0.0 71.2 jit_solution(17456429222984130396)
XLA Ops:
  0.6 67.6 %shard_map.191 = (bf16[6,36,2,384]{3,2,1,0:T(2,128)(2,1)}, bf16[6,36,2,384]{3,2,1,0:T(2,128)(2,1)}, f32[384,1152]{1,0:T(8,128)}, f32[384,384]{1,0:T(8,128)}, f32[12,1,3312]{2,1,0:T(1,128)}) custom-call(bf16[6,36,2,384]{3,2,1,0:T(2,128)(2,1)} %bitcast.6, bf16[6,36,2,384]{3,2,1,0:T(2,128)(2,1)} %bitcast.7, bf16[384,1152]{1,0:T(8,128)(2,1)} %refs_2_.1, ...), custom_call_target="tpu_custom_call" | custom-call | flops 6000000000 | bytes 10000000 | tf_op jit(solution)/shard_map/pallas_call | solution.py:682
  68.3 2.8 %shard_map.192 = (bf16[6,36,2,384]{3,2,1,0:T(2,128)(2,1)}, bf16[6,36,2,384]{3,2,1,0:T(2,128)(2,1)}, f32[384,1152]{1,0:T(8,128)}, f32[384,384]{1,0:T(8,128)}, f32[12,1,3312]{2,1,0:T(1,128)}) custom-call(bf16[6,36,2,384]{3,2,1,0:T(2,128)(2,1)} %get-tuple-element.15.refs_0_, bf16[6,36,2,384]{3,2,1,0:T(2,128)(2,1)} %get-tuple-element.16.refs_1_, ...), custom_call_target="tpu_custom_call" | custom-call | tf_op jit(solution)/shard_map/pallas_call | solution.py:716

commit v7 on v6

--- a/solution.py
+++ b/solution.py
@@ -26,7 +26,7 @@
 RIM_OF = ((0, 80), (80, 80), (160, 144))
 RIM = 304
 BIAS_TILES = 32
-CHUNKS = (128, 160)
+CHUNKS = (96, 96, 96)
 X_HI = 2
 F32 = jnp.float32
 BF16 = jnp.bfloat16
@@ -107,8 +107,8 @@
      load_sem, slab, rim_snd, rim_in, bt, db, x_w, dy_w, normed, normed_t, mix, dproj, wt, ow, rim_osnd, rim_out,
      kv, k_ts, q_ws, soft_s, m_ts, dm_ws, dq_ts, tab, rows_of, turned, n_s, rstd_s,
      halo_sem, *comm) = refs[N_IN + 5:]
-    chunk_refs = [comm[i * 9:i * 9 + 9] for i in range(len(CHUNKS))]
-    (bb, bcrecv, bs, bxrecv, by, byrecv, bfin, b_sem) = comm[len(CHUNKS) * 9:]
+    chunk_refs = [comm[i * 7:i * 7 + 7] for i in range(len(CHUNKS))]
+    (bb, bcrecv, bs, bxrecv, by, byrecv, bfin, b_sem) = comm[len(CHUNKS) * 7:]
     c = wout_ref.shape[0]
     n, nz = lon_size // 4, lat_size // X_HI
     half = WH * WW
@@ -120,8 +120,8 @@
     x_hi, z = lat // nz, lat % nz
     x = x_hi * 2 + x_lo
     other = 1 - core
-    one = jnp.where(core == 0, x, y)
-    two = jnp.where(core == 0, y, x)
+    nxy = n * n
+    p = y * n + x
 
     def dev(lon_at, lat_at):
         return {"lon": lon_at, "lat": lat_at}
@@ -130,12 +130,11 @@
         return dev((y_at * 2 + x_at % 2) * 2 + core, x_at // 2 * nz + z)
 
     sibling = dev(lon + 1 - 2 * core, lat)
-    ones, twos, zs, ys = [], [], [], []
+    plane, zs, ys = [], [], []
+    for o in range(1, nxy):
+        q = (p + o) % nxy
+        plane.append((q, chip(q % n, q // n)))
     for o in range(1, n):
-        q = (one + o) % n
-        ones.append((q, chip(jnp.where(core == 0, q, x), jnp.where(core == 0, y, q)), (one + n - o) % n))
-        q = (two + o) % n
-        twos.append((q, chip(jnp.where(core == 0, x, q), jnp.where(core == 0, q, y)), (two + n - o) % n))
         q = (y + o) % n
         ys.append((q, chip(x, q), (y + n - o) % n))
     for o in range(1, nz):
@@ -168,7 +167,7 @@
         pl.semaphore_signal(barrier, inc=1, device_id=device, device_id_type=MESH)
 
     partners = back + ahead + (sibling,)
-    partners += tuple(d for _, d, _ in ones + twos) + tuple(d for d, _ in zs)
+    partners += tuple(d for _, d in plane) + tuple(d for d, _ in zs)
     for device in partners:
         greet(device)
 
@@ -319,8 +318,8 @@
             t -= CHUNKS[i]
             i += 1
         half_tiles = CHUNKS[i] // 2
-        share = half_tiles // (n * n)
-        return i, (t // half_tiles, t % half_tiles // (n * share), t % (n * share) // share, t % share)
+        share = half_tiles // nxy
+        return i, (t // half_tiles, t % half_tiles // share, t % share)
 
     def put(t, value):
         i, at = tile_at(t)
@@ -344,7 +343,7 @@
 
     class Chain:
         def __init__(self, refs):
-            (self.gb, self.crecv, self.xs, self.arecv, self.ys, self.brecv, self.zbuf, self.fin, self.sem) = refs
+            (self.gb, self.crecv, self.xs, self.xrecv, self.zbuf, self.fin, self.sem) = refs
 
         def send(self, stage, src, dst, device):
             remote(src, dst, self.sem.at[0, stage], self.sem.at[1, stage], device).start()
@@ -358,60 +357,43 @@
         def first(self):
             self.wait(1, 0, self.crecv)
             self.xs[...] = (self.gb[core].astype(F32) + self.crecv[...].astype(F32)).astype(BF16)
-            for o, (q, d, _) in enumerate(ones):
-                self.send(1, self.xs.at[q], self.arecv.at[o], d)
+            for o, (q, d) in enumerate(plane):
+                self.send(1, self.xs.at[q], self.xrecv.at[o], d)
 
         def second(self):
-            self.wait(1, 1, self.arecv)
-            total = self.xs[one].astype(F32)
-            for o in range(n - 1):
-                total += self.arecv[o].astype(F32)
-            self.ys[...] = total.astype(BF16)
-            for o, (q, d, _) in enumerate(twos):
-                self.send(2, self.ys.at[q], self.brecv.at[o], d)
-
-        def third(self):
-            self.wait(1, 2, self.brecv)
-            total = self.ys[two].astype(F32)
-            for o in range(n - 1):
-                total += self.brecv[o].astype(F32)
+            self.wait(1, 1, self.xrecv)
+            total = self.xs[p].astype(F32)
+            for o in range(nxy - 1):
+                total += self.xrecv[o].astype(F32)
             self.zbuf[0] = total.astype(BF16)
             for o, (d, _) in enumerate(zs):
-                self.send(3, self.zbuf.at[0], self.zbuf.at[o + 1], d)
-
-        def fourth(self):
+                self.send(2, self.zbuf.at[0], self.zbuf.at[o + 1], d)
+
+        def third(self):
             if nz > 1:
-                self.wait(1, 3, self.zbuf.at[pl.ds(1, nz - 1)])
+                self.wait(1, 2, self.zbuf.at[pl.ds(1, nz - 1)])
             total = self.zbuf[z].astype(F32)
             for k in range(1, nz):
                 total += self.zbuf[(z + nz - k) % nz].astype(F32)
-            mine_at = self.fin.at[core, one, two]
+            mine_at = self.fin.at[core, p]
             mine_at[...] = total.astype(BF16)
-            for _, d, _ in twos:
-                self.send(4, mine_at, mine_at, d)
-
-        def fifth(self):
-            self.wait(1, 4, self.fin.at[core, one, pl.ds(0, n - 1)])
-            mine_at = self.fin.at[core, one]
-            for _, d, _ in ones:
-                self.send(5, mine_at, mine_at, d)
-
-        def sixth(self):
-            self.wait(1, 5, self.fin.at[core, pl.ds(0, n - 1)])
-            self.send(6, self.fin.at[core], self.fin.at[core], sibling)
+            for _, d in plane:
+                self.send(3, mine_at, mine_at, d)
+
+        def fourth(self):
+            self.wait(1, 3, self.xrecv)
+            self.send(4, self.fin.at[core], self.fin.at[core], sibling)
 
         def last(self):
-            self.wait(1, 6, self.fin.at[other])
+            self.wait(1, 4, self.fin.at[other])
 
         def drain(self):
             self.wait(0, 0, self.crecv)
-            self.wait(0, 1, self.arecv)
-            self.wait(0, 2, self.brecv)
+            self.wait(0, 1, self.xrecv)
             if nz > 1:
-                self.wait(0, 3, self.zbuf.at[pl.ds(1, nz - 1)])
-            self.wait(0, 4, self.brecv)
-            self.wait(0, 5, self.arecv)
-            self.wait(0, 6, self.crecv)
+                self.wait(0, 2, self.zbuf.at[pl.ds(1, nz - 1)])
+            self.wait(0, 3, self.xrecv)
+            self.wait(0, 4, self.crecv)
 
     chains = [Chain(r) for r in chunk_refs]
 
@@ -542,7 +524,7 @@
             full, r = (upper, s) if s < WH // 2 else (lower, s - WH // 2)
             ref[s] = full[r * PITCH:r * PITCH + COLS * LEV].reshape(COLS, LEV, c)
 
-    c0, c1 = chains
+    c0, c1, c2 = chains
     for w in range(WINDOWS):
         forward(w)
     ow[0] = (x_w[...].astype(F32) + nn(mix[...], wout_ref[...])).astype(BF16)
@@ -563,42 +545,45 @@
     c0.first()
     backward(1, 2)
     qkv_grads(1)
+    c1.start()
     backward(2, 0)
-    c0.second()
     backward(2, 1)
+    c1.first()
     backward(2, 2)
     qkv_grads(2)
-    c1.start()
-    c0.third()
+    c2.start()
+    c0.second()
     dn = nt(dproj[...], wqkv_ref[...])
     n_w = n_s[...]
     dx = dn - jnp.mean(dn, axis=-1, keepdims=True) - n_w * jnp.mean(dn * n_w, axis=-1, keepdims=True)
     ow[1] = (dx * rstd_s[...] + dy_w[...].astype(F32)).astype(BF16)
-    c1.first()
+    c2.first()
     pack_out(1)
+    c1.second()
     bias_core()
-    c0.fourth()
-    c1.second()
-    bias_x()
-    c0.fifth()
-    c1.third()
+    c0.third()
+    c2.second()
     for copy in rims_out[1]:
         copy.start()
+    bias_x()
+    c1.third()
+    finish(0, out_ref)
+    c0.fourth()
+    c2.third()
     bias_y()
-    finish(0, out_ref)
-    c0.sixth()
+    c0.last()
+    unpack(0, 96)
     c1.fourth()
     bias_back_y()
-    c0.last()
-    unpack(0, CHUNKS[0])
-    c1.fifth()
+    c2.fourth()
     bias_back_x()
+    c1.last()
+    unpack(96, 192)
     finish(1, dx_ref)
     bias_back_core()
-    c1.sixth()
     bias_end()
-    c1.last()
-    unpack(CHUNKS[0], sum(CHUNKS))
+    c2.last()
+    unpack(192, 288)
     for chain in chains:
         chain.drain()
 
@@ -649,15 +634,13 @@
     for tiles in CHUNKS:
         share = tiles // (2 * n * n)
         scratch += [
-            vm((2, n, n, share) + tile, BF16),
-            vm((n, n, share) + tile, BF16),
-            vm((n, n, share) + tile, BF16),
-            vm((n - 1, n, share) + tile, BF16),
-            vm((n, share) + tile, BF16),
-            vm((n - 1, share) + tile, BF16),
+            vm((2, n * n, share) + tile, BF16),
+            vm((n * n, share) + tile, BF16),
+            vm((n * n, share) + tile, BF16),
+            vm((n * n - 1, share) + tile, BF16),
             vm((nz, share) + tile, BF16),
-            vm((2, n, n, share) + tile, BF16),
-            dma((2, 7)),
+            vm((2, n * n, share) + tile, BF16),
+            dma((2, 5)),
         ]
     scratch += [
         vm((2, 2, n, bshare) + tile, BF16),

time: 71.3 us -> 67 us (0.940)
  Pallas kernels: 70.4 us -> 66.1 us
    pallas_call x1, Pallas kernels: 67.6 us -> 63.3 us  [fused(): pl.pallas_call(kernel, out_shape=out_shape, in_specs=[pl.BlockSpec(memory...]
where the time goes in v7:
time: 67 us; the launch traced here: 66.9 us
  Pallas kernels  66.1 us (99%)
  between operations  0.8 us (1%)
    pallas_call x1, Pallas kernels, fused(): pl.pallas_call(kernel, out_shape=out_shape, in_specs=[pl.BlockSpec(memory...  63.3 us
    pallas_call x1, Pallas kernels, handed_out(): pl.pallas_call(move, out_shape=tuple((jax.ShapeDtypeStruct(a.shape, a.dty...  2.83 us

profile of v7, /device:TPU:1, one launch (start us, length us, event | category | flops | bytes accessed | tf_op | source)
XLA Modules:
  0.0 66.9 jit_solution(6167602855769435783)
XLA Ops:
  0.6 63.3 %shard_map.191 = (bf16[6,36,2,384]{3,2,1,0:T(2,128)(2,1)}, bf16[6,36,2,384]{3,2,1,0:T(2,128)(2,1)}, f32[384,1152]{1,0:T(8,128)}, f32[384,384]{1,0:T(8,128)}, f32[12,1,3312]{2,1,0:T(1,128)}) custom-call(bf16[6,36,2,384]{3,2,1,0:T(2,128)(2,1)} %bitcast.6, bf16[6,36,2,384]{3,2,1,0:T(2,128)(2,1)} %bitcast.7, bf16[384,1152]{1,0:T(8,128)(2,1)} %refs_2_.1, ...), custom_call_target="tpu_custom_call" | custom-call | flops 6000000000 | bytes 10000000 | tf_op jit(solution)/shard_map/pallas_call | solution.py:665
  63.9 2.8 %shard_map.192 = (bf16[6,36,2,384]{3,2,1,0:T(2,128)(2,1)}, bf16[6,36,2,384]{3,2,1,0:T(2,128)(2,1)}, f32[384,1152]{1,0:T(8,128)}, f32[384,384]{1,0:T(8,128)}, f32[12,1,3312]{2,1,0:T(1,128)}) custom-call(bf16[6,36,2,384]{3,2,1,0:T(2,128)(2,1)} %get-tuple-element.15.refs_0_, bf16[6,36,2,384]{3,2,1,0:T(2,128)(2,1)} %get-tuple-element.16.refs_1_, ...), custom_call_target="tpu_custom_call" | custom-call | tf_op jit(solution)/shard_map/pallas_call | solution.py:699

commit v8 on v7

--- a/solution.py
+++ b/solution.py
@@ -100,15 +100,16 @@
 def body(lon_size, lat_size, groups, scale, grad_scale, *refs):
     (cells_h, cot_h, wqkv_h, wout_h, r_h) = refs[:5]
     consts_h = refs[5:N_IN]
-    (out_ref, dx_ref, gqkv_ref, gout_ref, dr_ref) = refs[N_IN:N_IN + 5]
+    outs_h = refs[N_IN:N_IN + 5]
     (cells_v, cot_v, wqkv_ref, wout_ref, r_ref,
      spread_ref, gather_ref, pick_ref, cross_ref, own_ref, rim_ref, send_ref, ownt_ref, rimt_ref, sendt_ref,
      side_ref,
      load_sem, slab, rim_snd, rim_in, bt, db, x_w, dy_w, normed, normed_t, mix, dproj, wt, ow, rim_osnd, rim_out,
      kv, k_ts, q_ws, soft_s, m_ts, dm_ws, dq_ts, tab, rows_of, turned, n_s, rstd_s,
      halo_sem, *comm) = refs[N_IN + 5:]
+    (out_ref, dx_ref, gqkv_ref, gout_ref, dr_ref, out_sem) = comm[-6:]
     chunk_refs = [comm[i * 7:i * 7 + 7] for i in range(len(CHUNKS))]
-    (bb, bcrecv, bs, bxrecv, by, byrecv, bfin, b_sem) = comm[len(CHUNKS) * 7:]
+    (bb, brecv, bfin, b_sem) = comm[len(CHUNKS) * 7:-6]
     c = wout_ref.shape[0]
     n, nz = lon_size // 4, lat_size // X_HI
     half = WH * WW
@@ -130,16 +131,15 @@
         return dev((y_at * 2 + x_at % 2) * 2 + core, x_at // 2 * nz + z)
 
     sibling = dev(lon + 1 - 2 * core, lat)
-    plane, zs, ys = [], [], []
+    plane, zs, line = [], [], []
     for o in range(1, nxy):
         q = (p + o) % nxy
         plane.append((q, chip(q % n, q // n)))
-    for o in range(1, n):
-        q = (y + o) % n
-        ys.append((q, chip(x, q), (y + n - o) % n))
+    for o in range(1, lon_size):
+        q = (lon + o) % lon_size
+        line.append((q, dev(q, lat)))
     for o in range(1, nz):
         zs.append((dev(lon, x_hi * nz + (z + o) % nz), (z + nz - o) % nz))
-    pair = dev((y * 2 + 1 - x_lo) * 2 + core, lat)
 
     lon_prev, lon_next = (lon + lon_size - 1) % lon_size, (lon + 1) % lon_size
     lat_prev, lat_next = (lat + lat_size - 1) % lat_size, (lat + 1) % lat_size
@@ -166,8 +166,8 @@
     def greet(device):
         pl.semaphore_signal(barrier, inc=1, device_id=device, device_id_type=MESH)
 
-    partners = back + ahead + (sibling,)
-    partners += tuple(d for _, d in plane) + tuple(d for d, _ in zs)
+    partners = back + ahead
+    partners += tuple(d for _, d in plane + line) + tuple(d for d, _ in zs)
     for device in partners:
         greet(device)
 
@@ -409,32 +409,10 @@
                 g, part = (k - 3) // 3, (k - 3) % 3
                 gqkv_ref[rows, g_of(g, part)] = value
 
-    bshare = BIAS_TILES // (4 * n)
-
-    def bcopy(k, src, dst, device):
-        return remote(src, dst, b_sem.at[0, k], b_sem.at[1, k], device)
-
-    def bcore_copy():
-        return bcopy(0, bb.at[other], bcrecv, sibling)
-
-    def bx_copy():
-        return bcopy(1, bs.at[1 - x_lo], bxrecv, pair)
-
-    def by_copies():
-        return [bcopy(2 + o, by.at[q], byrecv.at[o], d) for o, (q, d, _) in enumerate(ys)]
-
-    def by_back(here=True):
-        at = [y if here else q for _, _, q in ys]
-        return [
-            bcopy(5 + o, bfin.at[core, x_lo, at[o]], bfin.at[core, x_lo, at[o]], d)
-            for o, (_, d, _) in enumerate(ys)
-        ]
-
-    def bx_back(x_at):
-        return bcopy(8, bfin.at[core, x_at], bfin.at[core, x_at], pair)
-
-    def bcore_back(half_at):
-        return bcopy(9, bfin.at[half_at], bfin.at[half_at], sibling)
+    bshare = BIAS_TILES // lon_size
+
+    def bias_wait(side, stage):
+        pltpu.make_async_copy(brecv, brecv, b_sem.at[side, stage]).wait()
 
     def bias_core():
         rows = jnp.concatenate(
@@ -457,47 +435,24 @@
             k, r = t // 9, t % 9
             tile = dr[r * 16:(r + 1) * 16, k * 128:(k + 1) * 128] if k < 3 else jnp.zeros((16, 128), BF16)
             bb[bias_at(t)] = tile
-        bcore_copy().start()
+        for o, (q, d) in enumerate(line):
+            remote(bb.at[q], brecv.at[o], b_sem.at[0, 0], b_sem.at[1, 0], d).start()
 
     def bias_at(t):
-        return t // 16, t % 16 // (n * bshare), t % (n * bshare) // bshare, t % bshare
-
-    def bias_x():
-        bcore_copy().wait()
-        bs[...] = (bb[core].astype(F32) + bcrecv[...].astype(F32)).astype(BF16)
-        bx_copy().start()
-
-    def bias_y():
-        bx_copy().wait()
-        by[...] = (bs[x_lo].astype(F32) + bxrecv[...].astype(F32)).astype(BF16)
-        for copy in by_copies():
-            copy.start()
-
-    def bias_back_y():
-        for copy in by_copies():
-            copy.wait()
-        total = by[y].astype(F32)
-        for o in range(n - 1):
-            total += byrecv[o].astype(F32)
-        bfin[core, x_lo, y] = total.astype(BF16)
-        for copy in by_back():
-            copy.start()
-
-    def bias_back_x():
-        for copy in by_back():
-            copy.wait_send()
-        for copy in by_back(False):
-            copy.wait_recv()
-        bx_back(x_lo).start()
-
-    def bias_back_core():
-        bx_back(x_lo).wait_send()
-        bx_back(1 - x_lo).wait_recv()
-        bcore_back(core).start()
+        return t // bshare, t % bshare
+
+    def bias_back():
+        bias_wait(1, 0)
+        total = bb[lon].astype(F32)
+        for o in range(lon_size - 1):
+            total += brecv[o].astype(F32)
+        mine_at = bfin.at[lon]
+        mine_at[...] = total.astype(BF16)
+        for _, d in line:
+            remote(mine_at, mine_at, b_sem.at[0, 1], b_sem.at[1, 1], d).start()
 
     def bias_end():
-        bcore_back(core).wait_send()
-        bcore_back(other).wait_recv()
+        bias_wait(1, 1)
         turned[144:, :] = jnp.zeros((256 - 144, 384), F32)
         for t in range(27):
             k, r = t // 9, t % 9
@@ -523,6 +478,17 @@
         for s in range(WH):
             full, r = (upper, s) if s < WH // 2 else (lower, s - WH // 2)
             ref[s] = full[r * PITCH:r * PITCH + COLS * LEV].reshape(COLS, LEV, c)
+
+    stores = []
+
+    def store(src, dst):
+        stores.append(pltpu.make_async_copy(src, dst, out_sem.at[len(stores)]))
+        stores[-1].start()
+
+    def store_columns(first, end):
+        for k in range(first, end):
+            at = (slice(None), g_of(k // 3, k % 3))
+            store(gqkv_ref.at[at], outs_h[2].at[at])
 
     c0, c1, c2 = chains
     for w in range(WINDOWS):
@@ -565,27 +531,33 @@
     c2.second()
     for copy in rims_out[1]:
         copy.start()
-    bias_x()
+    finish(0, out_ref)
+    store(out_ref, outs_h[0])
     c1.third()
-    finish(0, out_ref)
     c0.fourth()
+    bias_back()
     c2.third()
-    bias_y()
     c0.last()
     unpack(0, 96)
+    store(gout_ref, outs_h[3])
     c1.fourth()
-    bias_back_y()
-    c2.fourth()
-    bias_back_x()
+    bias_end()
+    store(dr_ref, outs_h[4])
+    finish(1, dx_ref)
+    store(dx_ref, outs_h[1])
     c1.last()
     unpack(96, 192)
-    finish(1, dx_ref)
-    bias_back_core()
-    bias_end()
+    store_columns(0, 5)
+    c2.fourth()
     c2.last()
     unpack(192, 288)
+    store_columns(5, 9)
+    for copy in stores:
+        copy.wait()
     for chain in chains:
         chain.drain()
+    bias_wait(0, 0)
+    bias_wait(0, 1)
 
 
 def fused(cells, cot, qkv_weight, out_weight, table, lon_size, lat_size, cells_total):
@@ -595,10 +567,17 @@
     consts = constants()
     ins = (cells, cot, qkv_weight, out_weight, table) + consts
     n, nz = lon_size // 4, lat_size // X_HI
-    bshare = BIAS_TILES // (4 * n)
+    bshare = BIAS_TILES // lon_size
     gw = GROUP * HEAD
     vm = pltpu.VMEM
     dma = pltpu.SemaphoreType.DMA
+    out_shape = (
+        jax.ShapeDtypeStruct(cells.shape, BF16),
+        jax.ShapeDtypeStruct(cells.shape, BF16),
+        jax.ShapeDtypeStruct((c, 3 * c), F32),
+        jax.ShapeDtypeStruct((c, c), F32),
+        jax.ShapeDtypeStruct(table.shape, F32),
+    )
     scratch = [vm(a.shape, a.dtype) for a in ins] + [
         dma((len(ins),)),
         vm((2, WH * PITCH, c), BF16),
@@ -643,30 +622,20 @@
             dma((2, 5)),
         ]
     scratch += [
-        vm((2, 2, n, bshare) + tile, BF16),
-        vm((2, n, bshare) + tile, BF16),
-        vm((2, n, bshare) + tile, BF16),
-        vm((n, bshare) + tile, BF16),
-        vm((n, bshare) + tile, BF16),
-        vm((n - 1, bshare) + tile, BF16),
-        vm((2, 2, n, bshare) + tile, BF16),
-        dma((2, 10)),
+        vm((lon_size, bshare) + tile, BF16),
+        vm((lon_size - 1, bshare) + tile, BF16),
+        vm((lon_size, bshare) + tile, BF16),
+        dma((2, 2)),
     ]
+    scratch += [vm(a.shape, a.dtype) for a in out_shape] + [dma((13,))]
     kernel = functools.partial(
         body, lon_size, lat_size, groups, (c // heads) ** -0.5, cells_total ** -0.5
-    )
-    out_shape = (
-        jax.ShapeDtypeStruct(cells.shape, BF16),
-        jax.ShapeDtypeStruct(cells.shape, BF16),
-        jax.ShapeDtypeStruct((c, 3 * c), F32),
-        jax.ShapeDtypeStruct((c, c), F32),
-        jax.ShapeDtypeStruct(table.shape, F32),
     )
     results = pl.pallas_call(
         kernel,
         out_shape=out_shape,
         in_specs=[pl.BlockSpec(memory_space=pl.ANY)] * len(ins),
-        out_specs=(pl.BlockSpec(memory_space=pltpu.VMEM),) * len(out_shape),
+        out_specs=(pl.BlockSpec(memory_space=pl.ANY),) * len(out_shape),
         scratch_shapes=scratch,
         compiler_params=pltpu.CompilerParams(
             vmem_limit_bytes=60 * 1024 * 1024, collective_id=0, has_side_effects=True

time: 67 us -> 62.9 us (0.939)
  Pallas kernels: 66.1 us -> 62 us
    pallas_call x1, Pallas kernels: 63.3 us -> 59.2 us  [fused(): pl.pallas_call(kernel, out_shape=out_shape, in_specs=[pl.BlockSpec(memory...]
where the time goes in v8:
time: 62.9 us; the launch traced here: 62.8 us
  Pallas kernels  62 us (99%)
  between operations  0.8 us (1%)
    pallas_call x1, Pallas kernels, fused(): pl.pallas_call(kernel, out_shape=out_shape, in_specs=[pl.BlockSpec(memory...  59.2 us
    pallas_call x1, Pallas kernels, handed_out(): pl.pallas_call(move, out_shape=tuple((jax.ShapeDtypeStruct(a.shape, a.dty...  2.83 us

profile of v8, /device:TPU:1, one launch (start us, length us, event | category | flops | bytes accessed | tf_op | source)
XLA Modules:
  0.0 62.8 jit_solution(13818041979320692839)
XLA Ops:
  0.6 59.2 %shard_map.191 = (bf16[6,36,2,384]{3,2,1,0:T(2,128)(2,1)}, bf16[6,36,2,384]{3,2,1,0:T(2,128)(2,1)}, f32[384,1152]{1,0:T(8,128)}, f32[384,384]{1,0:T(8,128)}, f32[12,1,3312]{2,1,0:T(1,128)}) custom-call(bf16[6,36,2,384]{3,2,1,0:T(2,128)(2,1)} %bitcast.6, bf16[6,36,2,384]{3,2,1,0:T(2,128)(2,1)} %bitcast.7, bf16[384,1152]{1,0:T(8,128)(2,1)} %refs_2_.1, ...), custom_call_target="tpu_custom_call" | custom-call | flops 6000000000 | bytes 10000000 | tf_op jit(solution)/shard_map/pallas_call | solution.py:634
  59.8 2.8 %shard_map.192 = (bf16[6,36,2,384]{3,2,1,0:T(2,128)(2,1)}, bf16[6,36,2,384]{3,2,1,0:T(2,128)(2,1)}, f32[384,1152]{1,0:T(8,128)}, f32[384,384]{1,0:T(8,128)}, f32[12,1,3312]{2,1,0:T(1,128)}) custom-call(bf16[6,36,2,384]{3,2,1,0:T(2,128)(2,1)} %get-tuple-element.15.refs_0_, bf16[6,36,2,384]{3,2,1,0:T(2,128)(2,1)} %get-tuple-element.16.refs_1_, ...), custom_call_target="tpu_custom_call" | custom-call | tf_op jit(solution)/shard_map/pallas_call | solution.py:668

commit v9 on v8

--- a/solution.py
+++ b/solution.py
@@ -26,7 +26,7 @@
 RIM_OF = ((0, 80), (80, 80), (160, 144))
 RIM = 304
 BIAS_TILES = 32
-CHUNKS = (96, 96, 96)
+CHUNKS = (128, 96, 64)
 X_HI = 2
 F32 = jnp.float32
 BF16 = jnp.bfloat16
@@ -310,7 +310,9 @@
         ds = ds.astype(BF16)
         dq_ts[w * gw:(w + 1) * gw, :] = (nn(k_ts[w, g_of(g), :], ds) * (mine * scale)).astype(BF16)
         dproj[at, g_of(g, 1)] = (nt(ds, q_ws[w, g]) * scale).astype(BF16)
-        dproj[at, g_of(g, 2)] = nt(soft.astype(BF16), dm_wide).astype(BF16)
+
+    def values(g, w):
+        dproj[at_of(w), g_of(g, 2)] = nt(soft_s[w, g].astype(BF16), dm_ws[w, g]).astype(BF16)
 
     def tile_at(t):
         i = 0
@@ -332,14 +334,20 @@
             for r in range(24):
                 put(k * 24 + r, grad[r * 16:(r + 1) * 16, k * 128:(k + 1) * 128])
 
-    def qkv_grads(g):
+    def column_grad(k, g, part):
+        grad = nn(normed_t[...], dproj[:, g_of(g, part)]) * grad_scale
+        for r in range(24):
+            put(24 * k + r, grad[r * 16:(r + 1) * 16])
+
+    def qk_grads(g):
         dq = nt(pick, dq_ts[...]).astype(BF16)
         for w in range(WINDOWS):
             dproj[at_of(w), g_of(g)] = dq[:, w * gw:(w + 1) * gw]
-        for part in range(3):
-            grad = nn(normed_t[...], dproj[:, g_of(g, part)]) * grad_scale
-            for r in range(24):
-                put(72 + 72 * g + part * 24 + r, grad[r * 16:(r + 1) * 16])
+        for part in range(2):
+            column_grad(6 + 2 * g + part, g, part)
+
+    def columns_of(k):
+        return g_of(k - 3, 2) if k < 6 else g_of((k - 6) // 2, (k - 6) % 2)
 
     class Chain:
         def __init__(self, refs):
@@ -406,8 +414,7 @@
             if k < 3:
                 gout_ref[rows, k * 128:(k + 1) * 128] = value
             else:
-                g, part = (k - 3) // 3, (k - 3) % 3
-                gqkv_ref[rows, g_of(g, part)] = value
+                gqkv_ref[rows, columns_of(k)] = value
 
     bshare = BIAS_TILES // lon_size
 
@@ -487,7 +494,7 @@
 
     def store_columns(first, end):
         for k in range(first, end):
-            at = (slice(None), g_of(k // 3, k % 3))
+            at = (slice(None), columns_of(k))
             store(gqkv_ref.at[at], outs_h[2].at[at])
 
     c0, c1, c2 = chains
@@ -502,21 +509,23 @@
     out_grads()
     for w in range(WINDOWS):
         widen(w)
+    for g in range(groups):
+        for w in range(WINDOWS):
+            values(g, w)
+        column_grad(3 + g, g, 2)
+    c0.start()
     for w in range(WINDOWS):
         backward(0, w)
-    qkv_grads(0)
-    c0.start()
-    backward(1, 0)
-    backward(1, 1)
     c0.first()
-    backward(1, 2)
-    qkv_grads(1)
+    qk_grads(0)
+    for w in range(WINDOWS):
+        backward(1, w)
+    qk_grads(1)
     c1.start()
-    backward(2, 0)
-    backward(2, 1)
+    for w in range(WINDOWS):
+        backward(2, w)
     c1.first()
-    backward(2, 2)
-    qkv_grads(2)
+    qk_grads(2)
     c2.start()
     c0.second()
     dn = nt(dproj[...], wqkv_ref[...])
@@ -538,20 +547,21 @@
     bias_back()
     c2.third()
     c0.last()
-    unpack(0, 96)
+    unpack(0, 128)
     store(gout_ref, outs_h[3])
+    store_columns(3, 5)
     c1.fourth()
     bias_end()
     store(dr_ref, outs_h[4])
     finish(1, dx_ref)
     store(dx_ref, outs_h[1])
     c1.last()
-    unpack(96, 192)
-    store_columns(0, 5)
+    unpack(128, 224)
+    store_columns(5, 9)
     c2.fourth()
     c2.last()
-    unpack(192, 288)
-    store_columns(5, 9)
+    unpack(224, 288)
+    store_columns(9, 12)
     for copy in stores:
         copy.wait()
     for chain in chains:

time: 62.9 us -> 63.4 us (level)
  no operation moved by 1% of the time
where the time goes in v9:
time: 63.4 us; the launch traced here: 63.3 us
  Pallas kernels  62.5 us (99%)
  between operations  0.8 us (1%)
    pallas_call x1, Pallas kernels, fused(): pl.pallas_call(kernel, out_shape=out_shape, in_specs=[pl.BlockSpec(memory...  59.7 us
    pallas_call x1, Pallas kernels, handed_out(): pl.pallas_call(move, out_shape=tuple((jax.ShapeDtypeStruct(a.shape, a.dty...  2.83 us

profile of v9, /device:TPU:1, one launch (start us, length us, event | category | flops | bytes accessed | tf_op | source)
XLA Modules:
  0.0 63.3 jit_solution(5369782512259593036)
XLA Ops:
  0.6 59.7 %shard_map.191 = (bf16[6,36,2,384]{3,2,1,0:T(2,128)(2,1)}, bf16[6,36,2,384]{3,2,1,0:T(2,128)(2,1)}, f32[384,1152]{1,0:T(8,128)}, f32[384,384]{1,0:T(8,128)}, f32[12,1,3312]{2,1,0:T(1,128)}) custom-call(bf16[6,36,2,384]{3,2,1,0:T(2,128)(2,1)} %bitcast.6, bf16[6,36,2,384]{3,2,1,0:T(2,128)(2,1)} %bitcast.7, bf16[384,1152]{1,0:T(8,128)(2,1)} %refs_2_.1, ...), custom_call_target="tpu_custom_call" | custom-call | flops 6000000000 | bytes 10000000 | tf_op jit(solution)/shard_map/pallas_call | solution.py:644
  60.3 2.8 %shard_map.192 = (bf16[6,36,2,384]{3,2,1,0:T(2,128)(2,1)}, bf16[6,36,2,384]{3,2,1,0:T(2,128)(2,1)}, f32[384,1152]{1,0:T(8,128)}, f32[384,384]{1,0:T(8,128)}, f32[12,1,3312]{2,1,0:T(1,128)}) custom-call(bf16[6,36,2,384]{3,2,1,0:T(2,128)(2,1)} %get-tuple-element.15.refs_0_, bf16[6,36,2,384]{3,2,1,0:T(2,128)(2,1)} %get-tuple-element.16.refs_1_, ...), custom_call_target="tpu_custom_call" | custom-call | tf_op jit(solution)/shard_map/pallas_call | solution.py:678

commit v10 on v9

--- a/solution.py
+++ b/solution.py
@@ -108,8 +108,9 @@
      kv, k_ts, q_ws, soft_s, m_ts, dm_ws, dq_ts, tab, rows_of, turned, n_s, rstd_s,
      halo_sem, *comm) = refs[N_IN + 5:]
     (out_ref, dx_ref, gqkv_ref, gout_ref, dr_ref, out_sem) = comm[-6:]
-    chunk_refs = [comm[i * 7:i * 7 + 7] for i in range(len(CHUNKS))]
-    (bb, brecv, bfin, b_sem) = comm[len(CHUNKS) * 7:-6]
+    many = 7 * (len(CHUNKS) - 1)
+    chunk_refs = [comm[i:i + 7] for i in range(0, many, 7)] + [comm[many:many + 5]]
+    (bb, brecv, bfin, b_sem) = comm[many + 5:-6]
     c = wout_ref.shape[0]
     n, nz = lon_size // 4, lat_size // X_HI
     half = WH * WW
@@ -135,6 +136,12 @@
     for o in range(1, nxy):
         q = (p + o) % nxy
         plane.append((q, chip(q % n, q // n)))
+    rank = core * nxy + p
+    wide = []
+    for o in range(1, 2 * nxy):
+        q = (rank + o) % (2 * nxy)
+        at = q % nxy
+        wide.append((q, dev((at // n * 2 + at % n % 2) * 2 + q // nxy, at % n // 2 * nz + z)))
     for o in range(1, lon_size):
         q = (lon + o) % lon_size
         line.append((q, dev(q, lat)))
@@ -167,7 +174,7 @@
         pl.semaphore_signal(barrier, inc=1, device_id=device, device_id_type=MESH)
 
     partners = back + ahead
-    partners += tuple(d for _, d in plane + line) + tuple(d for d, _ in zs)
+    partners += tuple(d for _, d in wide) + tuple(d for d, _ in zs)
     for device in partners:
         greet(device)
 
@@ -319,6 +326,9 @@
         while t >= CHUNKS[i]:
             t -= CHUNKS[i]
             i += 1
+        if i == len(CHUNKS) - 1:
+            share = CHUNKS[i] // (2 * nxy)
+            return i, (t // share, t % share)
         half_tiles = CHUNKS[i] // 2
         share = half_tiles // nxy
         return i, (t // half_tiles, t % half_tiles // share, t % share)
@@ -403,7 +413,44 @@
             self.wait(0, 3, self.xrecv)
             self.wait(0, 4, self.crecv)
 
-    chains = [Chain(r) for r in chunk_refs]
+    class Wide(Chain):
+        def __init__(self, refs):
+            (self.gb, self.xrecv, self.zbuf, self.fin, self.sem) = refs
+
+        def start(self):
+            for o, (q, d) in enumerate(wide):
+                self.send(0, self.gb.at[q], self.xrecv.at[o], d)
+
+        def second(self):
+            self.wait(1, 0, self.xrecv)
+            total = self.gb[rank].astype(F32)
+            for o in range(2 * nxy - 1):
+                total += self.xrecv[o].astype(F32)
+            self.zbuf[0] = total.astype(BF16)
+            for o, (d, _) in enumerate(zs):
+                self.send(1, self.zbuf.at[0], self.zbuf.at[o + 1], d)
+
+        def third(self):
+            if nz > 1:
+                self.wait(1, 1, self.zbuf.at[pl.ds(1, nz - 1)])
+            total = self.zbuf[z].astype(F32)
+            for k in range(1, nz):
+                total += self.zbuf[(z + nz - k) % nz].astype(F32)
+            mine_at = self.fin.at[rank]
+            mine_at[...] = total.astype(BF16)
+            for _, d in wide:
+                self.send(2, mine_at, mine_at, d)
+
+        def last(self):
+            self.wait(1, 2, self.xrecv)
+
+        def drain(self):
+            self.wait(0, 0, self.xrecv)
+            if nz > 1:
+                self.wait(0, 1, self.zbuf.at[pl.ds(1, nz - 1)])
+            self.wait(0, 2, self.xrecv)
+
+    chains = [Chain(r) for r in chunk_refs[:-1]] + [Wide(chunk_refs[-1])]
 
     def unpack(first, end):
         for t in range(first, end):
@@ -532,7 +579,6 @@
     n_w = n_s[...]
     dx = dn - jnp.mean(dn, axis=-1, keepdims=True) - n_w * jnp.mean(dn * n_w, axis=-1, keepdims=True)
     ow[1] = (dx * rstd_s[...] + dy_w[...].astype(F32)).astype(BF16)
-    c2.first()
     pack_out(1)
     c1.second()
     bias_core()
@@ -558,7 +604,6 @@
     c1.last()
     unpack(128, 224)
     store_columns(5, 9)
-    c2.fourth()
     c2.last()
     unpack(224, 288)
     store_columns(9, 12)
@@ -620,7 +665,7 @@
         dma((2, 14)),
     ]
     tile = (16, 128)
-    for tiles in CHUNKS:
+    for tiles in CHUNKS[:-1]:
         share = tiles // (2 * n * n)
         scratch += [
             vm((2, n * n, share) + tile, BF16),
@@ -631,6 +676,14 @@
             vm((2, n * n, share) + tile, BF16),
             dma((2, 5)),
         ]
+    share = CHUNKS[-1] // (2 * n * n)
+    scratch += [
+        vm((2 * n * n, share) + tile, BF16),
+        vm((2 * n * n - 1, share) + tile, BF16),
+        vm((nz, share) + tile, BF16),
+        vm((2 * n * n, share) + tile, BF16),
+        dma((2, 3)),
+    ]
     scratch += [
         vm((lon_size, bshare) + tile, BF16),
         vm((lon_size - 1, bshare) + tile, BF16),

time: 63.4 us -> 63.6 us (level)
  no operation moved by 1% of the time
where the time goes in v10:
time: 63.6 us; the launch traced here: 63.5 us
  Pallas kernels  62.7 us (99%)
  between operations  0.8 us (1%)
    pallas_call x1, Pallas kernels, fused(): pl.pallas_call(kernel, out_shape=out_shape, in_specs=[pl.BlockSpec(memory...  59.9 us
    pallas_call x1, Pallas kernels, handed_out(): pl.pallas_call(move, out_shape=tuple((jax.ShapeDtypeStruct(a.shape, a.dty...  2.83 us

profile of v10, /device:TPU:1, one launch (start us, length us, event | category | flops | bytes accessed | tf_op | source)
XLA Modules:
  0.0 63.5 jit_solution(3993105504547055259)
XLA Ops:
  0.6 59.9 %shard_map.191 = (bf16[6,36,2,384]{3,2,1,0:T(2,128)(2,1)}, bf16[6,36,2,384]{3,2,1,0:T(2,128)(2,1)}, f32[384,1152]{1,0:T(8,128)}, f32[384,384]{1,0:T(8,128)}, f32[12,1,3312]{2,1,0:T(1,128)}) custom-call(bf16[6,36,2,384]{3,2,1,0:T(2,128)(2,1)} %bitcast.6, bf16[6,36,2,384]{3,2,1,0:T(2,128)(2,1)} %bitcast.7, bf16[384,1152]{1,0:T(8,128)(2,1)} %refs_2_.1, ...), custom_call_target="tpu_custom_call" | custom-call | flops 6000000000 | bytes 10000000 | tf_op jit(solution)/shard_map/pallas_call | solution.py:697
  60.5 2.8 %shard_map.192 = (bf16[6,36,2,384]{3,2,1,0:T(2,128)(2,1)}, bf16[6,36,2,384]{3,2,1,0:T(2,128)(2,1)}, f32[384,1152]{1,0:T(8,128)}, f32[384,384]{1,0:T(8,128)}, f32[12,1,3312]{2,1,0:T(1,128)}) custom-call(bf16[6,36,2,384]{3,2,1,0:T(2,128)(2,1)} %get-tuple-element.15.refs_0_, bf16[6,36,2,384]{3,2,1,0:T(2,128)(2,1)} %get-tuple-element.16.refs_1_, ...), custom_call_target="tpu_custom_call" | custom-call | tf_op jit(solution)/shard_map/pallas_call | solution.py:731

commit v11 on v10

--- a/solution.py
+++ b/solution.py
@@ -569,38 +569,39 @@
         backward(1, w)
     qk_grads(1)
     c1.start()
-    for w in range(WINDOWS):
-        backward(2, w)
+    backward(2, 0)
+    backward(2, 1)
+    c0.second()
+    backward(2, 2)
     c1.first()
     qk_grads(2)
     c2.start()
-    c0.second()
     dn = nt(dproj[...], wqkv_ref[...])
     n_w = n_s[...]
     dx = dn - jnp.mean(dn, axis=-1, keepdims=True) - n_w * jnp.mean(dn * n_w, axis=-1, keepdims=True)
     ow[1] = (dx * rstd_s[...] + dy_w[...].astype(F32)).astype(BF16)
     pack_out(1)
-    c1.second()
-    bias_core()
-    c0.third()
-    c2.second()
     for copy in rims_out[1]:
         copy.start()
+    c0.third()
+    bias_core()
+    c1.second()
+    c2.second()
     finish(0, out_ref)
     store(out_ref, outs_h[0])
+    c0.fourth()
     c1.third()
-    c0.fourth()
     bias_back()
-    c2.third()
     c0.last()
     unpack(0, 128)
     store(gout_ref, outs_h[3])
     store_columns(3, 5)
+    c2.third()
+    finish(1, dx_ref)
+    store(dx_ref, outs_h[1])
     c1.fourth()
     bias_end()
     store(dr_ref, outs_h[4])
-    finish(1, dx_ref)
-    store(dx_ref, outs_h[1])
     c1.last()
     unpack(128, 224)
     store_columns(5, 9)

time: 63.6 us -> 66.4 us (1.044)
  Pallas kernels: 62.7 us -> 65.5 us
    pallas_call x1, Pallas kernels: 59.9 us -> 62.6 us  [fused(): pl.pallas_call(kernel, out_shape=out_shape, in_specs=[pl.BlockSpec(memory...]
where the time goes in v11:
time: 66.4 us; the launch traced here: 66.3 us
  Pallas kernels  65.5 us (99%)
  between operations  0.8 us (1%)
    pallas_call x1, Pallas kernels, fused(): pl.pallas_call(kernel, out_shape=out_shape, in_specs=[pl.BlockSpec(memory...  62.6 us
    pallas_call x1, Pallas kernels, handed_out(): pl.pallas_call(move, out_shape=tuple((jax.ShapeDtypeStruct(a.shape, a.dty...  2.83 us

profile of v11, /device:TPU:1, one launch (start us, length us, event | category | flops | bytes accessed | tf_op | source)
XLA Modules:
  0.0 66.3 jit_solution(1809733744461768072)
XLA Ops:
  0.6 62.6 %shard_map.191 = (bf16[6,36,2,384]{3,2,1,0:T(2,128)(2,1)}, bf16[6,36,2,384]{3,2,1,0:T(2,128)(2,1)}, f32[384,1152]{1,0:T(8,128)}, f32[384,384]{1,0:T(8,128)}, f32[12,1,3312]{2,1,0:T(1,128)}) custom-call(bf16[6,36,2,384]{3,2,1,0:T(2,128)(2,1)} %bitcast.6, bf16[6,36,2,384]{3,2,1,0:T(2,128)(2,1)} %bitcast.7, bf16[384,1152]{1,0:T(8,128)(2,1)} %refs_2_.1, ...), custom_call_target="tpu_custom_call" | custom-call | flops 6000000000 | bytes 10000000 | tf_op jit(solution)/shard_map/pallas_call | solution.py:698
  63.3 2.8 %shard_map.192 = (bf16[6,36,2,384]{3,2,1,0:T(2,128)(2,1)}, bf16[6,36,2,384]{3,2,1,0:T(2,128)(2,1)}, f32[384,1152]{1,0:T(8,128)}, f32[384,384]{1,0:T(8,128)}, f32[12,1,3312]{2,1,0:T(1,128)}) custom-call(bf16[6,36,2,384]{3,2,1,0:T(2,128)(2,1)} %get-tuple-element.15.refs_0_, bf16[6,36,2,384]{3,2,1,0:T(2,128)(2,1)} %get-tuple-element.16.refs_1_, ...), custom_call_target="tpu_custom_call" | custom-call | tf_op jit(solution)/shard_map/pallas_call | solution.py:732

commit v12 on v11

--- a/solution.py
+++ b/solution.py
@@ -571,26 +571,26 @@
     c1.start()
     backward(2, 0)
     backward(2, 1)
-    c0.second()
     backward(2, 2)
     c1.first()
     qk_grads(2)
     c2.start()
+    c0.second()
     dn = nt(dproj[...], wqkv_ref[...])
     n_w = n_s[...]
     dx = dn - jnp.mean(dn, axis=-1, keepdims=True) - n_w * jnp.mean(dn * n_w, axis=-1, keepdims=True)
     ow[1] = (dx * rstd_s[...] + dy_w[...].astype(F32)).astype(BF16)
     pack_out(1)
+    c1.second()
+    bias_core()
+    c0.third()
+    c2.second()
+    c1.third()
     for copy in rims_out[1]:
         copy.start()
-    c0.third()
-    bias_core()
-    c1.second()
-    c2.second()
     finish(0, out_ref)
     store(out_ref, outs_h[0])
     c0.fourth()
-    c1.third()
     bias_back()
     c0.last()
     unpack(0, 128)

time: 66.4 us -> 65 us (0.979)
  Pallas kernels: 65.5 us -> 64.1 us
    pallas_call x1, Pallas kernels: 62.6 us -> 61.3 us  [fused(): pl.pallas_call(kernel, out_shape=out_shape, in_specs=[pl.BlockSpec(memory...]
where the time goes in v12:
time: 65 us; the launch traced here: 64.9 us
  Pallas kernels  64.1 us (99%)
  between operations  0.8 us (1%)
    pallas_call x1, Pallas kernels, fused(): pl.pallas_call(kernel, out_shape=out_shape, in_specs=[pl.BlockSpec(memory...  61.3 us
    pallas_call x1, Pallas kernels, handed_out(): pl.pallas_call(move, out_shape=tuple((jax.ShapeDtypeStruct(a.shape, a.dty...  2.83 us

profile of v12, /device:TPU:1, one launch (start us, length us, event | category | flops | bytes accessed | tf_op | source)
XLA Modules:
  0.0 64.9 jit_solution(8624756667486574255)
XLA Ops:
  0.6 61.3 %shard_map.191 = (bf16[6,36,2,384]{3,2,1,0:T(2,128)(2,1)}, bf16[6,36,2,384]{3,2,1,0:T(2,128)(2,1)}, f32[384,1152]{1,0:T(8,128)}, f32[384,384]{1,0:T(8,128)}, f32[12,1,3312]{2,1,0:T(1,128)}) custom-call(bf16[6,36,2,384]{3,2,1,0:T(2,128)(2,1)} %bitcast.6, bf16[6,36,2,384]{3,2,1,0:T(2,128)(2,1)} %bitcast.7, bf16[384,1152]{1,0:T(8,128)(2,1)} %refs_2_.1, ...), custom_call_target="tpu_custom_call" | custom-call | flops 6000000000 | bytes 10000000 | tf_op jit(solution)/shard_map/pallas_call | solution.py:698
  61.9 2.8 %shard_map.192 = (bf16[6,36,2,384]{3,2,1,0:T(2,128)(2,1)}, bf16[6,36,2,384]{3,2,1,0:T(2,128)(2,1)}, f32[384,1152]{1,0:T(8,128)}, f32[384,384]{1,0:T(8,128)}, f32[12,1,3312]{2,1,0:T(1,128)}) custom-call(bf16[6,36,2,384]{3,2,1,0:T(2,128)(2,1)} %get-tuple-element.15.refs_0_, bf16[6,36,2,384]{3,2,1,0:T(2,128)(2,1)} %get-tuple-element.16.refs_1_, ...), custom_call_target="tpu_custom_call" | custom-call | tf_op jit(solution)/shard_map/pallas_call | solution.py:732

commit v13 on v8

--- a/solution.py
+++ b/solution.py
@@ -189,7 +189,8 @@
         rim_copies(1, rim_osnd, rim_out, ahead, 11, RIMS),
     )
     low = WH // 2 * PITCH
-    for f, src in enumerate((cells_v, cot_v)):
+    def enter(f):
+        src = (cells_v, cot_v)[f]
         loads[2 * f].wait()
         for s in range(WH):
             slab[f, s * PITCH:(s + 1) * PITCH, :] = jnp.concatenate(
@@ -204,6 +205,8 @@
             pl.semaphore_wait(barrier, len(partners))
         for copy in rims_in[f]:
             copy.start()
+
+    enter(0)
 
     for load in loads[3:6]:
         load.wait()
@@ -491,8 +494,10 @@
             store(gqkv_ref.at[at], outs_h[2].at[at])
 
     c0, c1, c2 = chains
-    for w in range(WINDOWS):
-        forward(w)
+    forward(0)
+    enter(1)
+    forward(1)
+    forward(2)
     ow[0] = (x_w[...].astype(F32) + nn(mix[...], wout_ref[...])).astype(BF16)
     pack_out(0)
     for copy in rims_out[0]:

time: 62.9 us -> 62.8 us (level)
  no operation moved by 1% of the time
where the time goes in v13:
time: 62.8 us; the launch traced here: 62.7 us
  Pallas kernels  61.9 us (99%)
  between operations  0.8 us (1%)
    pallas_call x1, Pallas kernels, fused(): pl.pallas_call(kernel, out_shape=out_shape, in_specs=[pl.BlockSpec(memory...  59.1 us
    pallas_call x1, Pallas kernels, handed_out(): pl.pallas_call(move, out_shape=tuple((jax.ShapeDtypeStruct(a.shape, a.dty...  2.83 us

profile of v13, /device:TPU:1, one launch (start us, length us, event | category | flops | bytes accessed | tf_op | source)
XLA Modules:
  0.0 62.7 jit_solution(13211586865764868632)
XLA Ops:
  0.6 59.1 %shard_map.191 = (bf16[6,36,2,384]{3,2,1,0:T(2,128)(2,1)}, bf16[6,36,2,384]{3,2,1,0:T(2,128)(2,1)}, f32[384,1152]{1,0:T(8,128)}, f32[384,384]{1,0:T(8,128)}, f32[12,1,3312]{2,1,0:T(1,128)}) custom-call(bf16[6,36,2,384]{3,2,1,0:T(2,128)(2,1)} %bitcast.6, bf16[6,36,2,384]{3,2,1,0:T(2,128)(2,1)} %bitcast.7, bf16[384,1152]{1,0:T(8,128)(2,1)} %refs_2_.1, ...), custom_call_target="tpu_custom_call" | custom-call | flops 6000000000 | bytes 10000000 | tf_op jit(solution)/shard_map/pallas_call | solution.py:639
  59.7 2.8 %shard_map.192 = (bf16[6,36,2,384]{3,2,1,0:T(2,128)(2,1)}, bf16[6,36,2,384]{3,2,1,0:T(2,128)(2,1)}, f32[384,1152]{1,0:T(8,128)}, f32[384,384]{1,0:T(8,128)}, f32[12,1,3312]{2,1,0:T(1,128)}) custom-call(bf16[6,36,2,384]{3,2,1,0:T(2,128)(2,1)} %get-tuple-element.15.refs_0_, bf16[6,36,2,384]{3,2,1,0:T(2,128)(2,1)} %get-tuple-element.16.refs_1_, ...), custom_call_target="tpu_custom_call" | custom-call | tf_op jit(solution)/shard_map/pallas_call | solution.py:673
